TPU v7x, 32 devices: a whole 2x2x4 slice. The times are simulated.
32 devices in a mesh: star: 8 (over y, x, core), gas: 4 (over z).
Axes of the slice: x: 2, y: 2, z: 4, core: 2. Of those that a mesh axis runs over, the one named last changes fastest.
Arguments:
- star_pos: float32 [3, 16384], P(None, ('star', 'gas')), may hold values from 0 to 32
- star_vel: float32 [3, 16384], P(None, ('star', 'gas')), may hold values from -6 to 6
- star_accel: float32 [6, 16384], P(None, ('star', 'gas')), may hold values from -6 to 6
- star_mass: float32 [16384], P(('star', 'gas')), may hold values from 0.1 to 2
- active: int32 [256], replicated, may hold values from 0 to 16383, as said below
- density: float32 [32, 32, 64], P('star', 'gas'), may hold values from 0.5 to 4
- flow_in: float32 [3, 32, 32, 64], P(None, 'star', 'gas'), may hold values from -2 to 2
- field_in: float32 [3, 32, 32, 64], P(None, 'star', 'gas'), may hold values from -4 to 4
Outputs:
- star_new: float32 [12, 16384], P(None, ('star', 'gas'))
- flow: float32 [3, 32, 32, 64], P(None, 'star', 'gas')
- field_out: float32 [3, 32, 32, 64], P(None, 'star', 'gas')
Inputs may be any that keep to these rules, and one draw needn't show every extreme that they name: Distinct and increasing; among the 512 consecutive indices of one device at most 24 are active, and in every draw some device holds exactly 24.
All inputs are finite; a program needn't handle non-finite values.
Results may differ from a plain program's by a relative error of at most 0.0001.
Values sent between devices are 32-bit elements; how exact they have to be, the bound alone decides.
No kernel may reach another device: no remote copies, remote signals or barrier semaphores. Data moves between devices by JAX's collectives and lax.ppermute only.
A program may use at most 64 MiB of HBM per device.

v0:
```python
import math

import jax
import jax.numpy as jnp
from jax import lax
from jax.sharding import PartitionSpec as P

gravity = 0.02
soften = 4.0
time_step = 1.5
field_step = 0.1
highest = lax.Precision.HIGHEST


def with_halo(block, sides, width):
    for axis, dim in sides:
        count = lax.axis_size(axis)
        forward = [(i, i + 1) for i in range(count - 1)]
        forward.append((count - 1, 0))
        backward = [(target, source) for source, target in forward]
        low = lax.ppermute(
            lax.slice_in_dim(block, block.shape[dim] - width, None, axis=dim), axis, forward
        )
        high = lax.ppermute(lax.slice_in_dim(block, 0, width, axis=dim), axis, backward)
        block = jnp.concatenate([low, block, high], axis=dim)
    return block


def grad_x(values):
    return 0.5 * (values[2:, 1:-1] - values[:-2, 1:-1])


def grad_y(values):
    return 0.5 * (values[1:-1, 2:] - values[1:-1, :-2])


def grad_z(values):
    return 0.5 * (jnp.roll(values, -1, 2) - jnp.roll(values, 1, 2))[1:-1, 1:-1]


def trim_rim(values):
    return values[1:-1, 1:-1]


def curl_of(comp_a, comp_b, comp_c):
    return (
        grad_y(comp_c) - grad_z(comp_b),
        grad_z(comp_a) - grad_x(comp_c),
        grad_x(comp_b) - grad_y(comp_a),
    )


def cross_of(lhs_vec, rhs_vec):
    return (
        lhs_vec[1] * rhs_vec[2] - lhs_vec[2] * rhs_vec[1],
        lhs_vec[2] * rhs_vec[0] - lhs_vec[0] * rhs_vec[2],
        lhs_vec[0] * rhs_vec[1] - lhs_vec[1] * rhs_vec[0],
    )


def field_rate(padded_field, padded_flow, padded_density):
    current = curl_of(padded_field[0], padded_field[1], padded_field[2])
    inner_field = (trim_rim(padded_field[0]), trim_rim(padded_field[1]), trim_rim(padded_field[2]))
    inner_flow = (trim_rim(padded_flow[0]), trim_rim(padded_flow[1]), trim_rim(padded_flow[2]))
    resist = trim_rim(padded_density) ** (-1.5)
    lorentz = cross_of(current, inner_field)
    drift = cross_of(lorentz, inner_field)
    motion = cross_of(inner_flow, inner_field)
    emf_a = motion[0] + resist * drift[0]
    emf_b = motion[1] + resist * drift[1]
    emf_c = motion[2] + resist * drift[2]
    return jnp.stack(curl_of(emf_a, emf_b, emf_c))


def pair_terms(target, resident, cell_place, cell_mass):
    star_gap = resident[0:3, None, :] - target[0:3, :, None]
    rel_vel = resident[3:6, None, :] - target[3:6, :, None]
    inv_r = lax.rsqrt(jnp.sum(star_gap * star_gap, 0) + soften)
    weight = gravity * resident[6][None, :] * inv_r * inv_r * inv_r
    star_acc = jnp.sum(weight[None] * star_gap, 2)
    approach = jnp.sum(star_gap * rel_vel, 0)
    star_jerk = jnp.sum(
        weight[None] * (rel_vel - 3.0 * (approach * inv_r * inv_r)[None] * star_gap), 2
    )
    cell_gap = cell_place[:, None, :] - target[0:3, :, None]
    inv_g = lax.rsqrt(jnp.sum(cell_gap * cell_gap, 0) + soften)
    inv_cube = gravity * inv_g * inv_g * inv_g
    gas_acc = jnp.sum((inv_cube * cell_mass[None, :])[None] * cell_gap, 2)
    cell_kick = -jnp.sum((inv_cube * target[6][:, None])[None] * cell_gap, 1)
    return (jnp.concatenate([star_acc + gas_acc, star_jerk], 0), cell_kick)


def all_terms(targets, resident, cell_place, cell_mass):
    target_total = targets.shape[1]
    block_width = math.gcd(target_total, 64)
    blocks = targets.reshape(7, target_total // block_width, block_width).transpose(1, 0, 2)

    def one_block(running, target_block):
        terms_here, cell_kick = pair_terms(target_block, resident, cell_place, cell_mass)
        return (running + cell_kick, terms_here)

    kick_sum, block_terms = lax.scan(one_block, jnp.zeros(cell_place.shape, jnp.float32), blocks)
    return (block_terms.transpose(1, 0, 2).reshape(6, target_total), kick_sum)


def body(star_pos, star_vel, star_accel, star_mass, active, density, flow_in, field_in):
    resident_total = star_pos.shape[1]
    old_acc = star_accel[0:3]
    old_jerk = star_accel[3:6]
    pred_pos = (
        star_pos
        + time_step * star_vel
        + time_step**2 / 2.0 * old_acc
        + time_step**3 / 6.0 * old_jerk
    )
    pred_vel = star_vel + time_step * old_acc + time_step**2 / 2.0 * old_jerk
    resident = jnp.concatenate([pred_pos, pred_vel, star_mass[None]], 0)
    my_rank = lax.axis_index("star") * lax.axis_size("gas") + lax.axis_index("gas")
    owner_of = active // resident_total
    local_slot = active % resident_total
    is_mine = owner_of == my_rank
    rows_iota = jnp.arange(resident_total, dtype=jnp.int32)
    owned = (is_mine[None, :] & (local_slot[None, :] == rows_iota[:, None])).astype(jnp.float32)
    active_mask = jnp.sum(owned, 1) > 0.5
    ext_x, ext_y, ext_z = density.shape
    grid_shape = (ext_x, ext_y, ext_z)
    coord_x = (lax.axis_index("star") * ext_x + jnp.arange(ext_x)).astype(jnp.float32) + 0.5
    coord_y = (lax.axis_index("gas") * ext_y + jnp.arange(ext_y)).astype(jnp.float32) + 0.5
    coord_z = jnp.arange(ext_z).astype(jnp.float32) + 0.5
    cell_place = jnp.stack(
        [
            jnp.broadcast_to(coord_x[:, None, None], grid_shape),
            jnp.broadcast_to(coord_y[None, :, None], grid_shape),
            jnp.broadcast_to(coord_z[None, None, :], grid_shape),
        ]
    ).reshape(3, -1)
    cell_mass = density.reshape(-1)
    placed = jnp.dot(resident, owned, precision=highest)
    targets = lax.psum(placed, ("star", "gas"))
    partial_terms, kick_sum = all_terms(targets, resident, cell_place, cell_mass)
    summed = lax.psum(partial_terms, ("star", "gas"))
    own_terms = jnp.dot(summed, owned.T, precision=highest)
    new_acc = own_terms[0:3]
    new_jerk = own_terms[3:6]
    vel_one = (
        star_vel
        + time_step * (old_acc + new_acc) / 2.0
        + time_step**2 * (old_jerk - new_jerk) / 12.0
    )
    pos_one = (
        star_pos
        + time_step * (star_vel + vel_one) / 2.0
        + time_step**2 * (old_acc - new_acc) / 12.0
    )
    updated = jnp.concatenate([pos_one, vel_one, new_acc, new_jerk], 0)
    base = jnp.concatenate([star_pos, star_vel, star_accel], 0)
    star_new = jnp.where(active_mask[None, :], updated, base)
    flow = flow_in + time_step * kick_sum.reshape(3, ext_x, ext_y, ext_z)

    def rate_of(values):
        padded = with_halo(
            jnp.concatenate([values, flow, density[None]], 0), (("star", 1), ("gas", 2)), 2
        )
        return field_rate(padded[0:3], padded[3:6], padded[6])

    first_section = field_in + field_step * rate_of(field_in)
    field_out = 0.5 * (field_in + first_section + field_step * rate_of(first_section))
    return (star_new, flow, field_out)


def solution(mesh):
    placed = (
        P(None, ("star", "gas")),
        P(None, ("star", "gas")),
        P(None, ("star", "gas")),
        P(("star", "gas")),
        P(),
        P("star", "gas", None),
        P(None, "star", "gas", None),
        P(None, "star", "gas", None),
    )
    return jax.shard_map(
        body,
        mesh=mesh,
        in_specs=placed,
        out_specs=(
            P(None, ("star", "gas")),
            P(None, "star", "gas", None),
            P(None, "star", "gas", None),
        ),
        check_vma=False,
    )
```

profile of v0, /device:TPU:0, one launch (start us, length us, event | category | flops | bytes accessed | tf_op | source)
XLA Modules:
  0.0 116.4 jit_solution(10615053682156892875)
XLA Ops:
  0.7 0.7 and_select_fusion
  1.4 0.7 fusion.93
  2.1 0.8 multiply_add_fusion.8
  2.9 0.9 fusion.15
  3.8 0.1 reshape.125
  4.0 42.1 %psum.14 = f32[4,7,64]{2,1,0:T(8,128)S(1)} all-reduce(f32[4,7,64]{2,1,0:T(8,128)S(1)} %bitcast.79), channel_id=1, replica_groups=mesh['star'=8,'gas'=4] {'star','gas'}, use_global_device_ids=true, to_apply=%region_1.2 | all-reduce | flops 1792 | bytes 14336 | tf_op jit(solution)/shard_map/psum | solution.py:139
  46.2 0.1 sub.546
  46.4 0.4 copy-done.4
  46.9 5.9 %while.14 = (s32[]{:T(128)}, f32[3,2048]{1,0:T(4,128)S(1)}, f32[4,6,64]{2,1,0:T(8,128)S(1)}, f32[3,4,8,64]{3,2,1,0:T(8,128)}, f32[4,7,64]{2,1,0:T(8,128)S(1)}, /...) while((s32[]{:T(128)}, f32[3,2048]{1,0:T(4,128)S(1)}, ...), condition=%wide.wide.region_10.11_spmd.clone, body=%wide.wide.region_2.10_spmd.clone.sunk | while | flops 5353987 | bytes 4405647 | solution.py:102
  46.9 0.1 fusion.138
  47.1 0.3 fusion.140
  47.4 0.2 fusion.135
  47.6 0.1 fusion.136
  47.8 0.5 fusion.137
  48.4 0.1 fusion.138
  48.6 0.3 fusion.140
  48.9 0.2 fusion.135
  49.1 0.1 fusion.136
  49.3 0.5 fusion.137
  49.9 0.1 fusion.138
  50.1 0.3 fusion.140
  50.4 0.2 fusion.135
  50.6 0.1 fusion.136
  50.8 0.5 fusion.137
  51.4 0.1 fusion.138
  51.6 0.3 fusion.140
  51.9 0.2 fusion.135
  52.1 0.1 fusion.136
  52.3 0.5 fusion.137
  52.9 0.1 mul.422
  53.0 0.7 pad_maximum_fusion.9
  53.8 2.6 %collective-permute-start.1 = (f32[7,2,8,64]{3,2,1,0:T(8,128)S(1)}, f32[7,2,8,64]{3,2,1,0:T(8,128)S(1)}, u32[]{:S(2)}, u32[]{:S(2)}) collective-permute-start(f32[7,2,8,64]{3,2,1,0:T(8,128)S(1)} %get-tuple-element.150), channel_id=1, source_target_pairs={{4,0},{8,4},{12,8},{16,12},{20,16},{24,20},{28,24},{0,28},{5,1},{9... | collective-permute-start | bytes 86024 | tf_op jit(solution)/shard_map/ppermute | solution.py:24
  56.5 0.1 reshape.126
  56.6 39.6 %psum.15 = f32[6,256]{1,0:T(8,128)S(1)} all-reduce(f32[6,256]{1,0:T(8,128)S(1)} %reshape.126), channel_id=1, replica_groups=mesh['star'=8,'gas'=4] {'star','gas'}, use_global_device_ids=true, to_apply=%region_11.12 | all-reduce | flops 1536 | bytes 12288 | tf_op jit(solution)/shard_map/psum | solution.py:141
  96.2 0.3 fusion.13
  96.7 0.6 collective-permute-start.2
  97.2 3.3 %collective-permute-start.3 = (f32[7,8,2,64]{3,2,1,0:T(2,128)S(1)}, f32[7,8,2,64]{3,2,1,0:T(2,128)S(1)}, u32[]{:S(2)}, u32[]{:S(2)}) collective-permute-start(f32[7,8,2,64]{3,2,1,0:T(2,128)S(1)} %get-tuple-element.146), channel_id=1, source_target_pairs={{1,0},{2,1},{3,2},{0,3},{5,4},{6,5},{7,6},{4,7},{9,8},{10,9},{11,1... | collective-permute-start | bytes 86024 | tf_op jit(solution)/shard_map/ppermute | solution.py:24
  100.5 0.2 convert_reduce_fusion
  100.7 2.0 %collective-permute-done.2 = f32[7,8,2,64]{3,2,1,0:T(2,128)S(1)} collective-permute-done((f32[7,8,2,64]{3,2,1,0:T(2,128)S(1)}, f32[7,8,2,64]{3,2,1,0:T(2,128)S(1)}, u32[]{:S(2)}, u32[]{:S(2)}) %collective-permute-start.2) | collective-permute-done | bytes 28704 | tf_op jit(solution)/shard_map/ppermute | solution.py:21
  102.7 0.1 fusion.20
  102.9 0.1 fusion.109
  103.0 0.1 fusion.108
  103.1 0.2 multiply_add_fusion.5
  103.4 0.1 fusion.118
  103.4 0.1 fusion.119
  103.5 0.1 fusion.116
  103.6 0.1 fusion.117
  103.7 0.1 fusion.84
  103.9 2.6 %collective-permute-start.5 = (f32[7,2,8,64]{3,2,1,0:T(8,128)S(1)}, f32[7,2,8,64]{3,2,1,0:T(8,128)S(1)}, u32[]{:S(2)}, u32[]{:S(2)}) collective-permute-start(f32[7,2,8,64]{3,2,1,0:T(8,128)S(1)} %get-tuple-element.148), channel_id=1, source_target_pairs={{4,0},{8,4},{12,8},{16,12},{20,16},{24,20},{28,24},{0,28},{5,1},{9... | collective-permute-start | bytes 86024 | tf_op jit(solution)/shard_map/ppermute | solution.py:24
  106.6 1.9 %collective-permute-done.4 = f32[7,2,8,64]{3,2,1,0:T(8,128)S(1)} collective-permute-done((f32[7,2,8,64]{3,2,1,0:T(8,128)S(1)}, f32[7,2,8,64]{3,2,1,0:T(8,128)S(1)}, u32[]{:S(2)}, u32[]{:S(2)}) %collective-permute-start.4) | collective-permute-done | bytes 28704 | tf_op jit(solution)/shard_map/ppermute | solution.py:21
  108.6 3.9 %collective-permute-start.7 = (f32[7,8,2,64]{3,2,1,0:T(2,128)S(1)}, f32[7,8,2,64]{3,2,1,0:T(2,128)S(1)}, u32[]{:S(2)}, u32[]{:S(2)}) collective-permute-start(f32[7,8,2,64]{3,2,1,0:T(2,128)S(1)} %get-tuple-element.144), channel_id=1, source_target_pairs={{1,0},{2,1},{3,2},{0,3},{5,4},{6,5},{7,6},{4,7},{9,8},{10,9},{11,1... | collective-permute-start | bytes 86024 | tf_op jit(solution)/shard_map/ppermute | solution.py:24
  112.4 0.6 maximum_select_fusion
  113.1 1.5 %collective-permute-done.6 = f32[7,8,2,64]{3,2,1,0:T(2,128)S(1)} collective-permute-done((f32[7,8,2,64]{3,2,1,0:T(2,128)S(1)}, f32[7,8,2,64]{3,2,1,0:T(2,128)S(1)}, u32[]{:S(2)}, u32[]{:S(2)}) %collective-permute-start.6) | collective-permute-done | bytes 28704 | tf_op jit(solution)/shard_map/ppermute | solution.py:21
  114.5 0.1 fusion.24
  114.7 0.1 fusion.104
  114.8 0.1 fusion.105
  114.8 0.1 fusion.106
  114.9 0.1 fusion.107
  115.0 0.2 multiply_add_fusion.2
  115.4 0.1 fusion.115
  115.5 0.1 fusion.112
  115.6 0.1 fusion.113
  115.7 0.1 fusion.70
  115.8 0.6 fusion.57
  (92 shorter events, 1.5 us)
Async XLA Ops:
  0.6 46.2 %copy-start.8 = (f32[512]{0:T(512)S(1)}, f32[512]{0:T(512)}, u32[]{:S(2)}) copy-start(f32[512]{0:T(512)} %param.13) | copy-start | bytes 6148
  0.6 45.7 %copy-start.2 = (f32[4,8,64]{2,1,0:T(8,128)S(1)}, f32[4,8,64]{2,1,0:T(8,128)}, u32[]{:S(2)}) copy-start(f32[4,8,64]{2,1,0:T(8,128)} %param.15) | copy-start | bytes 24580
  46.2 0.6 copy-start.4
  46.9 6.1 %copy-start.9 = (f32[3,4,8,64]{3,2,1,0:T(8,128)S(1)}, f32[3,4,8,64]{3,2,1,0:T(8,128)}, u32[]{:S(2)}) copy-start(f32[3,4,8,64]{3,2,1,0:T(8,128)} %param.16) | copy-start | bytes 73732
  46.9 6.1 %copy-start.1 = (f32[3,4,8,64]{3,2,1,0:T(8,128)S(1)}, f32[3,4,8,64]{3,2,1,0:T(8,128)}, u32[]{:S(2)}) copy-start(f32[3,4,8,64]{3,2,1,0:T(8,128)} %param.17) | copy-start | bytes 73732
  52.8 43.7 %copy-start.5 = (f32[6,512]{1,0:T(8,128)S(1)}, f32[6,512]{1,0:T(8,128)}, u32[]{:S(2)}) copy-start(f32[6,512]{1,0:T(8,128)} %param.12) | copy-start | bytes 36868
  52.8 43.7 %copy-start.6 = (f32[3,512]{1,0:T(4,128)S(1)}, f32[3,512]{1,0:T(4,128)}, u32[]{:S(2)}) copy-start(f32[3,512]{1,0:T(4,128)} %param.10) | copy-start | bytes 18436
  52.8 43.7 %copy-start.7 = (f32[3,512]{1,0:T(4,128)S(1)}, f32[3,512]{1,0:T(4,128)}, u32[]{:S(2)}) copy-start(f32[3,512]{1,0:T(4,128)} %param.11) | copy-start | bytes 18436
  52.9 43.7 %copy-start.3 = (f32[4,8,64]{2,1,0:T(8,128)S(1)}, f32[4,8,64]{2,1,0:T(8,128)}, u32[]{:S(2)}) copy-start(f32[4,8,64]{2,1,0:T(8,128)} %get-tuple-element.370) | copy-start | bytes 24580
  53.0 61.5 %copy-start = (f32[3,4,8,64]{3,2,1,0:T(8,128)}, f32[3,4,8,64]{3,2,1,0:T(8,128)S(1)}, u32[]{:S(2)}) copy-start(f32[3,4,8,64]{3,2,1,0:T(8,128)S(1)} %add.166) | copy-start | bytes 73732
  53.8 42.8 %collective-permute-start = (f32[7,2,8,64]{3,2,1,0:T(8,128)S(1)}, f32[7,2,8,64]{3,2,1,0:T(8,128)S(1)}, u32[]{:S(2)}, u32[]{:S(2)}) collective-permute-start(f32[7,2,8,64]{3,2,1,0:T(8,128)S(1)} %get-tuple-element.149), channel_id=1, source_target_pairs={{0,4},{4,8},{8,12},{12,16},{16,20},{20,24},{24,28},{28,0},{1,5},{5... | collective-permute-start | bytes 86024 | tf_op jit(solution)/shard_map/ppermute | solution.py:21
  53.8 42.7 %collective-permute-start.1 = (f32[7,2,8,64]{3,2,1,0:T(8,128)S(1)}, f32[7,2,8,64]{3,2,1,0:T(8,128)S(1)}, u32[]{:S(2)}, u32[]{:S(2)}) collective-permute-start(f32[7,2,8,64]{3,2,1,0:T(8,128)S(1)} %get-tuple-element.150), channel_id=1, source_target_pairs={{4,0},{8,4},{12,8},{16,12},{20,16},{24,20},{28,24},{0,28},{5,1},{9... | collective-permute-start | bytes 86024 | tf_op jit(solution)/shard_map/ppermute | solution.py:24
  96.7 6.0 %collective-permute-start.2 = (f32[7,8,2,64]{3,2,1,0:T(2,128)S(1)}, f32[7,8,2,64]{3,2,1,0:T(2,128)S(1)}, u32[]{:S(2)}, u32[]{:S(2)}) collective-permute-start(f32[7,8,2,64]{3,2,1,0:T(2,128)S(1)} %get-tuple-element.145), channel_id=1, source_target_pairs={{0,1},{1,2},{2,3},{3,0},{4,5},{5,6},{6,7},{7,4},{8,9},{9,10},{10,1... | collective-permute-start | bytes 86024 | tf_op jit(solution)/shard_map/ppermute | solution.py:21
  97.2 5.5 %collective-permute-start.3 = (f32[7,8,2,64]{3,2,1,0:T(2,128)S(1)}, f32[7,8,2,64]{3,2,1,0:T(2,128)S(1)}, u32[]{:S(2)}, u32[]{:S(2)}) collective-permute-start(f32[7,8,2,64]{3,2,1,0:T(2,128)S(1)} %get-tuple-element.146), channel_id=1, source_target_pairs={{1,0},{2,1},{3,2},{0,3},{5,4},{6,5},{7,6},{4,7},{9,8},{10,9},{11,1... | collective-permute-start | bytes 86024 | tf_op jit(solution)/shard_map/ppermute | solution.py:24
  103.9 4.6 %collective-permute-start.4 = (f32[7,2,8,64]{3,2,1,0:T(8,128)S(1)}, f32[7,2,8,64]{3,2,1,0:T(8,128)S(1)}, u32[]{:S(2)}, u32[]{:S(2)}) collective-permute-start(f32[7,2,8,64]{3,2,1,0:T(8,128)S(1)} %get-tuple-element.147), channel_id=1, source_target_pairs={{0,4},{4,8},{8,12},{12,16},{16,20},{20,24},{24,28},{28,0},{1,5},{5... | collective-permute-start | bytes 86024 | tf_op jit(solution)/shard_map/ppermute | solution.py:21
  103.9 4.5 %collective-permute-start.5 = (f32[7,2,8,64]{3,2,1,0:T(8,128)S(1)}, f32[7,2,8,64]{3,2,1,0:T(8,128)S(1)}, u32[]{:S(2)}, u32[]{:S(2)}) collective-permute-start(f32[7,2,8,64]{3,2,1,0:T(8,128)S(1)} %get-tuple-element.148), channel_id=1, source_target_pairs={{4,0},{8,4},{12,8},{16,12},{20,16},{24,20},{28,24},{0,28},{5,1},{9... | collective-permute-start | bytes 86024 | tf_op jit(solution)/shard_map/ppermute | solution.py:24
  108.5 6.0 %collective-permute-start.6 = (f32[7,8,2,64]{3,2,1,0:T(2,128)S(1)}, f32[7,8,2,64]{3,2,1,0:T(2,128)S(1)}, u32[]{:S(2)}, u32[]{:S(2)}) collective-permute-start(f32[7,8,2,64]{3,2,1,0:T(2,128)S(1)} %get-tuple-element.143), channel_id=1, source_target_pairs={{0,1},{1,2},{2,3},{3,0},{4,5},{5,6},{6,7},{7,4},{8,9},{9,10},{10,1... | collective-permute-start | bytes 86024 | tf_op jit(solution)/shard_map/ppermute | solution.py:21
  108.6 6.0 %collective-permute-start.7 = (f32[7,8,2,64]{3,2,1,0:T(2,128)S(1)}, f32[7,8,2,64]{3,2,1,0:T(2,128)S(1)}, u32[]{:S(2)}, u32[]{:S(2)}) collective-permute-start(f32[7,8,2,64]{3,2,1,0:T(2,128)S(1)} %get-tuple-element.144), channel_id=1, source_target_pairs={{1,0},{2,1},{3,2},{0,3},{5,4},{6,5},{7,6},{4,7},{9,8},{10,9},{11,1... | collective-permute-start | bytes 86024 | tf_op jit(solution)/shard_map/ppermute | solution.py:24
where the time goes:
time: 118 us; the launch traced here: 116 us
  blocking collectives  81.7 us (69%)
  starting transfers between devices  13.2 us (11%)
  other arithmetic  11.1 us (9%)
  waiting for transfers between devices  5.32 us (5%)
  local copies, waits for them, and re-layouts  2.49 us (2%)
  matrix products  1.27 us (1%)
    psum x1, blocking collectives, body(): targets = lax.psum(placed, ('star', 'gas'))  42.1 us
    psum x1, blocking collectives, body(): summed = lax.psum(partial_terms, ('star', 'gas'))  39.6 us
    ppermute x4, starting transfers between devices, with_halo(): lax.ppermute(lax.slice_in_dim(block, 0, width, axis=dim), axis, backward)  12.4 us
    ppermute x4, waiting for transfers between devices, with_halo(): lax.ppermute(lax.slice_in_dim(block, block.shape[dim] - width, None, axis...  5.31 us
  transfers between devices with their start and end apart: 8, of which 3 were waited for; matrix products, arithmetic and copies ran while one was open for 1% of the time, Pallas kernels for 0%

commit v1 on v0

v1 whole, which is shorter than its diff:
```python
import jax
import jax.numpy as jnp
from jax import lax
from jax.sharding import PartitionSpec as P

gravity = 0.02
soften = 4.0
time_step = 1.5
field_step = 0.1
highest = lax.Precision.HIGHEST
both = ("star", "gas")
reach = 4


def grad_x(values):
    return 0.5 * (values[2:, 1:-1] - values[:-2, 1:-1])


def grad_y(values):
    return 0.5 * (values[1:-1, 2:] - values[1:-1, :-2])


def grad_z(values):
    return 0.5 * (jnp.roll(values, -1, 2) - jnp.roll(values, 1, 2))[1:-1, 1:-1]


def trim_rim(values, width=1):
    return values[..., width:-width, width:-width, :]


def curl_of(comp_a, comp_b, comp_c):
    return (
        grad_y(comp_c) - grad_z(comp_b),
        grad_z(comp_a) - grad_x(comp_c),
        grad_x(comp_b) - grad_y(comp_a),
    )


def cross_of(lhs_vec, rhs_vec):
    return (
        lhs_vec[1] * rhs_vec[2] - lhs_vec[2] * rhs_vec[1],
        lhs_vec[2] * rhs_vec[0] - lhs_vec[0] * rhs_vec[2],
        lhs_vec[0] * rhs_vec[1] - lhs_vec[1] * rhs_vec[0],
    )


def field_rate(padded_field, inner_flow, inner_resist):
    current = curl_of(padded_field[0], padded_field[1], padded_field[2])
    inner_field = trim_rim(padded_field)
    drift = cross_of(cross_of(current, inner_field), inner_field)
    motion = cross_of(inner_flow, inner_field)
    emf = [motion[k] + inner_resist * drift[k] for k in range(3)]
    return jnp.stack(curl_of(*emf))


def pair_halo(block, axis, dim):
    count = lax.axis_size(axis)
    even = lax.axis_index(axis) % 2 == 0
    low = lax.slice_in_dim(block, 0, reach, axis=dim)
    high = lax.slice_in_dim(block, block.shape[dim] - reach, None, axis=dim)
    near = [(i, i ^ 1) for i in range(count)]
    far = [(i, (i + (1 if i % 2 else -1)) % count) for i in range(count)]
    from_far = lax.ppermute(jnp.where(even, low, high), axis, far)
    from_near = lax.ppermute(jnp.where(even, high, low), axis, near)
    below = jnp.where(even, from_far, from_near)
    above = jnp.where(even, from_near, from_far)
    return jnp.concatenate([below, block, above], axis=dim)


def pair_terms(target, resident, cell_place, cell_mass):
    star_gap = resident[0:3, None, :] - target[0:3, :, None]
    rel_vel = resident[3:6, None, :] - target[3:6, :, None]
    inv_r = lax.rsqrt(jnp.sum(star_gap * star_gap, 0) + soften)
    weight = gravity * resident[6][None, :] * inv_r * inv_r * inv_r
    star_acc = jnp.sum(weight[None] * star_gap, 2)
    approach = jnp.sum(star_gap * rel_vel, 0)
    star_jerk = jnp.sum(
        weight[None] * (rel_vel - 3.0 * (approach * inv_r * inv_r)[None] * star_gap), 2
    )
    cell_gap = cell_place[:, None, :] - target[0:3, :, None]
    inv_g = lax.rsqrt(jnp.sum(cell_gap * cell_gap, 0) + soften)
    inv_cube = gravity * inv_g * inv_g * inv_g
    gas_acc = jnp.sum((inv_cube * cell_mass[None, :])[None] * cell_gap, 2)
    return jnp.concatenate([star_acc + gas_acc, star_jerk], 0)


def kick_terms(target, cell_place):
    cell_gap = target[0:3, :, None] - cell_place[:, None, :]
    inv_g = lax.rsqrt(jnp.sum(cell_gap * cell_gap, 0) + soften)
    weight = gravity * inv_g * inv_g * inv_g * target[6][:, None]
    return jnp.sum(weight[None] * cell_gap, 1)


def in_blocks(targets, width):
    count = targets.shape[1] // width
    return targets.reshape(targets.shape[0], count, width).transpose(1, 0, 2)


def cells_at(first_x, count_x, total_x, first_y, count_y, total_y, count_z):
    shape = (count_x, count_y, count_z)
    place_x = ((first_x + jnp.arange(count_x)) % total_x).astype(jnp.float32) + 0.5
    place_y = ((first_y + jnp.arange(count_y)) % total_y).astype(jnp.float32) + 0.5
    place_z = jnp.arange(count_z).astype(jnp.float32) + 0.5
    return jnp.stack(
        [
            jnp.broadcast_to(place_x[:, None, None], shape),
            jnp.broadcast_to(place_y[None, :, None], shape),
            jnp.broadcast_to(place_z[None, None, :], shape),
        ]
    ).reshape(3, -1)


def body(star_pos, star_vel, star_accel, star_mass, active, density, flow_in, field_in):
    resident_total = star_pos.shape[1]
    listed = active.shape[0]
    star_count, gas_count = lax.axis_size("star"), lax.axis_size("gas")
    devices = star_count * gas_count
    slots = 4 * (listed // devices)
    ext_x, ext_y, ext_z = density.shape
    my_star, my_gas = lax.axis_index("star"), lax.axis_index("gas")
    base_row = (my_star * gas_count + my_gas) * resident_total
    old_acc = star_accel[0:3]
    old_jerk = star_accel[3:6]
    pred_pos = (
        star_pos
        + time_step * star_vel
        + time_step**2 / 2.0 * old_acc
        + time_step**3 / 6.0 * old_jerk
    )
    pred_vel = star_vel + time_step * old_acc + time_step**2 / 2.0 * old_jerk
    resident = jnp.concatenate([pred_pos, pred_vel, star_mass[None]], 0)

    owner_of = active // resident_total
    device_ids = jnp.arange(devices, dtype=jnp.int32)
    owned_by = (owner_of[None, :] == device_ids[:, None]).astype(jnp.float32)
    first_of = jnp.sum((owner_of[None, :] < device_ids[:, None]).astype(jnp.float32), 1)
    place_of = jnp.arange(listed) - jnp.sum(owned_by * first_of[:, None], 0).astype(jnp.int32)
    slot_hit = (place_of[None, :] == jnp.arange(slots)[:, None]).astype(jnp.float32)
    my_slot = jnp.where(
        owner_of[None, :] * resident_total == base_row, slot_hit, 0.0
    )
    local_row = (active - base_row)[:, None] == jnp.arange(resident_total)[None, :]
    slot_row = jnp.dot(my_slot, local_row.astype(jnp.float32))
    is_active = jnp.sum(slot_row, 0) > 0.5

    own = lax.dot_general(slot_row, resident, (((1,), (1,)), ((), ())), precision=highest)
    own = jnp.pad(own.T, ((0, 1), (0, 0))).reshape(8, slots)
    send = jnp.stack(
        [jnp.concatenate([own[0:3], own[6:7]]).reshape(-1), jnp.concatenate([own[3:6], own[7:8]]).reshape(-1)]
    )
    got = lax.all_to_all(
        jnp.broadcast_to(send[None], (devices,) + send.shape), both, 0, 0, tiled=True
    )
    spread = jnp.einsum("dl,dt->lt", got.reshape(devices, -1), owned_by, precision=highest)
    spread = jnp.sum(spread.reshape(8, slots, listed) * slot_hit[None], 1)
    targets = jnp.concatenate([spread[0:3], spread[4:7], spread[3:4]], 0)

    gas_block = jnp.concatenate([field_in, flow_in, density[None]], 0)
    padded = pair_halo(gas_block, "gas", 2)
    padded = pair_halo(padded, "star", 1)

    grid_x, grid_y = ext_x * star_count, ext_y * gas_count
    cell_place = cells_at(my_star * ext_x, ext_x, grid_x, my_gas * ext_y, ext_y, grid_y, ext_z)
    blocks = in_blocks(targets, min(listed, 128))
    partial = lax.map(
        lambda block: pair_terms(block, resident, cell_place, density.reshape(-1)), blocks
    )
    partial = partial.transpose(1, 0, 2).reshape(6, listed)
    partial = jnp.pad(partial.reshape(2, 3, listed), ((0, 0), (0, 1), (0, 0)))
    to_owner = jnp.einsum(
        "dt,pcst->dpcs", owned_by, partial[:, :, None, :] * slot_hit[None, None], precision=highest
    )
    back = lax.all_to_all(to_owner.reshape(devices, 2, 4 * slots), both, 0, 0, tiled=True)
    own_sum = jnp.sum(back, 0).reshape(2, 4, slots)[:, 0:3].reshape(6, slots)
    own_terms = jnp.dot(own_sum, slot_row, precision=highest)
    new_acc = own_terms[0:3]
    new_jerk = own_terms[3:6]
    vel_one = (
        star_vel
        + time_step * (old_acc + new_acc) / 2.0
        + time_step**2 * (old_jerk - new_jerk) / 12.0
    )
    pos_one = (
        star_pos
        + time_step * (star_vel + vel_one) / 2.0
        + time_step**2 * (old_acc - new_acc) / 12.0
    )
    updated = jnp.concatenate([pos_one, vel_one, new_acc, new_jerk], 0)
    base = jnp.concatenate([star_pos, star_vel, star_accel], 0)
    star_new = jnp.where(is_active[None, :], updated, base)

    rim = reach - 1
    rim_place = cells_at(
        my_star * ext_x - rim + grid_x, ext_x + 2 * rim, grid_x,
        my_gas * ext_y - rim + grid_y, ext_y + 2 * rim, grid_y, ext_z,
    )
    kick, _ = lax.scan(
        lambda total, block: (total + kick_terms(block, rim_place), None),
        jnp.zeros(rim_place.shape, jnp.float32), blocks,
    )
    rim_flow = trim_rim(padded[3:6])
    rim_flow = rim_flow + time_step * kick.reshape(rim_flow.shape)
    rim_resist = trim_rim(padded[6]) ** (-1.5)
    flow = trim_rim(rim_flow, rim)

    wide = padded[0:3]
    section = trim_rim(wide, 2) + field_step * field_rate(wide, rim_flow, rim_resist)
    rate = field_rate(section, trim_rim(rim_flow, 2), trim_rim(rim_resist, 2))
    field_out = 0.5 * (field_in + trim_rim(section, 2) + field_step * rate)
    return (star_new, flow, field_out)


def solution(mesh):
    placed = (
        P(None, both),
        P(None, both),
        P(None, both),
        P(both),
        P(),
        P("star", "gas", None),
        P(None, "star", "gas", None),
        P(None, "star", "gas", None),
    )
    return jax.shard_map(
        body,
        mesh=mesh,
        in_specs=placed,
        out_specs=(
            P(None, both),
            P(None, "star", "gas", None),
            P(None, "star", "gas", None),
        ),
        check_vma=False,
    )
```

time: 118 us -> 49.2 us (0.42)
  blocking collectives: 81.7 us -> 0 us
  other arithmetic: 11.1 us -> 21 us
  starting transfers between devices: 13.2 us -> 16.2 us
  local copies, waits for them, and re-layouts: 2.49 us -> 5.37 us
  waiting for transfers between devices: 5.32 us -> 2.65 us
    psum x2 -> x0, blocking collectives: 81.7 us -> none  [the longest x1 42.1 us: body(): targets = lax.psum(placed, ('star', 'gas'))]
    all_to_all x0 -> x2, starting transfers between devices: none -> 10.8 us  [the longest x1 7.3 us: body(): lax.all_to_all(jnp.broadcast_to(send[None], (devices,) + send.shape), bot...]
    ppermute x8 -> x4, starting transfers between devices: 13.2 us -> 5.35 us  [the longest x2 4.85 us: pair_halo(): from_far = lax.ppermute(jnp.where(even, low, high), axis, far)]
    reduce_sum x1 -> x7, other arithmetic: 0.17 us -> 7.2 us  [the longest x2 3.75 us: kick_terms(): inv_g = lax.rsqrt(jnp.sum(cell_gap * cell_gap, 0) + soften)]
    ppermute x8 -> x4, waiting for transfers between devices: 5.32 us -> 2.65 us  [the longest x2 1.44 us: pair_halo(): from_far = lax.ppermute(jnp.where(even, low, high), axis, far)]
    mul x6, other arithmetic: 1.25 us -> 2.98 us  [the longest x2 1.84 us: kick_terms(): weight = gravity * inv_g * inv_g * inv_g * target[6][:, None]]
    mul x4 -> x2, other arithmetic: 0.02 us -> 1.37 us  [pair_terms(): weight = gravity * resident[6][None, :] * inv_r * inv_r * inv_r]
  transfers between devices with their start and end apart: 8 -> 6, of which waited for: 3 -> 2; matrix products, arithmetic and copies ran while one was open for 1% -> 42% of each run, Pallas kernels for 0% -> 0%
where the time goes in v1:
time: 49.2 us; the launch traced here: 48.5 us
  other arithmetic  21 us (43%)
  starting transfers between devices  16.2 us (33%)
  local copies, waits for them, and re-layouts  5.37 us (11%)
  waiting for transfers between devices  2.65 us (5%)
  matrix products  1.93 us (4%)
  between operations  1.14 us (2%)
    all_to_all x1, starting transfers between devices, body(): lax.all_to_all(jnp.broadcast_to(send[None], (devices,) + send.shape), bot...  7.3 us
    ppermute x2, starting transfers between devices, pair_halo(): from_far = lax.ppermute(jnp.where(even, low, high), axis, far)  4.85 us
    reduce_sum x2, other arithmetic, kick_terms(): inv_g = lax.rsqrt(jnp.sum(cell_gap * cell_gap, 0) + soften)  3.75 us
    all_to_all x1, starting transfers between devices, body(): lax.all_to_all(to_owner.reshape(devices, 2, 4 * slots), both, 0, 0, tiled...  3.51 us
    reduce_sum x2, other arithmetic, kick_terms(): return jnp.sum(weight[None] * cell_gap, 1)  3.21 us
    mul x2, other arithmetic, kick_terms(): weight = gravity * inv_g * inv_g * inv_g * target[6][:, None]  1.84 us
    ppermute x2, waiting for transfers between devices, pair_halo(): from_far = lax.ppermute(jnp.where(even, low, high), axis, far)  1.44 us
    mul x2, other arithmetic, pair_terms(): weight = gravity * resident[6][None, :] * inv_r * inv_r * inv_r  1.37 us
  transfers between devices with their start and end apart: 6, of which 2 were waited for; matrix products, arithmetic and copies ran while one was open for 42% of the time, Pallas kernels for 0%

profile of v1, /device:TPU:0, one launch (start us, length us, event | category | flops | bytes accessed | tf_op | source)
XLA Modules:
  0.0 48.5 jit_solution(13357005177351827365)
XLA Ops:
  0.6 0.7 %multiply_compare_fusion = (pred[256]{0:T(512)(128)(4,1)S(1)}, s32[256]{0:T(256)S(1)}) fusion(s32[]{:T(128)S(6)} %mul.477, s32[256]{0:T(256)} %param.16), kind=kLoop, calls=%fused_computation.225 | loop fusion | flops 4352 | bytes 2308 | tf_op jit(solution)/shard_map/eq | solution.py:140
  1.3 0.1 convert_reduce_fusion
  1.4 0.1 select_reduce_fusion
  1.5 0.7 %convert_subtract_fusion = (s32[256]{0:T(256)S(1)}, s32[256]{0:T(256)S(1)}) fusion(f32[256]{0:T(256)S(1)} %select_reduce_fusion, s32[256]{0:T(256)} %param.16, s32[]{:T(128)S(6)} %mul.477), kind=kLoop, calls=%fused_computation.224 | loop fusion | flops 768 | bytes 4100 | tf_op jit(solution)/shard_map/sub | solution.py:137
  2.2 0.8 %multiply_add_fusion.7 = (f32[3,512]{1,0:T(4,128)S(1)}, f32[3,512]{1,0:T(4,128)S(1)}) fusion(f32[3,512]{1,0:T(4,128)} %param.13, f32[6,512]{1,0:T(8,128)} %param.14, f32[3,512]{1,0:T(4,128)} %param.12), kind=kLoop, calls=%fused_computation.203 | loop fusion | flops 15360 | bytes 36864 | tf_op jit(solution)/shard_map/add | solution.py:130
  3.0 0.3 fusion.128
  3.3 0.8 %fusion.78 = f32[7,32]{1,0:T(8,128)S(1)} fusion(f32[32,512]{1,0:T(8,128)S(1)} %get-tuple-element.191, f32[1,512]{1,0:T(1,128)} %bitcast.202, f32[3,512]{1,0:T(4,128)S(1)} %get-tuple-element.370, f32[3,512]{1,0:T(4,128)S(1)} %get-tuple-element.366), kind=kOutput, calls=%fused_computation.188 | convolution fusion | flops 1383424 | bytes 80768 | tf_op jit(solution)/shard_map/dot_general | solution.py:146
  4.3 0.1 stack_reshape.6
  4.4 0.6 %broadcast_in_dim.32 = f32[32,2,128]{2,1,0:T(2,128)} broadcast(f32[2,128]{1,0:T(2,128)S(1)} %pad_maximum_fusion.22), dimensions={1,2} | broadcast | bytes 33792 | tf_op jit(solution)/shard_map/broadcast_in_dim | solution.py:152
  5.0 7.3 %all-to-all-start = ((f32[32,2,128]{2,1,0:T(2,128)}), f32[32,2,128]{2,1,0:T(2,128)S(1)}, u32[]{:S(2)}, u32[]{:S(2)}) async-start(f32[32,2,128]{2,1,0:T(2,128)} %broadcast_in_dim.32), calls=%async_computation | async-start | bytes 65536 | tf_op jit(solution)/shard_map/all_to_all | solution.py:151
  12.3 0.9 %pad_maximum_fusion.3 = f32[7,4,8,64]{3,2,1,0:T(8,128)S(1)} fusion(f32[1,4,8,64]{3,2,1,0:T(8,128)} %bitcast.198, f32[3,4,8,64]{3,2,1,0:T(8,128)} %param.18, f32[3,4,8,64]{3,2,1,0:T(8,128)} %param.19), kind=kLoop, calls=%fused_computation.51 | loop fusion | flops 28672 | bytes 114688 | tf_op jit(solution)/shard_map/concatenate | solution.py:158
  13.2 3.7 %collective-permute-start = (f32[7,4,4,64]{3,2,1,0:T(4,128)S(1)}, f32[7,4,4,64]{3,2,1,0:T(4,128)S(1)}, u32[]{:S(2)}, u32[]{:S(2)}) collective-permute-start(f32[7,4,4,64]{3,2,1,0:T(4,128)S(1)} %get-tuple-element.145), channel_id=1, source_target_pairs={{0,3},{1,2},{2,1},{3,0},{4,7},{5,6},{6,5},{7,4},{8,11},{9,10},{10,... | collective-permute-start | bytes 86024 | tf_op jit(solution)/shard_map/ppermute | solution.py:63
  17.4 0.8 %mul.824 = f32[2048]{0:T(1024)S(1)} reshape(f32[4,8,64]{2,1,0:T(8,128)} %param.17) | data formatting | bytes 16384 | tf_op jit(solution)/shard_map/while/body/eval_jaxpr/mul | solution.py:83
  18.2 0.1 sub.576
  18.3 0.1 sub.590
  18.4 1.4 %collective-permute-done = f32[7,4,4,64]{3,2,1,0:T(4,128)S(1)} collective-permute-done((f32[7,4,4,64]{3,2,1,0:T(4,128)S(1)}, f32[7,4,4,64]{3,2,1,0:T(4,128)S(1)}, u32[]{:S(2)}, u32[]{:S(2)}) %collective-permute-start) | collective-permute-done | bytes 28704 | tf_op jit(solution)/shard_map/ppermute | solution.py:63
  19.9 1.2 %collective-permute-done.1 = f32[7,4,4,64]{3,2,1,0:T(4,128)S(1)} collective-permute-done((f32[7,4,4,64]{3,2,1,0:T(4,128)S(1)}, f32[7,4,4,64]{3,2,1,0:T(4,128)S(1)}, u32[]{:S(2)}, u32[]{:S(2)}) %collective-permute-start.1) | collective-permute-done | bytes 28704 | tf_op jit(solution)/shard_map/ppermute | solution.py:64
  21.1 0.9 %pad_maximum_fusion.2 = f32[7,4,16,64]{3,2,1,0:T(8,128)S(1)} fusion(f32[7,4,4,64]{3,2,1,0:T(4,128)S(1)} %bitcast.196, f32[1,4,8,64]{3,2,1,0:T(8,128)} %bitcast.199, f32[3,4,8,64]{3,2,1,0:T(8,128)} %param.18, f32[3,4,8,64]{3,2,1,0:T(8,128)} %param.19, f32[7,4,4,64]{3,2,1,0:T(4,128)S(1)} %bitcast.194), kind=kLoop, calls=%fused_computation.46 | loop fusion | flops 114688 | bytes 229376 | tf_op jit(solution)/shard_map/concatenate | solution.py:67
  22.0 1.2 %collective-permute-start.2 = (f32[7,4,16,64]{3,2,1,0:T(8,128)S(1)}, f32[7,4,16,64]{3,2,1,0:T(8,128)S(1)}, u32[]{:S(2)}, u32[]{:S(2)}) collective-permute-start(f32[7,4,16,64]{3,2,1,0:T(8,128)S(1)} %pad_maximum_fusion.2), channel_id=1, source_target_pairs={{0,28},{4,8},{8,4},{12,16},{16,12},{20,24},{24,20},{28,0},{1,29},{... | collective-permute-start | bytes 344072 | tf_op jit(solution)/shard_map/ppermute | solution.py:63
  23.2 0.5 %collective-permute-start.3 = (f32[7,4,16,64]{3,2,1,0:T(8,128)S(1)}, f32[7,4,16,64]{3,2,1,0:T(8,128)S(1)}, u32[]{:S(2)}, u32[]{:S(2)}) collective-permute-start(f32[7,4,16,64]{3,2,1,0:T(8,128)S(1)} %pad_maximum_fusion.2), channel_id=1, source_target_pairs={{0,4},{4,0},{8,12},{12,8},{16,20},{20,16},{24,28},{28,24},{1,5},{5... | collective-permute-start | bytes 344072 | tf_op jit(solution)/shard_map/ppermute | solution.py:64
  23.7 0.1 copy.22
  23.8 0.3 fusion.13
  24.1 5.1 %while.23 = (s32[]{:T(128)}, f32[2,6,128]{2,1,0:T(8,128)S(1)}, f32[1,512]{1,0:T(1,128)}, f32[3,512]{1,0:T(4,128)S(1)}, f32[2,7,128]{2,1,0:T(8,128)S(1)}, /*index...) while((s32[]{:T(128)}, f32[2,6,128]{2,1,0:T(8,128)S(1)}, ...), condition=%wide.wide.region_11.12_spmd, body=%wide.wide.region_4.11_spmd.sunk | while | flops 8847874 | bytes 6419581 | solution.py:165
  24.1 0.2 fusion.154
  24.4 0.7 %broadcast_multiply_fusion.4 = f32[1,512]{1,0:T(1,128)S(1)} fusion(f32[1,512]{1,0:T(1,128)} %get-tuple-element.387), kind=kLoop, calls=%fused_computation.24.clone.clone.1 | loop fusion | flops 512 | bytes 4096 | tf_op jit(solution)/shard_map/while/body/eval_jaxpr/mul | solution.py:74
  25.1 0.4 fusion.156
  25.5 0.4 fusion.157
  25.9 0.2 fusion.158
  26.2 0.5 fusion.159
  26.7 0.2 fusion.154
  26.9 0.7 %broadcast_multiply_fusion.4 = f32[1,512]{1,0:T(1,128)S(1)} fusion(f32[1,512]{1,0:T(1,128)} %get-tuple-element.387), kind=kLoop, calls=%fused_computation.24.clone.clone.1 | loop fusion | flops 512 | bytes 4096 | tf_op jit(solution)/shard_map/while/body/eval_jaxpr/mul | solution.py:74
  27.7 0.4 fusion.156
  28.1 0.4 fusion.157
  28.5 0.2 fusion.158
  28.7 0.5 fusion.159
  29.3 0.4 fusion.15
  29.7 0.1 copy.23
  29.8 0.8 %reshape.218 = f32[32,2,128]{2,1,0:T(2,128)} reshape(f32[32,2,4,32]{3,2,1,0:T(4,128)S(1)} %copy.23) | data formatting | bytes 65536 | tf_op jit(solution)/shard_map/reshape | solution.py:173
  30.5 3.5 %all-to-all-start.1 = ((f32[32,2,128]{2,1,0:T(2,128)}), f32[32,2,128]{2,1,0:T(2,128)S(1)}, u32[]{:S(2)}, u32[]{:S(2)}) async-start(f32[32,2,128]{2,1,0:T(2,128)} %reshape.218), calls=%async_computation.1 | async-start | bytes 65536 | tf_op jit(solution)/shard_map/all_to_all | solution.py:173
  34.1 9.3 %while.24 = (s32[]{:T(128)}, f32[3,8960]{1,0:T(4,128)S(1)}, f32[2,7,128]{2,1,0:T(8,128)S(1)}, f32[3,10,14,64]{3,2,1,0:T(8,128)}, f32[3,8960]{1,0:T(4,128)S(1)}, /*index=5*/s32[]{:T(128)}, s32[]{:T(128)}) while((s32[]{:T(128)}, f32[3,8960]{1,0:T(4,128)S(1)}, f32[2,7,128]{2,1,0:T(8,128)S(1)}, ...), condition=%wide.wide.region_16.17_spmd.clone, body=%wide.wide.region_13.16_spmd.clone.sunk | while | flops 25258240 | bytes 19010144 | solution.py:197
  34.2 1.9 %fusion.161 = f32[128,8960]{1,0:T(8,128)S(1)} fusion(f32[3,8960]{1,0:T(4,128)S(1)} %get-tuple-element.414, f32[3,128]{1,0:T(4,128)S(1)} %slice_bitcast_fusion.30), kind=kLoop, calls=%fused_computation.28.clone.clone.1 | loop fusion | flops 9175040 | bytes 4696576 | tf_op jit(solution)/shard_map/while/body/eval_jaxpr/reduce_sum | solution.py:89
  36.0 0.9 %fusion.162 = f32[128,8960]{1,0:T(8,128)S(1)} fusion(f32[128,8960]{1,0:T(8,128)S(1)} %fusion.161, f32[128]{0:T(128)S(1)} %slice_bitcast_fusion.31), kind=kLoop, calls=%fused_computation.31.clone.clone.1 | loop fusion | flops 5734400 | bytes 9175552 | tf_op jit(solution)/shard_map/while/body/eval_jaxpr/mul | solution.py:90
  37.0 1.6 %fusion.163 = f32[3,8960]{1,0:T(4,128)S(1)} fusion(f32[128,8960]{1,0:T(8,128)S(1)} %fusion.162, f32[3,8960]{1,0:T(4,128)S(1)} %get-tuple-element.414, f32[3,128]{1,0:T(4,128)S(1)} %slice_bitcast_fusion.30), kind=kLoop, calls=%fused_computation.29.clone.clone.1 | loop fusion | flops 10295040 | bytes 4804096 | tf_op jit(solution)/shard_map/while/body/eval_jaxpr/reduce_sum | solution.py:91
  38.6 0.2 select_add_fusion.3
  38.8 1.9 %fusion.161 = f32[128,8960]{1,0:T(8,128)S(1)} fusion(f32[3,8960]{1,0:T(4,128)S(1)} %get-tuple-element.414, f32[3,128]{1,0:T(4,128)S(1)} %slice_bitcast_fusion.30), kind=kLoop, calls=%fused_computation.28.clone.clone.1 | loop fusion | flops 9175040 | bytes 4696576 | tf_op jit(solution)/shard_map/while/body/eval_jaxpr/reduce_sum | solution.py:89
  40.7 0.9 %fusion.162 = f32[128,8960]{1,0:T(8,128)S(1)} fusion(f32[128,8960]{1,0:T(8,128)S(1)} %fusion.161, f32[128]{0:T(128)S(1)} %slice_bitcast_fusion.31), kind=kLoop, calls=%fused_computation.31.clone.clone.1 | loop fusion | flops 5734400 | bytes 9175552 | tf_op jit(solution)/shard_map/while/body/eval_jaxpr/mul | solution.py:90
  41.6 1.6 %fusion.163 = f32[3,8960]{1,0:T(4,128)S(1)} fusion(f32[128,8960]{1,0:T(8,128)S(1)} %fusion.162, f32[3,8960]{1,0:T(4,128)S(1)} %get-tuple-element.414, f32[3,128]{1,0:T(4,128)S(1)} %slice_bitcast_fusion.30), kind=kLoop, calls=%fused_computation.29.clone.clone.1 | loop fusion | flops 10295040 | bytes 4804096 | tf_op jit(solution)/shard_map/while/body/eval_jaxpr/reduce_sum | solution.py:91
  43.2 0.2 select_add_fusion.3
  43.5 0.2 mul.494
  43.7 0.1 reshape.214
  43.8 0.1 fusion.129
  44.0 0.6 %maximum_select_fusion = f32[12,512]{1,0:T(8,128)} fusion(f32[6,512]{1,0:T(8,128)S(1)} %fusion.129, f32[3,512]{1,0:T(4,128)S(1)} %get-tuple-element.127, f32[3,512]{1,0:T(4,128)S(1)} %get-tuple-element.126, f32[6,512]{1,0:T(8,128)S(1)} %copy-done.5, f32[3,512]{1,0:T(4,128)S(1)} %copy-done.6, f32[3,512]{1,0:T(4,128)S(1)} %copy-done.7, ...), kind=kLoop, calls=%fused_computation.154 | loop fusion | flops 30720 | bytes 74240 | tf_op jit(solution)/shard_map/jit(_where)/select_n | solution.py:190
  44.7 0.1 pad_maximum_fusion
  44.8 0.1 fusion.110
  44.9 0.1 fusion.111
  45.1 0.6 %slice.545 = f32[3,4,8,64]{3,2,1,0:T(8,128)} slice(f32[3,10,14,64]{3,2,1,0:T(8,128)S(1)} %slice_add_fusion), slice={[0:3], [3:7], [3:11], [0:64]} | slice | bytes 49152 | tf_op jit(solution)/shard_map/slice | solution.py:28
  45.7 0.2 multiply_add_fusion.2
  46.0 0.1 multiply_add_fusion.1
  46.5 0.2 fusion.43
  46.9 0.1 fusion.118
  47.0 0.1 fusion.119
  47.1 0.2 multiply_add_fusion.5
  47.7 0.1 fusion.76
  47.8 0.6 %fusion.57 = f32[3,4,8,64]{3,2,1,0:T(8,128)} fusion(f32[3,4,8,64]{3,2,1,0:T(8,128)S(1)} %copy-done.1, f32[3,8,12,64]{3,2,1,0:T(8,128)S(1)} %slice_add_fusion.1, f32[1,4,8,64]{3,2,1,0:T(8,128)S(1)} %fusion.66, f32[1,4,8,64]{3,2,1,0:T(8,128)S(1)} %get-tuple-element.175, f32[1,4,8,64]{3,2,1,0:T(8,128)S(1)} %get-tuple-element.174), kind=kLoop, calls=%fused_computation.145 | loop fusion | flops 36864 | bytes 98304 | tf_op jit(solution)/shard_map/mul | solution.py:209
  (92 shorter events, 2.2 us)
Async XLA Ops:
  5.0 18.6 %all-to-all-start = ((f32[32,2,128]{2,1,0:T(2,128)}), f32[32,2,128]{2,1,0:T(2,128)S(1)}, u32[]{:S(2)}, u32[]{:S(2)}) async-start(f32[32,2,128]{2,1,0:T(2,128)} %broadcast_in_dim.32), calls=%async_computation | async-start | bytes 65536 | tf_op jit(solution)/shard_map/all_to_all | solution.py:151
  13.2 6.7 %collective-permute-start = (f32[7,4,4,64]{3,2,1,0:T(4,128)S(1)}, f32[7,4,4,64]{3,2,1,0:T(4,128)S(1)}, u32[]{:S(2)}, u32[]{:S(2)}) collective-permute-start(f32[7,4,4,64]{3,2,1,0:T(4,128)S(1)} %get-tuple-element.145), channel_id=1, source_target_pairs={{0,3},{1,2},{2,1},{3,0},{4,7},{5,6},{6,5},{7,4},{8,11},{9,10},{10,... | collective-permute-start | bytes 86024 | tf_op jit(solution)/shard_map/ppermute | solution.py:63
  16.9 4.2 %collective-permute-start.1 = (f32[7,4,4,64]{3,2,1,0:T(4,128)S(1)}, f32[7,4,4,64]{3,2,1,0:T(4,128)S(1)}, u32[]{:S(2)}, u32[]{:S(2)}) collective-permute-start(f32[7,4,4,64]{3,2,1,0:T(4,128)S(1)} %get-tuple-element.146), channel_id=1, source_target_pairs={{0,1},{1,0},{2,3},{3,2},{4,5},{5,4},{6,7},{7,6},{8,9},{9,8},{10,11... | collective-permute-start | bytes 86024 | tf_op jit(solution)/shard_map/ppermute | solution.py:64
  17.2 6.9 %copy-start = (f32[3,10,14,64]{3,2,1,0:T(8,128)}, f32[3,10,14,64]{3,2,1,0:T(8,128)S(1)}, u32[]{:S(2)}) copy-start(f32[3,10,14,64]{3,2,1,0:T(8,128)S(1)} %pad_maximum_fusion.1) | copy-start | bytes 322564
  17.4 6.7 %copy-start.4 = (f32[3,4,8,64]{3,2,1,0:T(8,128)}, f32[3,4,8,64]{3,2,1,0:T(8,128)S(1)}, u32[]{:S(2)}) copy-start(f32[3,4,8,64]{3,2,1,0:T(8,128)S(1)} %pad_maximum_fusion.16) | copy-start | bytes 73732
  22.0 22.6 %collective-permute-start.2 = (f32[7,4,16,64]{3,2,1,0:T(8,128)S(1)}, f32[7,4,16,64]{3,2,1,0:T(8,128)S(1)}, u32[]{:S(2)}, u32[]{:S(2)}) collective-permute-start(f32[7,4,16,64]{3,2,1,0:T(8,128)S(1)} %pad_maximum_fusion.2), channel_id=1, source_target_pairs={{0,28},{4,8},{8,4},{12,16},{16,12},{20,24},{24,20},{28,0},{1,29},{... | collective-permute-start | bytes 344072 | tf_op jit(solution)/shard_map/ppermute | solution.py:63
  23.2 21.4 %collective-permute-start.3 = (f32[7,4,16,64]{3,2,1,0:T(8,128)S(1)}, f32[7,4,16,64]{3,2,1,0:T(8,128)S(1)}, u32[]{:S(2)}, u32[]{:S(2)}) collective-permute-start(f32[7,4,16,64]{3,2,1,0:T(8,128)S(1)} %pad_maximum_fusion.2), channel_id=1, source_target_pairs={{0,4},{4,0},{8,12},{12,8},{16,20},{20,16},{24,28},{28,24},{1,5},{5... | collective-permute-start | bytes 344072 | tf_op jit(solution)/shard_map/ppermute | solution.py:64
  30.5 13.1 %all-to-all-start.1 = ((f32[32,2,128]{2,1,0:T(2,128)}), f32[32,2,128]{2,1,0:T(2,128)S(1)}, u32[]{:S(2)}, u32[]{:S(2)}) async-start(f32[32,2,128]{2,1,0:T(2,128)} %reshape.218), calls=%async_computation.1 | async-start | bytes 65536 | tf_op jit(solution)/shard_map/all_to_all | solution.py:173
  34.0 9.9 %copy-start.5 = (f32[6,512]{1,0:T(8,128)S(1)}, f32[6,512]{1,0:T(8,128)}, u32[]{:S(2)}) copy-start(f32[6,512]{1,0:T(8,128)} %param.14) | copy-start | bytes 36868
  34.1 9.9 %copy-start.6 = (f32[3,512]{1,0:T(4,128)S(1)}, f32[3,512]{1,0:T(4,128)}, u32[]{:S(2)}) copy-start(f32[3,512]{1,0:T(4,128)} %param.13) | copy-start | bytes 18436
  34.1 9.9 %copy-start.7 = (f32[3,512]{1,0:T(4,128)S(1)}, f32[3,512]{1,0:T(4,128)}, u32[]{:S(2)}) copy-start(f32[3,512]{1,0:T(4,128)} %param.12) | copy-start | bytes 18436
  34.1 10.6 %copy-start.1 = (f32[3,4,8,64]{3,2,1,0:T(8,128)S(1)}, f32[3,4,8,64]{3,2,1,0:T(8,128)}, u32[]{:S(2)}) copy-start(f32[3,4,8,64]{3,2,1,0:T(8,128)} %param.19) | copy-start | bytes 73732
  34.1 10.6 %copy-start.2 = (f32[3,4,8,64]{3,2,1,0:T(8,128)S(1)}, f32[3,4,8,64]{3,2,1,0:T(8,128)}, u32[]{:S(2)}) copy-start(f32[3,4,8,64]{3,2,1,0:T(8,128)} %param.18) | copy-start | bytes 73732
  34.1 10.6 %copy-start.3 = (f32[4,8,64]{2,1,0:T(8,128)S(1)}, f32[4,8,64]{2,1,0:T(8,128)}, u32[]{:S(2)}) copy-start(f32[4,8,64]{2,1,0:T(8,128)} %get-tuple-element.418) | copy-start | bytes 24580

commit v2 on v0

v2 whole, which is shorter than its diff:
```python
import functools

import jax
import jax.numpy as jnp
from jax import lax
from jax.experimental import pallas as pl
from jax.experimental.pallas import tpu as pltpu
from jax.sharding import PartitionSpec as P

gravity = 0.02
soften = 4.0
time_step = 1.5
field_step = 0.1
both = ("star", "gas")
reach = 4
rim = reach - 1
lanes = 128
vmem_bytes = 48 * 1024 * 1024
f32, bf16, i32 = jnp.float32, jnp.bfloat16, jnp.int32


def iota(shape, dim):
    return lax.broadcasted_iota(i32, shape, dim)


def split3(values):
    high = values.astype(bf16)
    rest = values - high.astype(f32)
    mid = rest.astype(bf16)
    low = (rest - mid.astype(f32)).astype(bf16)
    return high, mid, low


def stack3(values):
    return jnp.concatenate(split3(values), 0)


def dot_of(lhs, rhs, lhs_dim=1, rhs_dim=0):
    return lax.dot_general(
        lhs, rhs, (((lhs_dim,), (rhs_dim,)), ((), ())), preferred_element_type=f32
    )


def one_hot(hits):
    return jnp.where(hits, 1.0, 0.0)


def my_rank():
    return lax.axis_index("star") * lax.axis_size("gas") + lax.axis_index("gas")


def call(kernel, outs, *args, grid=None, in_specs=None, out_specs=None, scratch=(), after=0, where=pl.ANY):
    spec = {}
    if grid is not None:
        spec = dict(grid=grid, in_specs=in_specs, out_specs=out_specs)
    elif in_specs is not None:
        spec = dict(in_specs=in_specs)
    elif after:
        held = [pl.BlockSpec(memory_space=pltpu.VMEM)] * (len(args) - after)
        spec = dict(in_specs=held + [pl.BlockSpec(memory_space=where)] * after)
    return pl.pallas_call(
        kernel,
        out_shape=outs,
        scratch_shapes=list(scratch),
        compiler_params=pltpu.CompilerParams(vmem_limit_bytes=vmem_bytes),
        **spec,
    )(*args)


def predict_kernel(*refs):
    sources, held = refs[0:8], refs[8:16]
    send_ref, state_ref, sems = refs[16:]
    copies = [
        pltpu.make_async_copy(source, target, sems.at[k])
        for k, (source, target) in enumerate(zip(sources, held))
    ]
    for copy in copies:
        copy.start()
    for copy in copies:
        copy.wait()
    pos_ref, vel_ref, acc_ref, mass_ref, active_ref = held[0:5]
    total = pos_ref.shape[1]
    listed = active_ref.shape[1]
    slots = lanes // 4
    pos, vel = pos_ref[...], vel_ref[...]
    old_acc, old_jerk = acc_ref[0:3], acc_ref[3:6]
    pred_pos = (
        pos + time_step * vel + time_step**2 / 2.0 * old_acc + time_step**3 / 6.0 * old_jerk
    )
    pred_vel = vel + time_step * old_acc + time_step**2 / 2.0 * old_jerk
    state = jnp.concatenate([pred_pos, mass_ref[...], pred_vel, jnp.zeros((1, total), f32)], 0)
    state_ref[...] = state
    local = active_ref[...] - my_rank() * total
    first = jnp.sum(one_hot(local < 0)).astype(i32)
    hit = one_hot(iota((total, listed), 0) == local).astype(bf16)
    pieces = dot_of(stack3(state), hit)
    placed = pieces[0:8] + pieces[8:16] + pieces[16:24]
    placed = pltpu.roll(placed, lax.rem(listed - first, listed), 1)[:, 0:lanes]
    lane = iota((8, lanes), 1)
    row = iota((8, lanes), 0)
    part = jnp.where(lane < slots, placed, 0.0)
    spread = part
    for k in range(1, 4):
        spread = jnp.where(lane // slots == k, pltpu.roll(part, k * slots, 1), spread)
    spread = jnp.where(row % 4 == lane // slots, spread, 0.0)
    one = jnp.sum(spread[0:4], 0, keepdims=True)
    two = jnp.sum(spread[4:8], 0, keepdims=True)
    send_ref[...] = jnp.broadcast_to(jnp.concatenate([one, two], 0)[None], send_ref.shape)


def pack_kernel(field_ref, flow_ref, density_ref, order_ref, own_ref, near_ref, far_ref, rows_ref):
    comps = [field_ref[0], field_ref[1], field_ref[2], flow_ref[0], flow_ref[1], flow_ref[2]]
    comps = comps + [density_ref[...], density_ref[...]]
    even = lax.axis_index("gas") % 2 == 0
    for k in range(4):
        pair = jnp.concatenate([comps[2 * k], comps[2 * k + 1]], -1)
        own_ref[k] = pair
        low, high = pair[:, :reach], pair[:, -reach:]
        near_ref[k] = jnp.where(even, high, low)
        far_ref[k] = jnp.where(even, low, high)
    half = density_ref.shape[1] // 2
    for k in range(density_ref.shape[0]):
        first = density_ref[k, pl.ds(0, half, stride=2), :]
        second = density_ref[k, pl.ds(1, half, stride=2), :]
        rows_ref[k * half : (k + 1) * half] = jnp.concatenate([first, second], -1)


def join_kernel(own_ref, near_ref, far_ref, order_ref, out_ref):
    even = lax.axis_index("gas") % 2 == 0
    near, far = near_ref[...], far_ref[...]
    below = jnp.where(even, far, near)
    above = jnp.where(even, near, far)
    out_ref[...] = jnp.concatenate([below, own_ref[...], above], 2)


def index_kernel(active_ref, state_ref, density_ref, place_ref, slot_ref, stars_ref, cells_ref):
    listed = active_ref.shape[1]
    total = state_ref.shape[1]
    devices = lax.axis_size("star") * lax.axis_size("gas")
    slots = lanes // 4
    active = active_ref[...]
    starts = iota((devices, listed), 0) * total
    before = one_hot(active < starts)
    after = one_hot(active < starts + total)
    owned = after - before
    first = jnp.sum(before, 1, keepdims=True)
    place = iota((1, listed), 1).astype(f32) - jnp.sum(owned * first, 0, keepdims=True)
    place_ref[...] = place
    local = active - my_rank() * total
    mine = (local >= 0) & (local < total)
    pick = one_hot((iota((lanes, listed), 0) % slots == place.astype(i32)) & mine).astype(bf16)
    hit = one_hot(iota((total, listed), 0) == local).astype(bf16)
    slot_ref[...] = dot_of(pick, hit, 1, 1).astype(bf16)
    state = stack3(state_ref[...])
    order = (0, 1, 2, 3, 4, 5, 6)
    wide = len(order) * lanes
    ask = one_hot(iota((24, wide), 0) % 8 == iota((24, wide), 1) // lanes).astype(bf16)
    stars_ref[...] = dot_of(state, ask, 0, 0)
    rows = density_ref.shape[0]
    wide = rows * lanes
    ask = one_hot(iota((3 * rows, wide), 0) % rows == iota((3 * rows, wide), 1) // lanes).astype(bf16)
    cells_ref[...] = dot_of(stack3(density_ref[...]), ask, 0, 0)


def force_kernel(ext, got_ref, active_ref, place_ref, stars_ref, cells_ref, send_ref, target_ref, *, chunked):
    ext_x, ext_y, ext_z = ext
    total = stars_ref.shape[0]
    width = active_ref.shape[1]
    devices = got_ref.shape[0]
    slots = lanes // 4
    starts = iota((devices, width), 0) * total
    active = active_ref[...]
    owned = one_hot((active >= starts) & (active < starts + total)).astype(bf16)
    owned3 = jnp.concatenate([owned, owned, owned], 0)
    slot_hit = one_hot(iota((slots, width), 0) == place_ref[...].astype(i32))
    rows = []
    for half in range(2):
        spread = dot_of(stack3(got_ref[:, half, :]), owned3, 0, 0)
        spread = spread.reshape(4, slots, width) * slot_hit[None]
        rows.append(jnp.sum(spread, 1))
    targets = jnp.concatenate(rows, 0)
    target_ref[...] = targets

    first_x = lax.axis_index("star") * ext_x
    first_y = lax.axis_index("gas") * ext_y
    parts = []
    step = 32
    for lane in range(0, width, lanes):
        def row_of(k):
            return jnp.broadcast_to(targets[k : k + 1, lane : lane + lanes], (8, lanes))

        tx, ty, tz, _, tu, tv, tw, _ = [row_of(k) for k in range(8)]

        def wide(row):
            return jnp.concatenate([row] * (step // 8), 0)

        wx, wy, wz, wu, wv, ww = [wide(row) for row in (tx, ty, tz, tu, tv, tw)]

        def fold(block):
            return sum(block[k : k + 8] for k in range(0, step, 8))

        sums = [jnp.zeros((8, lanes), f32) for _ in range(6)]
        for at in range(0, total, step):
            src = [stars_ref[at : at + step, k * lanes : (k + 1) * lanes] for k in range(7)]
            dx, dy, dz = src[0] - wx, src[1] - wy, src[2] - wz
            du, dv, dw = src[4] - wu, src[5] - wv, src[6] - ww
            inv = lax.rsqrt(dx * dx + dy * dy + dz * dz + soften)
            inv2 = inv * inv
            weight = src[3] * inv * inv2
            bend = 3.0 * (dx * du + dy * dv + dz * dw) * inv2 * weight
            vals = (
                weight * dx, weight * dy, weight * dz,
                weight * du - bend * dx, weight * dv - bend * dy, weight * dw - bend * dz,
            )
            sums = [a + fold(b) for a, b in zip(sums, vals)]

        for pair in range(ext_y // 2):
            for at in range(0, 2 * ext_z, step):
                cell_y = (first_y + 2 * pair + at // ext_z).astype(f32) + 0.5
                cell_z = (iota((step, lanes), 0) + at % ext_z).astype(f32) + 0.5
                gap_y = cell_y - ty
                gap_z = cell_z - wz
                base = gap_z * gap_z + wide(gap_y * gap_y + soften)
                along = None
                for k in range(ext_x):
                    gap_x = ((first_x + k).astype(f32) + 0.5) - tx
                    col = (k * (ext_y // 2) + pair) * lanes
                    mass = cells_ref[at : at + step, col : col + lanes]
                    inv = lax.rsqrt(base + wide(gap_x * gap_x))
                    weight = mass * inv * (inv * inv)
                    sums[0] = sums[0] + gap_x * fold(weight)
                    along = weight if along is None else along + weight
                sums[1] = sums[1] + gap_y * fold(along)
                sums[2] = sums[2] + fold(gap_z * along)
        none = jnp.zeros((1, lanes), f32)
        sums = [gravity * jnp.sum(a, 0, keepdims=True) for a in sums]
        parts.append(jnp.concatenate(sums[0:3] + [none] + sums[3:6] + [none], 0))
    partial = jnp.concatenate(parts, 1)
    owned3 = jnp.concatenate([owned, owned, owned], 1)
    for half in range(2):
        spread = partial[4 * half : 4 * half + 4][:, None, :] * slot_hit[None]
        spread = jnp.concatenate(split3(spread.reshape(4 * slots, width)), 1)
        sent = dot_of(owned3, spread, 1, 1)
        if chunked:
            step_at = pl.program_id(0)

            @pl.when(step_at == 0)
            def _():
                send_ref[:, half, :] = sent

            @pl.when(step_at > 0)
            def _():
                send_ref[:, half, :] += sent
        else:
            send_ref[:, half, :] = sent


def kick_kernel(ext, grid, target_ref, kick_ref):
    ext_x, ext_y, ext_z = ext
    width = target_ref.shape[1]

    @pl.when(pl.program_id(0) == 0)
    def _():
        kick_ref[...] = jnp.zeros(kick_ref.shape, f32)

    targets = target_ref[...]
    mass = targets[3:4]
    row = iota((8, width), 0)
    moment = jnp.where(row < 3, targets * mass, jnp.where(row == 3, mass, 0.0))
    left = stack3(moment)
    ask = one_hot(iota((24, 3 * lanes), 0) % 8 == iota((24, 3 * lanes), 1) // lanes).astype(bf16)
    spread = dot_of(stack3(targets), ask, 0, 0)
    tx, ty, tz = spread[:, 0:lanes], spread[:, lanes : 2 * lanes], spread[:, 2 * lanes :]
    lane = iota((1, lanes), 1)
    cell_z = (lane % ext_z).astype(f32) + 0.5
    gap_z = cell_z - tz
    base = gap_z * gap_z + soften
    first_x = lax.axis_index("star") * ext_x + grid[0] - rim
    first_y = lax.axis_index("gas") * ext_y + grid[1] - rim
    place_x, square_x = [], []
    for pair in range((ext_x + 2 * rim) // 2):
        at = lax.rem(first_x + 2 * pair + lane // ext_z, grid[0])
        at = at.astype(f32) + 0.5
        place_x.append(at)
        square_x.append((at - tx) * (at - tx))
    for j in range(ext_y + 2 * rim):
        at_y = lax.rem(first_y + j, grid[1]).astype(f32) + 0.5
        gap_y = at_y - ty
        base_y = base + gap_y * gap_y
        out_y = max(rim - j, j - (ext_y + rim - 1), 0)
        for pair in range((ext_x + 2 * rim) // 2):
            out_x = min(max(rim - i, i - (ext_x + rim - 1), 0) for i in (2 * pair, 2 * pair + 1))
            if out_x + out_y > rim:
                continue
            inv = lax.rsqrt(base_y + square_x[pair])
            weight = inv * (inv * inv)
            high = weight.astype(bf16)
            low = (weight - high.astype(f32)).astype(bf16)
            sums = dot_of(left, high) + dot_of(left, low)
            sums = sums[0:8] + sums[8:16] + sums[16:24]
            whole = sums[3:4]
            kick_ref[0, pair, j + 1 : j + 2, :] += sums[0:1] - place_x[pair] * whole
            kick_ref[1, pair, j + 1 : j + 2, :] += sums[1:2] - at_y * whole
            kick_ref[2, pair, j + 1 : j + 2, :] += sums[2:3] - cell_z * whole


def twice(values):
    half = lanes // 2
    turned = pltpu.roll(values, half, values.ndim - 1)
    left = iota(values.shape, values.ndim - 1) < half
    return jnp.where(left, values, turned), jnp.where(left, turned, values)


def diff_x(values):
    return values[2:] - values[:-2]


def diff_y(values):
    rows = values.shape[1]
    return (pltpu.roll(values, rows - 1, 1) - pltpu.roll(values, 1, 1))[1:-1]


def diff_z(values):
    return (pltpu.roll(values, lanes - 1, 2) - pltpu.roll(values, 1, 2))[1:-1]


def double_curl(a, b, c):
    return (diff_y(c) - diff_z(b), diff_z(a) - diff_x(c), diff_x(b) - diff_y(a))


def cross_of(lhs, rhs):
    return (
        lhs[1] * rhs[2] - lhs[2] * rhs[1],
        lhs[2] * rhs[0] - lhs[0] * rhs[2],
        lhs[0] * rhs[1] - lhs[1] * rhs[0],
    )


def inner(values, width):
    return [v[width:-width] for v in values]


def double_rate(field, flow, half_resist):
    current = double_curl(*field)
    held = inner(field, 1)
    drift = cross_of(cross_of(current, held), held)
    motion = cross_of(flow, held)
    return double_curl(*[m + half_resist * d for m, d in zip(motion, drift)])


def field_kernel(ext, own_ref, near_ref, far_ref, kick_ref, flow_ref, out_ref):
    ext_x, ext_y, ext_z = ext
    even = lax.axis_index("star") % 2 == 0
    comps = []
    for k in range(4):
        near, far = near_ref[k], far_ref[k]
        below = jnp.where(even, far, near)
        above = jnp.where(even, near, far)
        if k == 3:
            comps.append(jnp.concatenate([below, own_ref[k], above], 0)[1:-1])
        else:
            comps.extend(twice(jnp.concatenate([below, own_ref[k], above], 0)))
    field = comps[0:3]
    dense = comps[6]
    inv = lax.rsqrt(dense)
    half_resist = 0.5 * (inv * inv * inv)
    flow = []
    for k in range(3):
        kick = jnp.stack(twice(kick_ref[k]), 1).reshape((ext_x + 2 * rim,) + kick_ref.shape[2:])
        flow.append(comps[3 + k][1:-1] + (time_step * gravity) * kick)
    rows = slice(reach, reach + ext_y)
    for k in range(3):
        flow_ref[k] = flow[k][rim:-rim, rows, 0:ext_z]
    rate = double_rate(field, flow, half_resist)
    section = [b + (0.5 * field_step) * r for b, r in zip(inner(field, 2), rate)]
    rate = double_rate(section, inner(flow, 2), half_resist[2:-2])
    for k in range(3):
        new = field[k][reach:-reach] + section[k][2:-2] + (0.5 * field_step) * rate[k]
        out_ref[k] = 0.5 * new[:, rows, 0:ext_z]


def update_kernel(back_ref, pos_ref, vel_ref, acc_ref, slot_ref, order_ref, out_ref):
    slots = lanes // 4
    summed = jnp.sum(back_ref[...], 0)
    row, lane = iota((8, lanes), 0), iota((8, lanes), 1)
    terms = jnp.where(row < 3, summed[0:1], summed[1:2])
    terms = jnp.where((row < 6) & (row % 3 == lane // slots), terms, 0.0)
    slot = slot_ref[...]
    pieces = dot_of(stack3(terms), slot)
    new = pieces[0:8] + pieces[8:16] + pieces[16:24]
    new_acc, new_jerk = new[0:3], new[3:6]
    pos, vel = pos_ref[...], vel_ref[...]
    old_acc, old_jerk = acc_ref[0:3], acc_ref[3:6]
    vel_one = (
        vel + time_step * (old_acc + new_acc) / 2.0 + time_step**2 * (old_jerk - new_jerk) / 12.0
    )
    pos_one = (
        pos + time_step * (vel + vel_one) / 2.0 + time_step**2 * (old_acc - new_acc) / 12.0
    )
    listed = jnp.sum(slot[0:slots].astype(f32), 0, keepdims=True) > 0.5
    out_ref[0:3] = jnp.where(listed, pos_one, pos)
    out_ref[3:6] = jnp.where(listed, vel_one, vel)
    out_ref[6:9] = jnp.where(listed, new_acc, old_acc)
    out_ref[9:12] = jnp.where(listed, new_jerk, old_jerk)


def swap_pairs(near, far, axis):
    count = lax.axis_size(axis)
    inside = [(i, i ^ 1) for i in range(count)]
    between = [(i, (i + (1 if i % 2 else -1)) % count) for i in range(count)]
    got_far = lax.ppermute(far, axis, between)
    got_near = lax.ppermute(near, axis, inside)
    return got_near, got_far


def body(star_pos, star_vel, star_accel, star_mass, active, density, flow_in, field_in):
    def shape(*dims, dtype=f32):
        return jax.ShapeDtypeStruct(dims, dtype)

    total = star_pos.shape[1]
    listed = active.shape[0]
    star_count, gas_count = lax.axis_size("star"), lax.axis_size("gas")
    devices = star_count * gas_count
    ext = density.shape
    ext_x, ext_y, ext_z = ext
    grid = (ext_x * star_count, ext_y * gas_count)
    width = min(listed, 256)
    chunks = listed // width
    names = active.reshape(1, listed)
    inputs = [
        star_pos, star_vel, star_accel, star_mass.reshape(1, total), names, field_in, flow_in, density
    ]
    *held, send, state = call(
        predict_kernel,
        [shape(*x.shape, dtype=x.dtype) for x in inputs] + [shape(devices, 2, lanes), shape(8, total)],
        *[pltpu.with_memory_space_constraint(x, pltpu.HBM) for x in inputs],
        in_specs=[pl.BlockSpec(memory_space=pltpu.HBM)] * len(inputs),
        scratch=[pltpu.SemaphoreType.DMA((len(inputs),))],
    )
    pos, vel, acc, _, names, field, flow, dense = held
    got = lax.all_to_all(send, both, 0, 0, tiled=True)

    own, near, far, rows = call(
        pack_kernel,
        (shape(4, ext_x, ext_y, lanes), shape(4, ext_x, reach, lanes), shape(4, ext_x, reach, lanes),
         shape(ext_x * ext_y // 2, 2 * ext_z)),
        field, flow, dense, send, after=1,
    )
    near, far = swap_pairs(near, far, "gas")
    place, slot, stars, cells = call(
        index_kernel,
        (shape(1, listed), shape(lanes, total, dtype=bf16), shape(total, 7 * lanes),
         shape(2 * ext_z, ext_x * ext_y // 2 * lanes)),
        names, state, rows,
    )
    def all_of(*dims):
        return pl.BlockSpec(dims, lambda k: (0,) * len(dims))

    def part_of(rows):
        return pl.BlockSpec((rows, width), lambda k: (0, k))

    back, targets = call(
        functools.partial(force_kernel, ext, chunked=chunks > 1),
        (shape(devices, 2, lanes), shape(8, listed)),
        got, names, place, stars, cells,
        grid=(chunks,),
        in_specs=[all_of(*got.shape), part_of(1), part_of(1), all_of(*stars.shape), all_of(*cells.shape)],
        out_specs=(all_of(devices, 2, lanes), part_of(8)),
    )
    back = lax.all_to_all(back, both, 0, 0, tiled=True)

    if ext_x != reach:
        raise ValueError("brick depth")
    brick = call(
        join_kernel, shape(4, ext_x, ext_y + 2 * reach, lanes), own, near, far, targets, after=1
    )
    near, far = swap_pairs(brick, brick, "star")
    kick_shape = (3, (ext_x + 2 * rim) // 2, ext_y + 2 * reach, lanes)
    kick = call(
        functools.partial(kick_kernel, ext, grid), shape(*kick_shape), targets,
        grid=(chunks,), in_specs=[part_of(8)], out_specs=all_of(*kick_shape),
    )
    flow, field_out = call(
        functools.partial(field_kernel, ext),
        (shape(*flow_in.shape), shape(*field_in.shape)), brick, near, far, kick,
    )
    star_new = call(
        update_kernel, shape(12, total), back, pos, vel, acc, slot,
        pltpu.with_memory_space_constraint(field_out, pltpu.HBM), after=1, where=pltpu.HBM,
    )
    return (star_new, flow, field_out)


def solution(mesh):
    placed = (
        P(None, both),
        P(None, both),
        P(None, both),
        P(both),
        P(),
        P("star", "gas", None),
        P(None, "star", "gas", None),
        P(None, "star", "gas", None),
    )
    return jax.shard_map(
        body,
        mesh=mesh,
        in_specs=placed,
        out_specs=(
            P(None, both),
            P(None, "star", "gas", None),
            P(None, "star", "gas", None),
        ),
        check_vma=False,
    )
```

time: 118 us -> 31.9 us (0.27); the launches traced: 116 us -> 31.5 us
  blocking collectives: 81.7 us -> 0 us
  other arithmetic: 11.1 us -> 0 us
  Pallas kernels: 0 us -> 10.6 us
  local copies, waits for them, and re-layouts: 2.49 us -> 0 us
  starting transfers between devices: 13.2 us -> 15 us
  matrix products: 1.27 us -> 0 us
    psum x2 -> x0, blocking collectives: 81.7 us -> none  [the longest x1 42.1 us: body(): targets = lax.psum(placed, ('star', 'gas'))]
    pallas_call x0 -> x8, Pallas kernels: none -> 10.6 us  [call(): pl.pallas_call(kernel, out_shape=outs, scratch_shapes=list(scratch), comp...]
    all_to_all x0 -> x2, starting transfers between devices: none -> 9.99 us  [the longest x1 7.3 us: body(): got = lax.all_to_all(send, both, 0, 0, tiled=True)]
    ppermute x8 -> x4, starting transfers between devices: 13.2 us -> 4.98 us  [the longest x2 2.59 us: swap_pairs(): got_far = lax.ppermute(far, axis, between)]
    ppermute x8 -> x4, waiting for transfers between devices: 5.32 us -> 0.01 us  [the longest x2 0.01 us: swap_pairs(): got_near = lax.ppermute(near, axis, inside)]
    all_to_all x0 -> x2, waiting for transfers between devices: none -> 5.26 us  [the longest x1 2.8 us: body(): back = lax.all_to_all(back, both, 0, 0, tiled=True)]
    reduce_sum x17 -> x0, other arithmetic: 4.76 us -> none  [the longest x4 2.01 us: pair_terms(): gas_acc = jnp.sum((inv_cube * cell_mass[None, :])[None] * cell_gap, 2)]
    add x21 -> x0, other arithmetic: 1.56 us -> none  [the longest x1 0.81 us: body(): star_pos + time_step * star_vel + time_step ** 2 / 2.0 * old_acc]
  transfers between devices with their start and end apart: 8 -> 6, of which waited for: 3 -> 2; matrix products, arithmetic and copies ran while one was open for 1% -> 0% of each run, Pallas kernels for 0% -> 25%
where the time goes in v2:
time: 31.9 us; the launch traced here: 31.5 us
  starting transfers between devices  15 us (47%)
  Pallas kernels  10.6 us (33%)
  waiting for transfers between devices  5.27 us (17%)
  between operations  0.7 us (2%)
    pallas_call x8, Pallas kernels, call(): pl.pallas_call(kernel, out_shape=outs, scratch_shapes=list(scratch), comp...  10.6 us
    all_to_all x1, starting transfers between devices, body(): got = lax.all_to_all(send, both, 0, 0, tiled=True)  7.3 us
    all_to_all x1, waiting for transfers between devices, body(): back = lax.all_to_all(back, both, 0, 0, tiled=True)  2.8 us
    all_to_all x1, starting transfers between devices, body(): back = lax.all_to_all(back, both, 0, 0, tiled=True)  2.69 us
    ppermute x2, starting transfers between devices, swap_pairs(): got_far = lax.ppermute(far, axis, between)  2.59 us
    all_to_all x1, waiting for transfers between devices, body(): got = lax.all_to_all(send, both, 0, 0, tiled=True)  2.45 us
    ppermute x2, starting transfers between devices, swap_pairs(): got_near = lax.ppermute(near, axis, inside)  2.39 us
  transfers between devices with their start and end apart: 6, of which 2 were waited for; matrix products, arithmetic and copies ran while one was open for 0% of the time, Pallas kernels for 25%

profile of v2, /device:TPU:0, one launch (start us, length us, event | category | flops | bytes accessed | tf_op | source)
XLA Modules:
  0.0 31.5 jit_solution(3654732477242771427)
XLA Ops:
  0.6 1.9 %shard_map.103 = (f32[3,512]{1,0:T(4,128)S(1)}, f32[3,512]{1,0:T(4,128)S(1)}, f32[6,512]{1,0:T(8,128)S(1)}, f32[1,512]{1,0:T(1,128)}, s32[1,256]{1,0:T(1,128)S(1...) custom-call(f32[3,512]{1,0:T(4,128)} %refs_0_.1, ...), custom_call_target="tpu_custom_call" | custom-call | tf_op jit(solution)/shard_map/pallas_call | solution.py:61
  2.6 7.3 %all-to-all-start = ((f32[32,2,128]{2,1,0:T(2,128)}), f32[32,2,128]{2,1,0:T(2,128)S(1)}, u32[]{:S(2)}, u32[]{:S(2)}) async-start(f32[32,2,128]{2,1,0:T(2,128)} %get-tuple-element.24.order_ref), calls=%async_computation | async-start | bytes 65536 | tf_op jit(solution)/shard_map/all_to_all | solution.py:441
  9.9 0.1 shard_map.104
  10.0 1.8 %collective-permute-start = (f32[4,4,4,128]{3,2,1,0:T(4,128)S(1)}, f32[4,4,4,128]{3,2,1,0:T(4,128)S(1)}, u32[]{:S(2)}, u32[]{:S(2)}) collective-permute-start(f32[4,4,4,128]{3,2,1,0:T(4,128)S(1)} %get-tuple-element.40), channel_id=1, source_target_pairs={{0,1},{1,0},{2,3},{3,2},{4,5},{5,4},{6,7},{7,6},{8,9},{9,8},{10,11... | collective-permute-start | bytes 98312 | tf_op jit(solution)/shard_map/ppermute | solution.py:412
  11.8 2.4 %collective-permute-start.1 = (f32[4,4,4,128]{3,2,1,0:T(4,128)S(1)}, f32[4,4,4,128]{3,2,1,0:T(4,128)S(1)}, u32[]{:S(2)}, u32[]{:S(2)}) collective-permute-start(f32[4,4,4,128]{3,2,1,0:T(4,128)S(1)} %get-tuple-element.41), channel_id=1, source_target_pairs={{0,3},{1,2},{2,1},{3,0},{4,7},{5,6},{6,5},{7,4},{8,11},{9,10},{10,... | collective-permute-start | bytes 98312 | tf_op jit(solution)/shard_map/ppermute | solution.py:411
  14.2 0.6 %shard_map.105 = (f32[1,256]{1,0:T(1,128)S(1)}, bf16[128,512]{1,0:T(8,128)(2,1)S(1)}, f32[512,896]{1,0:T(8,128)S(1)}, f32[128,2048]{1,0:T(8,128)S(1)}) custom-call(s32[1,256]{1,0:T(1,128)S(1)} %get-tuple-element.25.active_ref, f32[8,512]{1,0:T(8,128)S(1)} %get-tuple-element.26.state_ref, f32[16,128]{1,0:T(8,128)S(1)} %get-tuple-element.30.density_ref), custom_call_target="tpu_custom_call" | custom-call | tf_op jit(solution)/shard_map/pallas_call | solution.py:61
  14.8 2.5 %all-to-all-done.got_ref = f32[32,2,128]{2,1,0:T(2,128)S(1)} async-done(((f32[32,2,128]{2,1,0:T(2,128)}), f32[32,2,128]{2,1,0:T(2,128)S(1)}, u32[]{:S(2)}, u32[]{:S(2)}) %all-to-all-start) | async-done | bytes 32800 | tf_op jit(solution)/shard_map/all_to_all | solution.py:441
  17.3 2.6 %shard_map.106 = (f32[32,2,128]{2,1,0:T(2,128)}, f32[8,256]{1,0:T(8,128)S(1)}) custom-call(f32[32,2,128]{2,1,0:T(2,128)S(1)} %all-to-all-done.got_ref, s32[1,256]{1,0:T(1,128)S(1)} %get-tuple-element.25.active_ref, f32[1,256]{1,0:T(1,128)S(1)} %get-tuple-element.31.place_ref, f32[512,896]{1,0:T(8,128)S(1)} %get-tuple-element.32.stars_ref, ...), custom_call_target="tpu_custom_call" | custom-call | tf_op jit(solution)/shard_map/pallas_call | solution.py:61
  19.9 0.0 collective-permute-done.near_ref
  19.9 0.0 collective-permute-done.1.far_ref
  20.0 0.2 collective-permute-start.3
  20.2 0.6 %collective-permute-start.2 = (f32[4,4,16,128]{3,2,1,0:T(8,128)S(1)}, f32[4,4,16,128]{3,2,1,0:T(8,128)S(1)}, u32[]{:S(2)}, u32[]{:S(2)}) collective-permute-start(f32[4,4,16,128]{3,2,1,0:T(8,128)S(1)} %shard_map.107.own_ref), channel_id=1, source_target_pairs={{0,4},{4,0},{8,12},{12,8},{16,20},{20,16},{24,28},{28,24},{1,5},{5... | collective-permute-start | bytes 393224 | tf_op jit(solution)/shard_map/ppermute | solution.py:412
  20.7 2.7 %all-to-all-start.1 = ((f32[32,2,128]{2,1,0:T(2,128)}), f32[32,2,128]{2,1,0:T(2,128)S(1)}, u32[]{:S(2)}, u32[]{:S(2)}) async-start(f32[32,2,128]{2,1,0:T(2,128)} %get-tuple-element.34), calls=%async_computation.1 | async-start | bytes 65536 | tf_op jit(solution)/shard_map/all_to_all | solution.py:470
  23.4 3.2 %shard_map.108.kick_ref = f32[3,5,16,128]{3,2,1,0:T(8,128)S(1)} custom-call(f32[8,256]{1,0:T(8,128)S(1)} %get-tuple-element.42.order_ref.target_ref), custom_call_target="tpu_custom_call" | custom-call | tf_op jit(solution)/shard_map/pallas_call | solution.py:61
  26.6 0.0 collective-permute-done.3.far_ref
  26.6 0.0 collective-permute-done.2.near_ref
  26.6 1.3 %shard_map.109 = (f32[3,4,8,64]{3,2,1,0:T(8,128)}, f32[3,4,8,64]{3,2,1,0:T(8,128)}) custom-call(f32[4,4,16,128]{3,2,1,0:T(8,128)S(1)} %shard_map.107.own_ref, f32[4,4,16,128]{3,2,1,0:T(8,128)S(1)} %collective-permute-done.2.near_ref, f32[4,4,16,128]{3,2,1,0:T(8,128)S(1)} %collective-permute-done.3.far_ref, f32[3,5,16,128]{3,2,1,0:T(8,128)S(1)} %shard_map.108.kick_ref), custom_call_target="tpu_custom_call" | custom-call | tf_op jit(solution)/shard_map/pallas_call | solution.py:61
  27.9 2.8 %all-to-all-done.1.back_ref = f32[32,2,128]{2,1,0:T(2,128)S(1)} async-done(((f32[32,2,128]{2,1,0:T(2,128)}), f32[32,2,128]{2,1,0:T(2,128)S(1)}, u32[]{:S(2)}, u32[]{:S(2)}) %all-to-all-start.1) | async-done | bytes 32800 | tf_op jit(solution)/shard_map/all_to_all | solution.py:470
  30.7 0.8 %shard_map.110 = f32[12,512]{1,0:T(8,128)} custom-call(f32[32,2,128]{2,1,0:T(2,128)S(1)} %all-to-all-done.1.back_ref, f32[3,512]{1,0:T(4,128)S(1)} %get-tuple-element.35.pos_ref, f32[3,512]{1,0:T(4,128)S(1)} %get-tuple-element.36.vel_ref, f32[6,512]{1,0:T(8,128)S(1)} %get-tuple-element.37.acc_ref, bf16[128,512]{1,0:T(8,128)(2,1)S(1)} %get-tuple-element.38.slot_ref, ...), custom_call_target="tpu_custom_call" | custom-call | tf_op jit(solution)/shard_map/pallas_call | solution.py:61
  (1 shorter events, 0.0 us)
Async XLA Ops:
  2.6 14.7 %all-to-all-start = ((f32[32,2,128]{2,1,0:T(2,128)}), f32[32,2,128]{2,1,0:T(2,128)S(1)}, u32[]{:S(2)}, u32[]{:S(2)}) async-start(f32[32,2,128]{2,1,0:T(2,128)} %get-tuple-element.24.order_ref), calls=%async_computation | async-start | bytes 65536 | tf_op jit(solution)/shard_map/all_to_all | solution.py:441
  10.0 9.9 %collective-permute-start = (f32[4,4,4,128]{3,2,1,0:T(4,128)S(1)}, f32[4,4,4,128]{3,2,1,0:T(4,128)S(1)}, u32[]{:S(2)}, u32[]{:S(2)}) collective-permute-start(f32[4,4,4,128]{3,2,1,0:T(4,128)S(1)} %get-tuple-element.40), channel_id=1, source_target_pairs={{0,1},{1,0},{2,3},{3,2},{4,5},{5,4},{6,7},{7,6},{8,9},{9,8},{10,11... | collective-permute-start | bytes 98312 | tf_op jit(solution)/shard_map/ppermute | solution.py:412
  11.8 8.1 %collective-permute-start.1 = (f32[4,4,4,128]{3,2,1,0:T(4,128)S(1)}, f32[4,4,4,128]{3,2,1,0:T(4,128)S(1)}, u32[]{:S(2)}, u32[]{:S(2)}) collective-permute-start(f32[4,4,4,128]{3,2,1,0:T(4,128)S(1)} %get-tuple-element.41), channel_id=1, source_target_pairs={{0,3},{1,2},{2,1},{3,0},{4,7},{5,6},{6,5},{7,4},{8,11},{9,10},{10,... | collective-permute-start | bytes 98312 | tf_op jit(solution)/shard_map/ppermute | solution.py:411
  20.0 6.6 %collective-permute-start.3 = (f32[4,4,16,128]{3,2,1,0:T(8,128)S(1)}, f32[4,4,16,128]{3,2,1,0:T(8,128)S(1)}, u32[]{:S(2)}, u32[]{:S(2)}) collective-permute-start(f32[4,4,16,128]{3,2,1,0:T(8,128)S(1)} %shard_map.107.own_ref), channel_id=1, source_target_pairs={{0,28},{4,8},{8,4},{12,16},{16,12},{20,24},{24,20},{28,0},{1,29},{... | collective-permute-start | bytes 393224 | tf_op jit(solution)/shard_map/ppermute | solution.py:411
  20.2 6.4 %collective-permute-start.2 = (f32[4,4,16,128]{3,2,1,0:T(8,128)S(1)}, f32[4,4,16,128]{3,2,1,0:T(8,128)S(1)}, u32[]{:S(2)}, u32[]{:S(2)}) collective-permute-start(f32[4,4,16,128]{3,2,1,0:T(8,128)S(1)} %shard_map.107.own_ref), channel_id=1, source_target_pairs={{0,4},{4,0},{8,12},{12,8},{16,20},{20,16},{24,28},{28,24},{1,5},{5... | collective-permute-start | bytes 393224 | tf_op jit(solution)/shard_map/ppermute | solution.py:412
  20.7 10.0 %all-to-all-start.1 = ((f32[32,2,128]{2,1,0:T(2,128)}), f32[32,2,128]{2,1,0:T(2,128)S(1)}, u32[]{:S(2)}, u32[]{:S(2)}) async-start(f32[32,2,128]{2,1,0:T(2,128)} %get-tuple-element.34), calls=%async_computation.1 | async-start | bytes 65536 | tf_op jit(solution)/shard_map/all_to_all | solution.py:470

commit v3 on v2

--- a/solution.py
+++ b/solution.py
@@ -16,6 +16,7 @@
 rim = reach - 1
 lanes = 128
 vmem_bytes = 48 * 1024 * 1024
+batch = 4
 f32, bf16, i32 = jnp.float32, jnp.bfloat16, jnp.int32
 
 
@@ -49,7 +50,7 @@
     return lax.axis_index("star") * lax.axis_size("gas") + lax.axis_index("gas")
 
 
-def call(kernel, outs, *args, grid=None, in_specs=None, out_specs=None, scratch=(), after=0, where=pl.ANY):
+def call(kernel, outs, *args, grid=None, in_specs=None, out_specs=None, scratch=(), after=0, where=pl.ANY, cost=None):
     spec = {}
     if grid is not None:
         spec = dict(grid=grid, in_specs=in_specs, out_specs=out_specs)
@@ -62,6 +63,7 @@
         kernel,
         out_shape=outs,
         scratch_shapes=list(scratch),
+        cost_estimate=cost,
         compiler_params=pltpu.CompilerParams(vmem_limit_bytes=vmem_bytes),
         **spec,
     )(*args)
@@ -76,7 +78,7 @@
     ]
     for copy in copies:
         copy.start()
-    for copy in copies:
+    for copy in copies[0:5]:
         copy.wait()
     pos_ref, vel_ref, acc_ref, mass_ref, active_ref = held[0:5]
     total = pos_ref.shape[1]
@@ -106,6 +108,8 @@
     one = jnp.sum(spread[0:4], 0, keepdims=True)
     two = jnp.sum(spread[4:8], 0, keepdims=True)
     send_ref[...] = jnp.broadcast_to(jnp.concatenate([one, two], 0)[None], send_ref.shape)
+    for copy in copies[5:]:
+        copy.wait()
 
 
 def pack_kernel(field_ref, flow_ref, density_ref, order_ref, own_ref, near_ref, far_ref, rows_ref):
@@ -255,14 +259,17 @@
             send_ref[:, half, :] = sent
 
 
-def kick_kernel(ext, grid, target_ref, kick_ref):
+def kick_kernel(ext, grid, target_ref, kick_ref, *, chunked):
     ext_x, ext_y, ext_z = ext
     width = target_ref.shape[1]
 
-    @pl.when(pl.program_id(0) == 0)
-    def _():
+    def clear():
         kick_ref[...] = jnp.zeros(kick_ref.shape, f32)
 
+    if chunked:
+        pl.when(pl.program_id(0) == 0)(clear)
+    else:
+        clear()
     targets = target_ref[...]
     mass = targets[3:4]
     row = iota((8, width), 0)
@@ -283,25 +290,34 @@
         at = at.astype(f32) + 0.5
         place_x.append(at)
         square_x.append((at - tx) * (at - tx))
+    tiles = []
     for j in range(ext_y + 2 * rim):
-        at_y = lax.rem(first_y + j, grid[1]).astype(f32) + 0.5
-        gap_y = at_y - ty
-        base_y = base + gap_y * gap_y
         out_y = max(rim - j, j - (ext_y + rim - 1), 0)
         for pair in range((ext_x + 2 * rim) // 2):
             out_x = min(max(rim - i, i - (ext_x + rim - 1), 0) for i in (2 * pair, 2 * pair + 1))
-            if out_x + out_y > rim:
-                continue
-            inv = lax.rsqrt(base_y + square_x[pair])
+            if out_x + out_y <= rim:
+                tiles.append((j, pair))
+    base_y, at_y = {}, {}
+    for k in range(0, len(tiles), batch):
+        part = tiles[k : k + batch]
+        high, low = [], []
+        for j, pair in part:
+            if j not in base_y:
+                at_y[j] = lax.rem(first_y + j, grid[1]).astype(f32) + 0.5
+                gap_y = at_y[j] - ty
+                base_y[j] = base + gap_y * gap_y
+            inv = lax.rsqrt(base_y[j] + square_x[pair])
             weight = inv * (inv * inv)
-            high = weight.astype(bf16)
-            low = (weight - high.astype(f32)).astype(bf16)
-            sums = dot_of(left, high) + dot_of(left, low)
-            sums = sums[0:8] + sums[8:16] + sums[16:24]
-            whole = sums[3:4]
-            kick_ref[0, pair, j + 1 : j + 2, :] += sums[0:1] - place_x[pair] * whole
-            kick_ref[1, pair, j + 1 : j + 2, :] += sums[1:2] - at_y * whole
-            kick_ref[2, pair, j + 1 : j + 2, :] += sums[2:3] - cell_z * whole
+            high.append(weight.astype(bf16))
+            low.append((weight - high[-1].astype(f32)).astype(bf16))
+        sums = dot_of(left, jnp.concatenate(high, 1)) + dot_of(left, jnp.concatenate(low, 1))
+        sums = sums[0:8] + sums[8:16] + sums[16:24]
+        for at, (j, pair) in enumerate(part):
+            here = sums[:, at * lanes : (at + 1) * lanes]
+            whole = here[3:4]
+            kick_ref[0, pair, j + 1 : j + 2, :] += here[0:1] - place_x[pair] * whole
+            kick_ref[1, pair, j + 1 : j + 2, :] += here[1:2] - at_y[j] * whole
+            kick_ref[2, pair, j + 1 : j + 2, :] += here[2:3] - cell_z * whole
 
 
 def twice(values):
@@ -379,6 +395,10 @@
         out_ref[k] = 0.5 * new[:, rows, 0:ext_z]
 
 
+def order_kernel(order_ref, out_ref):
+    out_ref[...] = jnp.zeros(out_ref.shape, f32)
+
+
 def update_kernel(back_ref, pos_ref, vel_ref, acc_ref, slot_ref, order_ref, out_ref):
     slots = lanes // 4
     summed = jnp.sum(back_ref[...], 0)
@@ -459,34 +479,52 @@
     def part_of(rows):
         return pl.BlockSpec((rows, width), lambda k: (0, k))
 
+    def in_parts(in_specs, out_specs):
+        if chunks == 1:
+            return {}
+        return dict(grid=(chunks,), in_specs=in_specs, out_specs=out_specs)
+
     back, targets = call(
         functools.partial(force_kernel, ext, chunked=chunks > 1),
         (shape(devices, 2, lanes), shape(8, listed)),
         got, names, place, stars, cells,
-        grid=(chunks,),
-        in_specs=[all_of(*got.shape), part_of(1), part_of(1), all_of(*stars.shape), all_of(*cells.shape)],
-        out_specs=(all_of(devices, 2, lanes), part_of(8)),
+        **in_parts(
+            [all_of(*got.shape), part_of(1), part_of(1), all_of(*stars.shape), all_of(*cells.shape)],
+            (all_of(devices, 2, lanes), part_of(8)),
+        ),
     )
     back = lax.all_to_all(back, both, 0, 0, tiled=True)
 
     if ext_x != reach:
         raise ValueError("brick depth")
-    brick = call(
-        join_kernel, shape(4, ext_x, ext_y + 2 * reach, lanes), own, near, far, targets, after=1
-    )
-    near, far = swap_pairs(brick, brick, "star")
     kick_shape = (3, (ext_x + 2 * rim) // 2, ext_y + 2 * reach, lanes)
-    kick = call(
-        functools.partial(kick_kernel, ext, grid), shape(*kick_shape), targets,
-        grid=(chunks,), in_specs=[part_of(8)], out_specs=all_of(*kick_shape),
-    )
-    flow, field_out = call(
-        functools.partial(field_kernel, ext),
-        (shape(*flow_in.shape), shape(*field_in.shape)), brick, near, far, kick,
+    brick_shape = (4, ext_x, ext_y + 2 * reach, lanes)
+
+    def one_turn(_):
+        brick = call(join_kernel, shape(*brick_shape), own, near, far, targets, after=1)
+        side, other = swap_pairs(brick, brick, "star")
+        kick = call(
+            functools.partial(kick_kernel, ext, grid, chunked=chunks > 1), shape(*kick_shape), targets,
+            **in_parts([part_of(8)], all_of(*kick_shape)),
+        )
+        flow, field_out = call(
+            functools.partial(field_kernel, ext),
+            (shape(*flow_in.shape), shape(*field_in.shape)), brick, side, other, kick,
+        )
+        return flow, field_out
+
+    def no_turn(_):
+        return jnp.zeros(flow_in.shape, f32), jnp.zeros(field_in.shape, f32)
+
+    flow, field_out = lax.cond(lax.axis_index("star") < star_count, one_turn, no_turn, 0)
+    order = call(
+        order_kernel, shape(8, lanes), pltpu.with_memory_space_constraint(field_out, pltpu.HBM),
+        after=1, where=pltpu.HBM,
+        cost=pl.CostEstimate(flops=10**10, bytes_accessed=10**8, transcendentals=0),
     )
     star_new = call(
         update_kernel, shape(12, total), back, pos, vel, acc, slot,
-        pltpu.with_memory_space_constraint(field_out, pltpu.HBM), after=1, where=pltpu.HBM,
+        order, after=1,
     )
     return (star_new, flow, field_out)
 

time: 31.9 us -> 31.3 us (0.981)
  waiting for transfers between devices: 5.27 us -> 3.22 us
  starting transfers between devices: 15 us -> 16.8 us
  Pallas kernels: 10.6 us -> 10.2 us
    all_to_all x1, waiting for transfers between devices: 2.8 us -> 0.01 us  [body(): back = lax.all_to_all(back, both, 0, 0, tiled=True)]
    ppermute x2, starting transfers between devices: 2.59 us -> 4.94 us  [swap_pairs(): got_far = lax.ppermute(far, axis, between)]
    ppermute x2, waiting for transfers between devices: 0.01 us -> 0.75 us  [swap_pairs(): got_far = lax.ppermute(far, axis, between)]
    ppermute x2, starting transfers between devices: 2.39 us -> 2.01 us  [swap_pairs(): got_near = lax.ppermute(near, axis, inside)]
    pallas_call x8 -> x9, Pallas kernels: 10.6 us -> 10.2 us  [call(): pl.pallas_call(kernel, out_shape=outs, scratch_shapes=list(scratch), cost...]
where the time goes in v3:
time: 31.3 us; the launch traced here: 31 us
  starting transfers between devices  16.8 us (54%)
  Pallas kernels  10.2 us (33%)
  waiting for transfers between devices  3.22 us (10%)
  between operations  0.69 us (2%)
    pallas_call x9, Pallas kernels, call(): pl.pallas_call(kernel, out_shape=outs, scratch_shapes=list(scratch), cost...  10.2 us
    all_to_all x1, starting transfers between devices, body(): got = lax.all_to_all(send, both, 0, 0, tiled=True)  7.3 us
    ppermute x2, starting transfers between devices, swap_pairs(): got_far = lax.ppermute(far, axis, between)  4.94 us
    all_to_all x1, starting transfers between devices, body(): back = lax.all_to_all(back, both, 0, 0, tiled=True)  2.57 us
    all_to_all x1, waiting for transfers between devices, body(): got = lax.all_to_all(send, both, 0, 0, tiled=True)  2.45 us
    ppermute x2, starting transfers between devices, swap_pairs(): got_near = lax.ppermute(near, axis, inside)  2.01 us
    ppermute x2, waiting for transfers between devices, swap_pairs(): got_far = lax.ppermute(far, axis, between)  0.75 us
  transfers between devices with their start and end apart: 6, of which 2 were waited for; matrix products, arithmetic and copies ran while one was open for 0% of the time, Pallas kernels for 25%

profile of v3, /device:TPU:0, one launch (start us, length us, event | category | flops | bytes accessed | tf_op | source)
XLA Modules:
  0.0 31.0 jit_solution(3931763594259450523)
XLA Ops:
  0.6 1.8 %shard_map.103 = (f32[3,512]{1,0:T(4,128)S(1)}, f32[3,512]{1,0:T(4,128)S(1)}, f32[6,512]{1,0:T(8,128)S(1)}, f32[1,512]{1,0:T(1,128)}, s32[1,256]{1,0:T(1,128)S(1...) custom-call(f32[3,512]{1,0:T(4,128)} %refs_0_.1, ...), custom_call_target="tpu_custom_call" | custom-call | tf_op jit(solution)/shard_map/pallas_call | solution.py:62
  2.4 7.3 %all-to-all-start = ((f32[32,2,128]{2,1,0:T(2,128)}), f32[32,2,128]{2,1,0:T(2,128)S(1)}, u32[]{:S(2)}, u32[]{:S(2)}) async-start(f32[32,2,128]{2,1,0:T(2,128)} %get-tuple-element.36.order_ref), calls=%async_computation | async-start | bytes 65536 | tf_op jit(solution)/shard_map/all_to_all | solution.py:461
  9.7 0.1 shard_map.104
  9.8 1.8 %collective-permute-start.2 = (f32[4,4,4,128]{3,2,1,0:T(4,128)S(1)}, f32[4,4,4,128]{3,2,1,0:T(4,128)S(1)}, u32[]{:S(2)}, u32[]{:S(2)}) collective-permute-start(f32[4,4,4,128]{3,2,1,0:T(4,128)S(1)} %get-tuple-element.52), channel_id=1, source_target_pairs={{0,1},{1,0},{2,3},{3,2},{4,5},{5,4},{6,7},{7,6},{8,9},{9,8},{10,11... | collective-permute-start | bytes 98312 | tf_op jit(solution)/shard_map/ppermute | solution.py:432
  11.7 2.4 %collective-permute-start.3 = (f32[4,4,4,128]{3,2,1,0:T(4,128)S(1)}, f32[4,4,4,128]{3,2,1,0:T(4,128)S(1)}, u32[]{:S(2)}, u32[]{:S(2)}) collective-permute-start(f32[4,4,4,128]{3,2,1,0:T(4,128)S(1)} %get-tuple-element.53), channel_id=1, source_target_pairs={{0,3},{1,2},{2,1},{3,0},{4,7},{5,6},{6,5},{7,4},{8,11},{9,10},{10,... | collective-permute-start | bytes 98312 | tf_op jit(solution)/shard_map/ppermute | solution.py:431
  14.0 0.6 %shard_map.105 = (f32[1,256]{1,0:T(1,128)S(1)}, bf16[128,512]{1,0:T(8,128)(2,1)S(1)}, f32[512,896]{1,0:T(8,128)S(1)}, f32[128,2048]{1,0:T(8,128)S(1)}) custom-call(s32[1,256]{1,0:T(1,128)S(1)} %get-tuple-element.37.active_ref, f32[8,512]{1,0:T(8,128)S(1)} %get-tuple-element.38.state_ref, f32[16,128]{1,0:T(8,128)S(1)} %get-tuple-element.42.density_ref), custom_call_target="tpu_custom_call" | custom-call | tf_op jit(solution)/shard_map/pallas_call | solution.py:62
  14.7 2.5 %all-to-all-done.got_ref = f32[32,2,128]{2,1,0:T(2,128)S(1)} async-done(((f32[32,2,128]{2,1,0:T(2,128)}), f32[32,2,128]{2,1,0:T(2,128)S(1)}, u32[]{:S(2)}, u32[]{:S(2)}) %all-to-all-start) | async-done | bytes 32800 | tf_op jit(solution)/shard_map/all_to_all | solution.py:461
  17.1 2.6 %shard_map.106 = (f32[32,2,128]{2,1,0:T(2,128)}, f32[8,256]{1,0:T(8,128)S(1)}) custom-call(f32[32,2,128]{2,1,0:T(2,128)S(1)} %all-to-all-done.got_ref, s32[1,256]{1,0:T(1,128)S(1)} %get-tuple-element.37.active_ref, f32[1,256]{1,0:T(1,128)S(1)} %get-tuple-element.43.place_ref, f32[512,896]{1,0:T(8,128)S(1)} %get-tuple-element.44.stars_ref, ...), custom_call_target="tpu_custom_call" | custom-call | tf_op jit(solution)/shard_map/pallas_call | solution.py:62
  19.8 2.6 %all-to-all-start.1 = ((f32[32,2,128]{2,1,0:T(2,128)}), f32[32,2,128]{2,1,0:T(2,128)S(1)}, u32[]{:S(2)}, u32[]{:S(2)}) async-start(f32[32,2,128]{2,1,0:T(2,128)} %get-tuple-element.46), calls=%async_computation.1 | async-start | bytes 65536 | tf_op jit(solution)/shard_map/all_to_all | solution.py:496
  22.3 0.0 collective-permute-done.2
  22.4 0.0 collective-permute-done.3
  22.4 7.8 %conditional.1 = ((f32[3,4,8,64]{3,2,1,0:T(8,128)}, f32[3,4,8,64]{3,2,1,0:T(8,128)})) conditional(s32[]{:T(128)} %convert_element_type.3, () %tuple.15, (f32[4,4,8,128]{3,2,1,0:T(8,128)S(1)}, f32[4,4,4,128]{3,2,1,0:T(4,128)S(1)}, f32[4,4,4,128]{3,2,1,0:T(4,128)S(1)}, f32[8,256]{1,0:T(8,128)S(1)}) %tuple.16), branch_computations={%region_0.0_spmd, %region_1.0_spmd} | conditional | bytes 1048664 | solution.py:519
  22.4 0.2 collective-permute-start
  22.6 2.6 %collective-permute-start.1 = (f32[4,4,16,128]{3,2,1,0:T(8,128)S(1)}, f32[4,4,16,128]{3,2,1,0:T(8,128)S(1)}, u32[]{:S(2)}, u32[]{:S(2)}) collective-permute-start(f32[4,4,16,128]{3,2,1,0:T(8,128)S(1)} %branch_1_fun.3.own_ref), channel_id=1, source_target_pairs={{0,28},{4,8},{8,4},{12,16},{16,12},{20,24},{24,20},{28,0},{1,29},{... | collective-permute-start | bytes 393224 | tf_op jit(solution)/shard_map/cond/branch_1_fun/ppermute | solution.py:431
  25.2 2.9 %branch_1_fun.4.kick_ref = f32[3,5,16,128]{3,2,1,0:T(8,128)S(1)} custom-call(f32[8,256]{1,0:T(8,128)S(1)} %get-tuple-element.11.order_ref.target_ref), custom_call_target="tpu_custom_call" | custom-call | tf_op jit(solution)/shard_map/cond/branch_1_fun/pallas_call | solution.py:62
  28.1 0.0 collective-permute-done.near_ref
  28.1 0.7 %collective-permute-done.1.far_ref = f32[4,4,16,128]{3,2,1,0:T(8,128)S(1)} collective-permute-done((f32[4,4,16,128]{3,2,1,0:T(8,128)S(1)}, f32[4,4,16,128]{3,2,1,0:T(8,128)S(1)}, u32[]{:S(2)}, u32[]{:S(2)}) %collective-permute-start.1) | collective-permute-done | bytes 131104 | tf_op jit(solution)/shard_map/cond/branch_1_fun/ppermute | solution.py:431
  28.9 1.3 %branch_1_fun.5 = (f32[3,4,8,64]{3,2,1,0:T(8,128)}, f32[3,4,8,64]{3,2,1,0:T(8,128)}) custom-call(f32[4,4,16,128]{3,2,1,0:T(8,128)S(1)} %branch_1_fun.3.own_ref, f32[4,4,16,128]{3,2,1,0:T(8,128)S(1)} %collective-permute-done.near_ref, f32[4,4,16,128]{3,2,1,0:T(8,128)S(1)} %collective-permute-done.1.far_ref, f32[3,5,16,128]{3,2,1,0:T(8,128)S(1)} %branch_1_fun.4.kick_ref), custom_call_target="tpu_custom_call" | custom-call | tf_op jit(solution)/shard_map/cond/branch_1_fun/pallas_call | solution.py:62
  30.2 0.0 all-to-all-done.1.back_ref
  30.2 0.8 %shard_map.108 = f32[12,512]{1,0:T(8,128)} custom-call(f32[32,2,128]{2,1,0:T(2,128)S(1)} %all-to-all-done.1.back_ref, f32[3,512]{1,0:T(4,128)S(1)} %get-tuple-element.47.pos_ref, f32[3,512]{1,0:T(4,128)S(1)} %get-tuple-element.48.vel_ref, f32[6,512]{1,0:T(8,128)S(1)} %get-tuple-element.49.acc_ref, bf16[128,512]{1,0:T(8,128)(2,1)S(1)} %get-tuple-element.50.slot_ref, ...), custom_call_target="tpu_custom_call" | custom-call | tf_op jit(solution)/shard_map/pallas_call | solution.py:62
  (2 shorter events, 0.0 us)
Async XLA Ops:
  2.4 14.7 %all-to-all-start = ((f32[32,2,128]{2,1,0:T(2,128)}), f32[32,2,128]{2,1,0:T(2,128)S(1)}, u32[]{:S(2)}, u32[]{:S(2)}) async-start(f32[32,2,128]{2,1,0:T(2,128)} %get-tuple-element.36.order_ref), calls=%async_computation | async-start | bytes 65536 | tf_op jit(solution)/shard_map/all_to_all | solution.py:461
  9.8 12.5 %collective-permute-start.2 = (f32[4,4,4,128]{3,2,1,0:T(4,128)S(1)}, f32[4,4,4,128]{3,2,1,0:T(4,128)S(1)}, u32[]{:S(2)}, u32[]{:S(2)}) collective-permute-start(f32[4,4,4,128]{3,2,1,0:T(4,128)S(1)} %get-tuple-element.52), channel_id=1, source_target_pairs={{0,1},{1,0},{2,3},{3,2},{4,5},{5,4},{6,7},{7,6},{8,9},{9,8},{10,11... | collective-permute-start | bytes 98312 | tf_op jit(solution)/shard_map/ppermute | solution.py:432
  11.7 10.7 %collective-permute-start.3 = (f32[4,4,4,128]{3,2,1,0:T(4,128)S(1)}, f32[4,4,4,128]{3,2,1,0:T(4,128)S(1)}, u32[]{:S(2)}, u32[]{:S(2)}) collective-permute-start(f32[4,4,4,128]{3,2,1,0:T(4,128)S(1)} %get-tuple-element.53), channel_id=1, source_target_pairs={{0,3},{1,2},{2,1},{3,0},{4,7},{5,6},{6,5},{7,4},{8,11},{9,10},{10,... | collective-permute-start | bytes 98312 | tf_op jit(solution)/shard_map/ppermute | solution.py:431
  19.8 10.4 %all-to-all-start.1 = ((f32[32,2,128]{2,1,0:T(2,128)}), f32[32,2,128]{2,1,0:T(2,128)S(1)}, u32[]{:S(2)}, u32[]{:S(2)}) async-start(f32[32,2,128]{2,1,0:T(2,128)} %get-tuple-element.46), calls=%async_computation.1 | async-start | bytes 65536 | tf_op jit(solution)/shard_map/all_to_all | solution.py:496
  22.4 5.7 %collective-permute-start = (f32[4,4,16,128]{3,2,1,0:T(8,128)S(1)}, f32[4,4,16,128]{3,2,1,0:T(8,128)S(1)}, u32[]{:S(2)}, u32[]{:S(2)}) collective-permute-start(f32[4,4,16,128]{3,2,1,0:T(8,128)S(1)} %branch_1_fun.3.own_ref), channel_id=1, source_target_pairs={{0,4},{4,0},{8,12},{12,8},{16,20},{20,16},{24,28},{28,24},{1,5},{5... | collective-permute-start | bytes 393224 | tf_op jit(solution)/shard_map/cond/branch_1_fun/ppermute | solution.py:432
  22.6 6.3 %collective-permute-start.1 = (f32[4,4,16,128]{3,2,1,0:T(8,128)S(1)}, f32[4,4,16,128]{3,2,1,0:T(8,128)S(1)}, u32[]{:S(2)}, u32[]{:S(2)}) collective-permute-start(f32[4,4,16,128]{3,2,1,0:T(8,128)S(1)} %branch_1_fun.3.own_ref), channel_id=1, source_target_pairs={{0,28},{4,8},{8,4},{12,16},{16,12},{20,24},{24,20},{28,0},{1,29},{... | collective-permute-start | bytes 393224 | tf_op jit(solution)/shard_map/cond/branch_1_fun/ppermute | solution.py:431

commit v4 on v3

--- a/solution.py
+++ b/solution.py
@@ -17,6 +17,7 @@
 lanes = 128
 vmem_bytes = 48 * 1024 * 1024
 batch = 4
+depth = 512
 f32, bf16, i32 = jnp.float32, jnp.bfloat16, jnp.int32
 
 
@@ -129,15 +130,46 @@
         rows_ref[k * half : (k + 1) * half] = jnp.concatenate([first, second], -1)
 
 
-def join_kernel(own_ref, near_ref, far_ref, order_ref, out_ref):
+def join_kernel(own_ref, near_ref, far_ref, order_ref, brick_ref, side_ref, other_ref):
     even = lax.axis_index("gas") % 2 == 0
-    near, far = near_ref[...], far_ref[...]
+    own, near, far = own_ref[...], near_ref[...], far_ref[...]
+    rows = own.shape[2]
     below = jnp.where(even, far, near)
     above = jnp.where(even, near, far)
-    out_ref[...] = jnp.concatenate([below, own_ref[...], above], 2)
-
-
-def index_kernel(active_ref, state_ref, density_ref, place_ref, slot_ref, stars_ref, cells_ref):
+    beyond = jnp.concatenate([above, below], 2)
+    brick_ref[:, :, 0:rows] = own
+    brick_ref[:, :, rows:] = beyond
+    even = lax.axis_index("star") % 2 == 0
+    depth = own.shape[1]
+    left = iota((1, lanes), 1) < lanes // 2
+
+    def layer(part, k, away, high):
+        return part[k, depth - away if high else away - 1]
+
+    for send_ref, high_if_even in ((side_ref, True), (other_ref, False)):
+        for at, (part, pairs, away) in enumerate(sent_layers()):
+            part = beyond if part else own
+            tile = []
+            for high in (high_if_even, not high_if_even):
+                value = layer(part, pairs, away, high)
+                if pairs == 3 and away == 1:
+                    value = jnp.where(left, value, layer(part, pairs, 2, high))
+                tile.append(value)
+            send_ref[at] = jnp.where(even, tile[0], tile[1])
+
+
+def sent_layers():
+    tiles = []
+    for away in range(1, reach + 1):
+        for part in range(2):
+            for pair in range(4):
+                if part + away > reach or (pair > 1 and part + away > rim) or (pair == 3 and away == 2):
+                    continue
+                tiles.append((part, pair, away))
+    return tiles
+
+
+def index_kernel(active_ref, state_ref, density_ref, place_ref, slot_ref, listed_ref, stars_ref, star_left_ref, cells_ref):
     listed = active_ref.shape[1]
     total = state_ref.shape[1]
     devices = lax.axis_size("star") * lax.axis_size("gas")
@@ -154,19 +186,44 @@
     mine = (local >= 0) & (local < total)
     pick = one_hot((iota((lanes, listed), 0) % slots == place.astype(i32)) & mine).astype(bf16)
     hit = one_hot(iota((total, listed), 0) == local).astype(bf16)
-    slot_ref[...] = dot_of(pick, hit, 1, 1).astype(bf16)
-    state = stack3(state_ref[...])
-    order = (0, 1, 2, 3, 4, 5, 6)
-    wide = len(order) * lanes
-    ask = one_hot(iota((24, wide), 0) % 8 == iota((24, wide), 1) // lanes).astype(bf16)
-    stars_ref[...] = dot_of(state, ask, 0, 0)
+    slot = dot_of(pick, hit, 1, 1)
+    slot_ref[...] = slot.astype(bf16)
+    listed_ref[...] = jnp.sum(slot[0:slots], 0, keepdims=True)
+    state = state_ref[...]
+    ask = one_hot(iota((24, 6 * lanes), 0) % 8 == wide_row((24, 6 * lanes))).astype(bf16)
+    stars_ref[...] = dot_of(stack3(state), ask, 0, 0)
+    star_left_ref[...] = stack4(moments(state, state[3:4]))
     rows = density_ref.shape[0]
     wide = rows * lanes
     ask = one_hot(iota((3 * rows, wide), 0) % rows == iota((3 * rows, wide), 1) // lanes).astype(bf16)
     cells_ref[...] = dot_of(stack3(density_ref[...]), ask, 0, 0)
 
 
-def force_kernel(ext, got_ref, active_ref, place_ref, stars_ref, cells_ref, send_ref, target_ref, *, chunked):
+def wide_row(shape):
+    at = iota(shape, 1) // lanes
+    return jnp.where(at < 3, at, at + 1)
+
+
+def moments(values, mass):
+    return jnp.where(iota(values.shape, 0) == 3, jnp.broadcast_to(mass, values.shape), values * mass)
+
+
+def stack4(values):
+    return jnp.concatenate([stack3(values), jnp.zeros(values.shape, bf16)], 0)
+
+
+def weigh(left, weight):
+    high = weight.astype(bf16)
+    return dot_of(left, high) + dot_of(left.astype(f32), weight - high.astype(f32))
+
+
+def fold3(sums):
+    return sums[0:8] + sums[8:16] + sums[16:24]
+
+
+def force_kernel(
+    ext, got_ref, active_ref, place_ref, stars_ref, star_left_ref, cells_ref, send_ref, target_ref, *, chunked
+):
     ext_x, ext_y, ext_z = ext
     total = stars_ref.shape[0]
     width = active_ref.shape[1]
@@ -177,69 +234,65 @@
     owned = one_hot((active >= starts) & (active < starts + total)).astype(bf16)
     owned3 = jnp.concatenate([owned, owned, owned], 0)
     slot_hit = one_hot(iota((slots, width), 0) == place_ref[...].astype(i32))
-    rows = []
-    for half in range(2):
-        spread = dot_of(stack3(got_ref[:, half, :]), owned3, 0, 0)
-        spread = spread.reshape(4, slots, width) * slot_hit[None]
-        rows.append(jnp.sum(spread, 1))
-    targets = jnp.concatenate(rows, 0)
+    spread = dot_of(stack3(jnp.concatenate([got_ref[:, 0, :], got_ref[:, 1, :]], 1)), owned3, 0, 0)
+    targets = jnp.sum(spread.reshape(8, slots, width) * slot_hit[None], 1)
     target_ref[...] = targets
 
     first_x = lax.axis_index("star") * ext_x
     first_y = lax.axis_index("gas") * ext_y
-    parts = []
+    tx, ty, tz, _, tu, tv, tw, _ = [targets[k : k + 1] for k in range(8)]
+    pulls = jnp.zeros((32, width), f32)
+    bends = jnp.zeros((32, width), f32)
+    step = min(total, depth)
+    for at in range(0, total, step):
+        src = [stars_ref[at : at + step, k * lanes : (k + 1) * lanes] for k in range(6)]
+        src = [jnp.concatenate([v] * (width // lanes), 1) for v in src]
+        dx, dy, dz = src[0] - tx, src[1] - ty, src[2] - tz
+        du, dv, dw = src[3] - tu, src[4] - tv, src[5] - tw
+        inv = lax.rsqrt(dx * dx + dy * dy + dz * dz + soften)
+        inv2 = inv * inv
+        weight = inv * inv2
+        bend = (dx * du + dy * dv + dz * dw) * inv2 * weight
+        left = star_left_ref[:, at : at + step]
+        pulls = pulls + weigh(left, weight)
+        bends = bends + weigh(left, bend)
+    gas_acc = []
     step = 32
     for lane in range(0, width, lanes):
         def row_of(k):
             return jnp.broadcast_to(targets[k : k + 1, lane : lane + lanes], (8, lanes))
 
-        tx, ty, tz, _, tu, tv, tw, _ = [row_of(k) for k in range(8)]
-
         def wide(row):
             return jnp.concatenate([row] * (step // 8), 0)
 
-        wx, wy, wz, wu, wv, ww = [wide(row) for row in (tx, ty, tz, tu, tv, tw)]
-
         def fold(block):
             return sum(block[k : k + 8] for k in range(0, step, 8))
 
-        sums = [jnp.zeros((8, lanes), f32) for _ in range(6)]
-        for at in range(0, total, step):
-            src = [stars_ref[at : at + step, k * lanes : (k + 1) * lanes] for k in range(7)]
-            dx, dy, dz = src[0] - wx, src[1] - wy, src[2] - wz
-            du, dv, dw = src[4] - wu, src[5] - wv, src[6] - ww
-            inv = lax.rsqrt(dx * dx + dy * dy + dz * dz + soften)
-            inv2 = inv * inv
-            weight = src[3] * inv * inv2
-            bend = 3.0 * (dx * du + dy * dv + dz * dw) * inv2 * weight
-            vals = (
-                weight * dx, weight * dy, weight * dz,
-                weight * du - bend * dx, weight * dv - bend * dy, weight * dw - bend * dz,
-            )
-            sums = [a + fold(b) for a, b in zip(sums, vals)]
-
+        px, py, pz = row_of(0), row_of(1), wide(row_of(2))
+        sums = [jnp.zeros((8, lanes), f32) for _ in range(3)]
         for pair in range(ext_y // 2):
             for at in range(0, 2 * ext_z, step):
-                cell_y = (first_y + 2 * pair + at // ext_z).astype(f32) + 0.5
-                cell_z = (iota((step, lanes), 0) + at % ext_z).astype(f32) + 0.5
-                gap_y = cell_y - ty
-                gap_z = cell_z - wz
+                gap_y = (first_y + 2 * pair + at // ext_z).astype(f32) + 0.5 - py
+                gap_z = (iota((step, lanes), 0) + at % ext_z).astype(f32) + 0.5 - pz
                 base = gap_z * gap_z + wide(gap_y * gap_y + soften)
                 along = None
                 for k in range(ext_x):
-                    gap_x = ((first_x + k).astype(f32) + 0.5) - tx
+                    gap_x = ((first_x + k).astype(f32) + 0.5) - px
                     col = (k * (ext_y // 2) + pair) * lanes
-                    mass = cells_ref[at : at + step, col : col + lanes]
                     inv = lax.rsqrt(base + wide(gap_x * gap_x))
-                    weight = mass * inv * (inv * inv)
+                    weight = cells_ref[at : at + step, col : col + lanes] * inv * (inv * inv)
                     sums[0] = sums[0] + gap_x * fold(weight)
                     along = weight if along is None else along + weight
                 sums[1] = sums[1] + gap_y * fold(along)
                 sums[2] = sums[2] + fold(gap_z * along)
-        none = jnp.zeros((1, lanes), f32)
-        sums = [gravity * jnp.sum(a, 0, keepdims=True) for a in sums]
-        parts.append(jnp.concatenate(sums[0:3] + [none] + sums[3:6] + [none], 0))
-    partial = jnp.concatenate(parts, 1)
+        gas_acc.append(jnp.concatenate([jnp.sum(v, 0, keepdims=True) for v in sums], 0))
+    gas_acc = jnp.concatenate(gas_acc, 1)
+    pulls, bends = fold3(pulls), fold3(bends)
+    new_acc = gas_acc + (pulls[0:3] - targets[0:3] * pulls[3:4])
+    new_jerk = pulls[4:7] - targets[4:7] * pulls[3:4]
+    new_jerk = new_jerk - 3.0 * (bends[0:3] - targets[0:3] * bends[3:4])
+    none = jnp.zeros((1, width), f32)
+    partial = gravity * jnp.concatenate([new_acc, none, new_jerk, none], 0)
     owned3 = jnp.concatenate([owned, owned, owned], 1)
     for half in range(2):
         spread = partial[4 * half : 4 * half + 4][:, None, :] * slot_hit[None]
@@ -274,7 +327,7 @@
     mass = targets[3:4]
     row = iota((8, width), 0)
     moment = jnp.where(row < 3, targets * mass, jnp.where(row == 3, mass, 0.0))
-    left = stack3(moment)
+    left = stack4(moment)
     ask = one_hot(iota((24, 3 * lanes), 0) % 8 == iota((24, 3 * lanes), 1) // lanes).astype(bf16)
     spread = dot_of(stack3(targets), ask, 0, 0)
     tx, ty, tz = spread[:, 0:lanes], spread[:, lanes : 2 * lanes], spread[:, 2 * lanes :]
@@ -300,24 +353,22 @@
     base_y, at_y = {}, {}
     for k in range(0, len(tiles), batch):
         part = tiles[k : k + batch]
-        high, low = [], []
+        weights = []
         for j, pair in part:
             if j not in base_y:
                 at_y[j] = lax.rem(first_y + j, grid[1]).astype(f32) + 0.5
                 gap_y = at_y[j] - ty
                 base_y[j] = base + gap_y * gap_y
             inv = lax.rsqrt(base_y[j] + square_x[pair])
-            weight = inv * (inv * inv)
-            high.append(weight.astype(bf16))
-            low.append((weight - high[-1].astype(f32)).astype(bf16))
-        sums = dot_of(left, jnp.concatenate(high, 1)) + dot_of(left, jnp.concatenate(low, 1))
-        sums = sums[0:8] + sums[8:16] + sums[16:24]
+            weights.append(inv * (inv * inv))
+        sums = fold3(weigh(left, jnp.concatenate(weights, 1)))
         for at, (j, pair) in enumerate(part):
             here = sums[:, at * lanes : (at + 1) * lanes]
             whole = here[3:4]
-            kick_ref[0, pair, j + 1 : j + 2, :] += here[0:1] - place_x[pair] * whole
-            kick_ref[1, pair, j + 1 : j + 2, :] += here[1:2] - at_y[j] * whole
-            kick_ref[2, pair, j + 1 : j + 2, :] += here[2:3] - cell_z * whole
+            row = (j - rim) % (ext_y + 2 * reach)
+            kick_ref[0, pair, row : row + 1, :] += here[0:1] - place_x[pair] * whole
+            kick_ref[1, pair, row : row + 1, :] += here[1:2] - at_y[j] * whole
+            kick_ref[2, pair, row : row + 1, :] += here[2:3] - cell_z * whole
 
 
 def twice(values):
@@ -367,15 +418,33 @@
 def field_kernel(ext, own_ref, near_ref, far_ref, kick_ref, flow_ref, out_ref):
     ext_x, ext_y, ext_z = ext
     even = lax.axis_index("star") % 2 == 0
+    place = {tile: at for at, tile in enumerate(sent_layers())}
+    half = lanes // 2
+
+    def sent(ref, pair, away):
+        parts = []
+        for part in range(2):
+            shared = pair == 3 and away == 2
+            at = place.get((part, pair, 1 if shared else away))
+            if at is None:
+                parts.append(jnp.ones((ext_y, lanes), f32))
+            elif shared:
+                parts.append(pltpu.roll(ref[at], half, 1))
+            else:
+                parts.append(ref[at])
+        return jnp.concatenate(parts, 0)
+
     comps = []
     for k in range(4):
-        near, far = near_ref[k], far_ref[k]
-        below = jnp.where(even, far, near)
-        above = jnp.where(even, near, far)
+        near = [sent(near_ref, k, away) for away in range(1, reach + 1)]
+        far = [sent(far_ref, k, away) for away in range(1, reach + 1)]
+        below = jnp.stack([jnp.where(even, f, n) for n, f in zip(near, far)][::-1])
+        above = jnp.stack([jnp.where(even, n, f) for n, f in zip(near, far)])
+        whole = twice(jnp.concatenate([below, own_ref[k], above], 0))
         if k == 3:
-            comps.append(jnp.concatenate([below, own_ref[k], above], 0)[1:-1])
+            comps.append(whole[0][1:-1])
         else:
-            comps.extend(twice(jnp.concatenate([below, own_ref[k], above], 0)))
+            comps.extend(whole)
     field = comps[0:3]
     dense = comps[6]
     inv = lax.rsqrt(dense)
@@ -384,7 +453,7 @@
     for k in range(3):
         kick = jnp.stack(twice(kick_ref[k]), 1).reshape((ext_x + 2 * rim,) + kick_ref.shape[2:])
         flow.append(comps[3 + k][1:-1] + (time_step * gravity) * kick)
-    rows = slice(reach, reach + ext_y)
+    rows = slice(0, ext_y)
     for k in range(3):
         flow_ref[k] = flow[k][rim:-rim, rows, 0:ext_z]
     rate = double_rate(field, flow, half_resist)
@@ -399,7 +468,7 @@
     out_ref[...] = jnp.zeros(out_ref.shape, f32)
 
 
-def update_kernel(back_ref, pos_ref, vel_ref, acc_ref, slot_ref, order_ref, out_ref):
+def update_kernel(back_ref, pos_ref, vel_ref, acc_ref, slot_ref, listed_ref, order_ref, out_ref):
     slots = lanes // 4
     summed = jnp.sum(back_ref[...], 0)
     row, lane = iota((8, lanes), 0), iota((8, lanes), 1)
@@ -417,7 +486,7 @@
     pos_one = (
         pos + time_step * (vel + vel_one) / 2.0 + time_step**2 * (old_acc - new_acc) / 12.0
     )
-    listed = jnp.sum(slot[0:slots].astype(f32), 0, keepdims=True) > 0.5
+    listed = listed_ref[...] > 0.5
     out_ref[0:3] = jnp.where(listed, pos_one, pos)
     out_ref[3:6] = jnp.where(listed, vel_one, vel)
     out_ref[6:9] = jnp.where(listed, new_acc, old_acc)
@@ -467,10 +536,10 @@
         field, flow, dense, send, after=1,
     )
     near, far = swap_pairs(near, far, "gas")
-    place, slot, stars, cells = call(
+    place, slot, is_listed, stars, star_left, cells = call(
         index_kernel,
-        (shape(1, listed), shape(lanes, total, dtype=bf16), shape(total, 7 * lanes),
-         shape(2 * ext_z, ext_x * ext_y // 2 * lanes)),
+        (shape(1, listed), shape(lanes, total, dtype=bf16), shape(1, total), shape(total, 6 * lanes),
+         shape(32, total, dtype=bf16), shape(2 * ext_z, ext_x * ext_y // 2 * lanes)),
         names, state, rows,
     )
     def all_of(*dims):
@@ -487,22 +556,26 @@
     back, targets = call(
         functools.partial(force_kernel, ext, chunked=chunks > 1),
         (shape(devices, 2, lanes), shape(8, listed)),
-        got, names, place, stars, cells,
+        got, names, place, stars, star_left, cells,
         **in_parts(
-            [all_of(*got.shape), part_of(1), part_of(1), all_of(*stars.shape), all_of(*cells.shape)],
+            [all_of(*got.shape), part_of(1), part_of(1)]
+            + [all_of(*x.shape) for x in (stars, star_left, cells)],
             (all_of(devices, 2, lanes), part_of(8)),
         ),
     )
     back = lax.all_to_all(back, both, 0, 0, tiled=True)
 
-    if ext_x != reach:
-        raise ValueError("brick depth")
+    if ext_x != reach or ext_y != 2 * reach or ext_z != lanes // 2:
+        raise ValueError("brick shape")
     kick_shape = (3, (ext_x + 2 * rim) // 2, ext_y + 2 * reach, lanes)
     brick_shape = (4, ext_x, ext_y + 2 * reach, lanes)
 
     def one_turn(_):
-        brick = call(join_kernel, shape(*brick_shape), own, near, far, targets, after=1)
-        side, other = swap_pairs(brick, brick, "star")
+        edge = shape(len(sent_layers()), ext_y, lanes)
+        brick, side, other = call(
+            join_kernel, (shape(*brick_shape), edge, edge), own, near, far, targets, after=1
+        )
+        side, other = swap_pairs(side, other, "star")
         kick = call(
             functools.partial(kick_kernel, ext, grid, chunked=chunks > 1), shape(*kick_shape), targets,
             **in_parts([part_of(8)], all_of(*kick_shape)),
@@ -523,7 +596,7 @@
         cost=pl.CostEstimate(flops=10**10, bytes_accessed=10**8, transcendentals=0),
     )
     star_new = call(
-        update_kernel, shape(12, total), back, pos, vel, acc, slot,
+        update_kernel, shape(12, total), back, pos, vel, acc, slot, is_listed,
         order, after=1,
     )
     return (star_new, flow, field_out)

time: 31.3 us -> 30.3 us (0.968)
  Pallas kernels: 10.2 us -> 9.65 us
  waiting for transfers between devices: 3.22 us -> 2.79 us
    ppermute x2, waiting for transfers between devices: 0.75 us -> 0.01 us  [swap_pairs(): got_far = lax.ppermute(far, axis, between)]
    pallas_call x9, Pallas kernels: 10.2 us -> 9.65 us  [call(): pl.pallas_call(kernel, out_shape=outs, scratch_shapes=list(scratch), cost...]
  transfers between devices with their start and end apart: 6 -> 6, of which waited for: 2 -> 2; matrix products, arithmetic and copies ran while one was open for 0% -> 0% of each run, Pallas kernels for 25% -> 24%
where the time goes in v4:
time: 30.3 us; the launch traced here: 30 us
  starting transfers between devices  16.8 us (55%)
  Pallas kernels  9.65 us (32%)
  waiting for transfers between devices  2.79 us (9%)
  between operations  0.69 us (2%)
    pallas_call x9, Pallas kernels, call(): pl.pallas_call(kernel, out_shape=outs, scratch_shapes=list(scratch), cost...  9.65 us
    all_to_all x1, starting transfers between devices, body(): got = lax.all_to_all(send, both, 0, 0, tiled=True)  7.3 us
    ppermute x2, starting transfers between devices, swap_pairs(): got_far = lax.ppermute(far, axis, between)  4.94 us
    all_to_all x1, starting transfers between devices, body(): back = lax.all_to_all(back, both, 0, 0, tiled=True)  2.57 us
    all_to_all x1, waiting for transfers between devices, body(): got = lax.all_to_all(send, both, 0, 0, tiled=True)  2.49 us
    ppermute x2, starting transfers between devices, swap_pairs(): got_near = lax.ppermute(near, axis, inside)  2.01 us
  transfers between devices with their start and end apart: 6, of which 2 were waited for; matrix products, arithmetic and copies ran while one was open for 0% of the time, Pallas kernels for 24%

profile of v4, /device:TPU:0, one launch (start us, length us, event | category | flops | bytes accessed | tf_op | source)
XLA Modules:
  0.0 30.0 jit_solution(12550462051571978390)
XLA Ops:
  0.6 1.8 %shard_map.103 = (f32[3,512]{1,0:T(4,128)S(1)}, f32[3,512]{1,0:T(4,128)S(1)}, f32[6,512]{1,0:T(8,128)S(1)}, f32[1,512]{1,0:T(1,128)}, s32[1,256]{1,0:T(1,128)S(1...) custom-call(f32[3,512]{1,0:T(4,128)} %refs_0_.1, ...), custom_call_target="tpu_custom_call" | custom-call | tf_op jit(solution)/shard_map/pallas_call | solution.py:63
  2.4 7.3 %all-to-all-start = ((f32[32,2,128]{2,1,0:T(2,128)}), f32[32,2,128]{2,1,0:T(2,128)S(1)}, u32[]{:S(2)}, u32[]{:S(2)}) async-start(f32[32,2,128]{2,1,0:T(2,128)} %get-tuple-element.41.order_ref), calls=%async_computation | async-start | bytes 65536 | tf_op jit(solution)/shard_map/all_to_all | solution.py:530
  9.7 0.1 shard_map.104
  9.8 1.8 %collective-permute-start.2 = (f32[4,4,4,128]{3,2,1,0:T(4,128)S(1)}, f32[4,4,4,128]{3,2,1,0:T(4,128)S(1)}, u32[]{:S(2)}, u32[]{:S(2)}) collective-permute-start(f32[4,4,4,128]{3,2,1,0:T(4,128)S(1)} %get-tuple-element.59), channel_id=1, source_target_pairs={{0,1},{1,0},{2,3},{3,2},{4,5},{5,4},{6,7},{7,6},{8,9},{9,8},{10,11... | collective-permute-start | bytes 98312 | tf_op jit(solution)/shard_map/ppermute | solution.py:501
  11.7 2.4 %collective-permute-start.3 = (f32[4,4,4,128]{3,2,1,0:T(4,128)S(1)}, f32[4,4,4,128]{3,2,1,0:T(4,128)S(1)}, u32[]{:S(2)}, u32[]{:S(2)}) collective-permute-start(f32[4,4,4,128]{3,2,1,0:T(4,128)S(1)} %get-tuple-element.60), channel_id=1, source_target_pairs={{0,3},{1,2},{2,1},{3,0},{4,7},{5,6},{6,5},{7,4},{8,11},{9,10},{10,... | collective-permute-start | bytes 98312 | tf_op jit(solution)/shard_map/ppermute | solution.py:500
  14.0 0.6 %shard_map.105 = (f32[1,256]{1,0:T(1,128)S(1)}, bf16[128,512]{1,0:T(8,128)(2,1)S(1)}, f32[1,512]{1,0:T(1,128)S(1)}, f32[512,768]{1,0:T(8,128)S(1)}, bf16[32,512]...) custom-call(s32[1,256]{1,0:T(1,128)S(1)} %get-tuple-element.42.active_ref, f32[8,512]{1,0:T(8,128)S(1)} %get-tuple-element.43.state_ref, ...), custom_call_target="tpu_custom_call" | custom-call | tf_op jit(solution)/shard_map/pallas_call | solution.py:63
  14.6 2.5 %all-to-all-done.got_ref = f32[32,2,128]{2,1,0:T(2,128)S(1)} async-done(((f32[32,2,128]{2,1,0:T(2,128)}), f32[32,2,128]{2,1,0:T(2,128)S(1)}, u32[]{:S(2)}, u32[]{:S(2)}) %all-to-all-start) | async-done | bytes 32800 | tf_op jit(solution)/shard_map/all_to_all | solution.py:530
  17.1 2.2 %shard_map.106 = (f32[32,2,128]{2,1,0:T(2,128)}, f32[8,256]{1,0:T(8,128)S(1)}) custom-call(f32[32,2,128]{2,1,0:T(2,128)S(1)} %all-to-all-done.got_ref, s32[1,256]{1,0:T(1,128)S(1)} %get-tuple-element.42.active_ref, f32[1,256]{1,0:T(1,128)S(1)} %get-tuple-element.48.place_ref, f32[512,768]{1,0:T(8,128)S(1)} %get-tuple-element.49.stars_ref, ...), custom_call_target="tpu_custom_call" | custom-call | tf_op jit(solution)/shard_map/pallas_call | solution.py:63
  19.3 2.6 %all-to-all-start.1 = ((f32[32,2,128]{2,1,0:T(2,128)}), f32[32,2,128]{2,1,0:T(2,128)S(1)}, u32[]{:S(2)}, u32[]{:S(2)}) async-start(f32[32,2,128]{2,1,0:T(2,128)} %get-tuple-element.52), calls=%async_computation.1 | async-start | bytes 65536 | tf_op jit(solution)/shard_map/all_to_all | solution.py:566
  21.9 0.0 collective-permute-done.2
  21.9 0.0 collective-permute-done.3
  21.9 7.0 %conditional.1 = ((f32[3,4,8,64]{3,2,1,0:T(8,128)}, f32[3,4,8,64]{3,2,1,0:T(8,128)})) conditional(s32[]{:T(128)} %convert_element_type.3, () %tuple.15, (f32[4,4,8,128]{3,2,1,0:T(8,128)S(1)}, f32[4,4,4,128]{3,2,1,0:T(4,128)S(1)}, f32[4,4,4,128]{3,2,1,0:T(4,128)S(1)}, f32[8,256]{1,0:T(8,128)S(1)}) %tuple.16), branch_computations={%region_0.0_spmd, %region_1.0_spmd} | conditional | bytes 720984 | solution.py:592
  22.0 0.2 collective-permute-start
  22.1 2.6 %collective-permute-start.1 = (f32[22,8,128]{2,1,0:T(8,128)S(1)}, f32[22,8,128]{2,1,0:T(8,128)S(1)}, u32[]{:S(2)}, u32[]{:S(2)}) collective-permute-start(f32[22,8,128]{2,1,0:T(8,128)S(1)} %get-tuple-element.14), channel_id=1, source_target_pairs={{0,28},{4,8},{8,4},{12,16},{16,12},{20,24},{24,20},{28,0},{1,29},{... | collective-permute-start | bytes 270344 | tf_op jit(solution)/shard_map/cond/branch_1_fun/ppermute | solution.py:500
  24.7 2.9 %branch_1_fun.4.kick_ref = f32[3,5,16,128]{3,2,1,0:T(8,128)S(1)} custom-call(f32[8,256]{1,0:T(8,128)S(1)} %get-tuple-element.11.order_ref.target_ref), custom_call_target="tpu_custom_call" | custom-call | tf_op jit(solution)/shard_map/cond/branch_1_fun/pallas_call | solution.py:63
  27.6 0.0 collective-permute-done.near_ref
  27.6 0.0 collective-permute-done.1.far_ref
  27.6 1.3 %branch_1_fun.5 = (f32[3,4,8,64]{3,2,1,0:T(8,128)}, f32[3,4,8,64]{3,2,1,0:T(8,128)}) custom-call(f32[4,4,16,128]{3,2,1,0:T(8,128)S(1)} %get-tuple-element.12.own_ref, f32[22,8,128]{2,1,0:T(8,128)S(1)} %collective-permute-done.near_ref, f32[22,8,128]{2,1,0:T(8,128)S(1)} %collective-permute-done.1.far_ref, f32[3,5,16,128]{3,2,1,0:T(8,128)S(1)} %branch_1_fun.4.kick_ref), custom_call_target="tpu_custom_call" | custom-call | tf_op jit(solution)/shard_map/cond/branch_1_fun/pallas_call | solution.py:63
  28.9 0.3 all-to-all-done.1.back_ref
  29.2 0.8 %shard_map.108 = f32[12,512]{1,0:T(8,128)} custom-call(f32[32,2,128]{2,1,0:T(2,128)S(1)} %all-to-all-done.1.back_ref, f32[3,512]{1,0:T(4,128)S(1)} %get-tuple-element.53.pos_ref, f32[3,512]{1,0:T(4,128)S(1)} %get-tuple-element.54.vel_ref, f32[6,512]{1,0:T(8,128)S(1)} %get-tuple-element.55.acc_ref, bf16[128,512]{1,0:T(8,128)(2,1)S(1)} %get-tuple-element.56.slot_ref, ...), custom_call_target="tpu_custom_call" | custom-call | tf_op jit(solution)/shard_map/pallas_call | solution.py:63
  (2 shorter events, 0.0 us)
Async XLA Ops:
  2.4 14.7 %all-to-all-start = ((f32[32,2,128]{2,1,0:T(2,128)}), f32[32,2,128]{2,1,0:T(2,128)S(1)}, u32[]{:S(2)}, u32[]{:S(2)}) async-start(f32[32,2,128]{2,1,0:T(2,128)} %get-tuple-element.41.order_ref), calls=%async_computation | async-start | bytes 65536 | tf_op jit(solution)/shard_map/all_to_all | solution.py:530
  9.8 12.1 %collective-permute-start.2 = (f32[4,4,4,128]{3,2,1,0:T(4,128)S(1)}, f32[4,4,4,128]{3,2,1,0:T(4,128)S(1)}, u32[]{:S(2)}, u32[]{:S(2)}) collective-permute-start(f32[4,4,4,128]{3,2,1,0:T(4,128)S(1)} %get-tuple-element.59), channel_id=1, source_target_pairs={{0,1},{1,0},{2,3},{3,2},{4,5},{5,4},{6,7},{7,6},{8,9},{9,8},{10,11... | collective-permute-start | bytes 98312 | tf_op jit(solution)/shard_map/ppermute | solution.py:501
  11.7 10.2 %collective-permute-start.3 = (f32[4,4,4,128]{3,2,1,0:T(4,128)S(1)}, f32[4,4,4,128]{3,2,1,0:T(4,128)S(1)}, u32[]{:S(2)}, u32[]{:S(2)}) collective-permute-start(f32[4,4,4,128]{3,2,1,0:T(4,128)S(1)} %get-tuple-element.60), channel_id=1, source_target_pairs={{0,3},{1,2},{2,1},{3,0},{4,7},{5,6},{6,5},{7,4},{8,11},{9,10},{10,... | collective-permute-start | bytes 98312 | tf_op jit(solution)/shard_map/ppermute | solution.py:500
  19.3 9.9 %all-to-all-start.1 = ((f32[32,2,128]{2,1,0:T(2,128)}), f32[32,2,128]{2,1,0:T(2,128)S(1)}, u32[]{:S(2)}, u32[]{:S(2)}) async-start(f32[32,2,128]{2,1,0:T(2,128)} %get-tuple-element.52), calls=%async_computation.1 | async-start | bytes 65536 | tf_op jit(solution)/shard_map/all_to_all | solution.py:566
  22.0 5.7 %collective-permute-start = (f32[22,8,128]{2,1,0:T(8,128)S(1)}, f32[22,8,128]{2,1,0:T(8,128)S(1)}, u32[]{:S(2)}, u32[]{:S(2)}) collective-permute-start(f32[22,8,128]{2,1,0:T(8,128)S(1)} %get-tuple-element.13), channel_id=1, source_target_pairs={{0,4},{4,0},{8,12},{12,8},{16,20},{20,16},{24,28},{28,24},{1,5},{5... | collective-permute-start | bytes 270344 | tf_op jit(solution)/shard_map/cond/branch_1_fun/ppermute | solution.py:501
  22.1 5.5 %collective-permute-start.1 = (f32[22,8,128]{2,1,0:T(8,128)S(1)}, f32[22,8,128]{2,1,0:T(8,128)S(1)}, u32[]{:S(2)}, u32[]{:S(2)}) collective-permute-start(f32[22,8,128]{2,1,0:T(8,128)S(1)} %get-tuple-element.14), channel_id=1, source_target_pairs={{0,28},{4,8},{8,4},{12,16},{16,12},{20,24},{24,20},{28,0},{1,29},{... | collective-permute-start | bytes 270344 | tf_op jit(solution)/shard_map/cond/branch_1_fun/ppermute | solution.py:500

commit v5 on v4

--- a/solution.py
+++ b/solution.py
@@ -49,6 +49,20 @@
 
 def my_rank():
     return lax.axis_index("star") * lax.axis_size("gas") + lax.axis_index("gas")
+
+
+def rank_at(place):
+    star_count, gas_count = lax.axis_size("star"), lax.axis_size("gas")
+    pair, rest = place // (2 * star_count), place % (2 * star_count)
+    side, along = rest % 2, rest // 2
+    star = along + side * (star_count - 1 - 2 * along)
+    gas = pair + side * (gas_count - 1 - 2 * pair)
+    return star * gas_count + gas
+
+
+def exchange(pieces):
+    order = [rank_at(k) for k in range(pieces.shape[0])]
+    return lax.all_to_all(pieces, both, 0, 0, axis_index_groups=[order], tiled=True)
 
 
 def call(kernel, outs, *args, grid=None, in_specs=None, out_specs=None, scratch=(), after=0, where=pl.ANY, cost=None):
@@ -229,7 +243,7 @@
     width = active_ref.shape[1]
     devices = got_ref.shape[0]
     slots = lanes // 4
-    starts = iota((devices, width), 0) * total
+    starts = rank_at(iota((devices, width), 0)) * total
     active = active_ref[...]
     owned = one_hot((active >= starts) & (active < starts + total)).astype(bf16)
     owned3 = jnp.concatenate([owned, owned, owned], 0)
@@ -527,7 +541,7 @@
         scratch=[pltpu.SemaphoreType.DMA((len(inputs),))],
     )
     pos, vel, acc, _, names, field, flow, dense = held
-    got = lax.all_to_all(send, both, 0, 0, tiled=True)
+    got = exchange(send)
 
     own, near, far, rows = call(
         pack_kernel,
@@ -563,7 +577,7 @@
             (all_of(devices, 2, lanes), part_of(8)),
         ),
     )
-    back = lax.all_to_all(back, both, 0, 0, tiled=True)
+    back = exchange(back)
 
     if ext_x != reach or ext_y != 2 * reach or ext_z != lanes // 2:
         raise ValueError("brick shape")

time: 30.3 us -> 29.8 us (0.983)
  waiting for transfers between devices: 2.79 us -> 2.33 us
    all_to_all x2, waiting for transfers between devices: 2.78 us -> 2.32 us  [exchange(): lax.all_to_all(pieces, both, 0, 0, axis_index_groups=[order], tiled=True)]
where the time goes in v5:
time: 29.8 us; the launch traced here: 29.5 us
  starting transfers between devices  16.8 us (56%)
  Pallas kernels  9.65 us (32%)
  waiting for transfers between devices  2.33 us (8%)
  between operations  0.69 us (2%)
    all_to_all x2, starting transfers between devices, exchange(): lax.all_to_all(pieces, both, 0, 0, axis_index_groups=[order], tiled=True)  9.87 us
    pallas_call x9, Pallas kernels, call(): pl.pallas_call(kernel, out_shape=outs, scratch_shapes=list(scratch), cost...  9.65 us
    ppermute x2, starting transfers between devices, swap_pairs(): got_far = lax.ppermute(far, axis, between)  4.94 us
    all_to_all x2, waiting for transfers between devices, exchange(): lax.all_to_all(pieces, both, 0, 0, axis_index_groups=[order], tiled=True)  2.32 us
    ppermute x2, starting transfers between devices, swap_pairs(): got_near = lax.ppermute(near, axis, inside)  2.01 us
  transfers between devices with their start and end apart: 6, of which 2 were waited for; matrix products, arithmetic and copies ran while one was open for 0% of the time, Pallas kernels for 24%

profile of v5, /device:TPU:0, one launch (start us, length us, event | category | flops | bytes accessed | tf_op | source)
XLA Modules:
  0.0 29.5 jit_solution(7540812384732719552)
XLA Ops:
  0.6 1.8 %shard_map.103 = (f32[3,512]{1,0:T(4,128)S(1)}, f32[3,512]{1,0:T(4,128)S(1)}, f32[6,512]{1,0:T(8,128)S(1)}, f32[1,512]{1,0:T(1,128)}, s32[1,256]{1,0:T(1,128)S(1...) custom-call(f32[3,512]{1,0:T(4,128)} %refs_0_.1, ...), custom_call_target="tpu_custom_call" | custom-call | tf_op jit(solution)/shard_map/pallas_call | solution.py:77
  2.4 7.3 %all-to-all-start = ((f32[32,2,128]{2,1,0:T(2,128)}), f32[32,2,128]{2,1,0:T(2,128)S(1)}, u32[]{:S(2)}, u32[]{:S(2)}) async-start(f32[32,2,128]{2,1,0:T(2,128)} %get-tuple-element.41.order_ref), calls=%async_computation | async-start | bytes 65536 | tf_op jit(solution)/shard_map/all_to_all | solution.py:65
  9.7 0.1 shard_map.104
  9.8 1.8 %collective-permute-start.2 = (f32[4,4,4,128]{3,2,1,0:T(4,128)S(1)}, f32[4,4,4,128]{3,2,1,0:T(4,128)S(1)}, u32[]{:S(2)}, u32[]{:S(2)}) collective-permute-start(f32[4,4,4,128]{3,2,1,0:T(4,128)S(1)} %get-tuple-element.59), channel_id=1, source_target_pairs={{0,1},{1,0},{2,3},{3,2},{4,5},{5,4},{6,7},{7,6},{8,9},{9,8},{10,11... | collective-permute-start | bytes 98312 | tf_op jit(solution)/shard_map/ppermute | solution.py:515
  11.7 2.4 %collective-permute-start.3 = (f32[4,4,4,128]{3,2,1,0:T(4,128)S(1)}, f32[4,4,4,128]{3,2,1,0:T(4,128)S(1)}, u32[]{:S(2)}, u32[]{:S(2)}) collective-permute-start(f32[4,4,4,128]{3,2,1,0:T(4,128)S(1)} %get-tuple-element.60), channel_id=1, source_target_pairs={{0,3},{1,2},{2,1},{3,0},{4,7},{5,6},{6,5},{7,4},{8,11},{9,10},{10,... | collective-permute-start | bytes 98312 | tf_op jit(solution)/shard_map/ppermute | solution.py:514
  14.0 0.6 %shard_map.105 = (f32[1,256]{1,0:T(1,128)S(1)}, bf16[128,512]{1,0:T(8,128)(2,1)S(1)}, f32[1,512]{1,0:T(1,128)S(1)}, f32[512,768]{1,0:T(8,128)S(1)}, bf16[32,512]...) custom-call(s32[1,256]{1,0:T(1,128)S(1)} %get-tuple-element.42.active_ref, f32[8,512]{1,0:T(8,128)S(1)} %get-tuple-element.43.state_ref, ...), custom_call_target="tpu_custom_call" | custom-call | tf_op jit(solution)/shard_map/pallas_call | solution.py:77
  14.6 2.2 %all-to-all-done.got_ref = f32[32,2,128]{2,1,0:T(2,128)S(1)} async-done(((f32[32,2,128]{2,1,0:T(2,128)}), f32[32,2,128]{2,1,0:T(2,128)S(1)}, u32[]{:S(2)}, u32[]{:S(2)}) %all-to-all-start) | async-done | bytes 32800 | tf_op jit(solution)/shard_map/all_to_all | solution.py:65
  16.9 2.2 %shard_map.106 = (f32[32,2,128]{2,1,0:T(2,128)}, f32[8,256]{1,0:T(8,128)S(1)}) custom-call(f32[32,2,128]{2,1,0:T(2,128)S(1)} %all-to-all-done.got_ref, s32[1,256]{1,0:T(1,128)S(1)} %get-tuple-element.42.active_ref, f32[1,256]{1,0:T(1,128)S(1)} %get-tuple-element.48.place_ref, f32[512,768]{1,0:T(8,128)S(1)} %get-tuple-element.49.stars_ref, ...), custom_call_target="tpu_custom_call" | custom-call | tf_op jit(solution)/shard_map/pallas_call | solution.py:77
  19.0 2.6 %all-to-all-start.1 = ((f32[32,2,128]{2,1,0:T(2,128)}), f32[32,2,128]{2,1,0:T(2,128)S(1)}, u32[]{:S(2)}, u32[]{:S(2)}) async-start(f32[32,2,128]{2,1,0:T(2,128)} %get-tuple-element.52), calls=%async_computation.1 | async-start | bytes 65536 | tf_op jit(solution)/shard_map/all_to_all | solution.py:65
  21.6 0.0 collective-permute-done.2
  21.6 0.0 collective-permute-done.3
  21.6 7.0 %conditional.1 = ((f32[3,4,8,64]{3,2,1,0:T(8,128)}, f32[3,4,8,64]{3,2,1,0:T(8,128)})) conditional(s32[]{:T(128)} %convert_element_type.3, () %tuple.15, (f32[4,4,8,128]{3,2,1,0:T(8,128)S(1)}, f32[4,4,4,128]{3,2,1,0:T(4,128)S(1)}, f32[4,4,4,128]{3,2,1,0:T(4,128)S(1)}, f32[8,256]{1,0:T(8,128)S(1)}) %tuple.16), branch_computations={%region_0.0_spmd, %region_1.0_spmd} | conditional | bytes 720984 | solution.py:606
  21.7 0.2 collective-permute-start
  21.9 2.6 %collective-permute-start.1 = (f32[22,8,128]{2,1,0:T(8,128)S(1)}, f32[22,8,128]{2,1,0:T(8,128)S(1)}, u32[]{:S(2)}, u32[]{:S(2)}) collective-permute-start(f32[22,8,128]{2,1,0:T(8,128)S(1)} %get-tuple-element.14), channel_id=1, source_target_pairs={{0,28},{4,8},{8,4},{12,16},{16,12},{20,24},{24,20},{28,0},{1,29},{... | collective-permute-start | bytes 270344 | tf_op jit(solution)/shard_map/cond/branch_1_fun/ppermute | solution.py:514
  24.4 2.9 %branch_1_fun.4.kick_ref = f32[3,5,16,128]{3,2,1,0:T(8,128)S(1)} custom-call(f32[8,256]{1,0:T(8,128)S(1)} %get-tuple-element.11.order_ref.target_ref), custom_call_target="tpu_custom_call" | custom-call | tf_op jit(solution)/shard_map/cond/branch_1_fun/pallas_call | solution.py:77
  27.3 0.0 collective-permute-done.near_ref
  27.4 0.0 collective-permute-done.1.far_ref
  27.4 1.3 %branch_1_fun.5 = (f32[3,4,8,64]{3,2,1,0:T(8,128)}, f32[3,4,8,64]{3,2,1,0:T(8,128)}) custom-call(f32[4,4,16,128]{3,2,1,0:T(8,128)S(1)} %get-tuple-element.12.own_ref, f32[22,8,128]{2,1,0:T(8,128)S(1)} %collective-permute-done.near_ref, f32[22,8,128]{2,1,0:T(8,128)S(1)} %collective-permute-done.1.far_ref, f32[3,5,16,128]{3,2,1,0:T(8,128)S(1)} %branch_1_fun.4.kick_ref), custom_call_target="tpu_custom_call" | custom-call | tf_op jit(solution)/shard_map/cond/branch_1_fun/pallas_call | solution.py:77
  28.6 0.1 all-to-all-done.1.back_ref
  28.7 0.8 %shard_map.108 = f32[12,512]{1,0:T(8,128)} custom-call(f32[32,2,128]{2,1,0:T(2,128)S(1)} %all-to-all-done.1.back_ref, f32[3,512]{1,0:T(4,128)S(1)} %get-tuple-element.53.pos_ref, f32[3,512]{1,0:T(4,128)S(1)} %get-tuple-element.54.vel_ref, f32[6,512]{1,0:T(8,128)S(1)} %get-tuple-element.55.acc_ref, bf16[128,512]{1,0:T(8,128)(2,1)S(1)} %get-tuple-element.56.slot_ref, ...), custom_call_target="tpu_custom_call" | custom-call | tf_op jit(solution)/shard_map/pallas_call | solution.py:77
  (2 shorter events, 0.0 us)
Async XLA Ops:
  2.4 14.4 %all-to-all-start = ((f32[32,2,128]{2,1,0:T(2,128)}), f32[32,2,128]{2,1,0:T(2,128)S(1)}, u32[]{:S(2)}, u32[]{:S(2)}) async-start(f32[32,2,128]{2,1,0:T(2,128)} %get-tuple-element.41.order_ref), calls=%async_computation | async-start | bytes 65536 | tf_op jit(solution)/shard_map/all_to_all | solution.py:65
  9.8 11.8 %collective-permute-start.2 = (f32[4,4,4,128]{3,2,1,0:T(4,128)S(1)}, f32[4,4,4,128]{3,2,1,0:T(4,128)S(1)}, u32[]{:S(2)}, u32[]{:S(2)}) collective-permute-start(f32[4,4,4,128]{3,2,1,0:T(4,128)S(1)} %get-tuple-element.59), channel_id=1, source_target_pairs={{0,1},{1,0},{2,3},{3,2},{4,5},{5,4},{6,7},{7,6},{8,9},{9,8},{10,11... | collective-permute-start | bytes 98312 | tf_op jit(solution)/shard_map/ppermute | solution.py:515
  11.7 10.0 %collective-permute-start.3 = (f32[4,4,4,128]{3,2,1,0:T(4,128)S(1)}, f32[4,4,4,128]{3,2,1,0:T(4,128)S(1)}, u32[]{:S(2)}, u32[]{:S(2)}) collective-permute-start(f32[4,4,4,128]{3,2,1,0:T(4,128)S(1)} %get-tuple-element.60), channel_id=1, source_target_pairs={{0,3},{1,2},{2,1},{3,0},{4,7},{5,6},{6,5},{7,4},{8,11},{9,10},{10,... | collective-permute-start | bytes 98312 | tf_op jit(solution)/shard_map/ppermute | solution.py:514
  19.0 9.7 %all-to-all-start.1 = ((f32[32,2,128]{2,1,0:T(2,128)}), f32[32,2,128]{2,1,0:T(2,128)S(1)}, u32[]{:S(2)}, u32[]{:S(2)}) async-start(f32[32,2,128]{2,1,0:T(2,128)} %get-tuple-element.52), calls=%async_computation.1 | async-start | bytes 65536 | tf_op jit(solution)/shard_map/all_to_all | solution.py:65
  21.7 5.7 %collective-permute-start = (f32[22,8,128]{2,1,0:T(8,128)S(1)}, f32[22,8,128]{2,1,0:T(8,128)S(1)}, u32[]{:S(2)}, u32[]{:S(2)}) collective-permute-start(f32[22,8,128]{2,1,0:T(8,128)S(1)} %get-tuple-element.13), channel_id=1, source_target_pairs={{0,4},{4,0},{8,12},{12,8},{16,20},{20,16},{24,28},{28,24},{1,5},{5... | collective-permute-start | bytes 270344 | tf_op jit(solution)/shard_map/cond/branch_1_fun/ppermute | solution.py:515
  21.9 5.5 %collective-permute-start.1 = (f32[22,8,128]{2,1,0:T(8,128)S(1)}, f32[22,8,128]{2,1,0:T(8,128)S(1)}, u32[]{:S(2)}, u32[]{:S(2)}) collective-permute-start(f32[22,8,128]{2,1,0:T(8,128)S(1)} %get-tuple-element.14), channel_id=1, source_target_pairs={{0,28},{4,8},{8,4},{12,16},{16,12},{20,24},{24,20},{28,0},{1,29},{... | collective-permute-start | bytes 270344 | tf_op jit(solution)/shard_map/cond/branch_1_fun/ppermute | solution.py:514

commit v6 on v5

--- a/solution.py
+++ b/solution.py
@@ -16,7 +16,7 @@
 rim = reach - 1
 lanes = 128
 vmem_bytes = 48 * 1024 * 1024
-batch = 4
+batch = 2
 depth = 512
 f32, bf16, i32 = jnp.float32, jnp.bfloat16, jnp.int32
 
@@ -139,9 +139,9 @@
         far_ref[k] = jnp.where(even, low, high)
     half = density_ref.shape[1] // 2
     for k in range(density_ref.shape[0]):
-        first = density_ref[k, pl.ds(0, half, stride=2), :]
-        second = density_ref[k, pl.ds(1, half, stride=2), :]
-        rows_ref[k * half : (k + 1) * half] = jnp.concatenate([first, second], -1)
+        rows_ref[k * half : (k + 1) * half] = jnp.concatenate(
+            [density_ref[k, 0:half, :], density_ref[k, half:, :]], -1
+        )
 
 
 def join_kernel(own_ref, near_ref, far_ref, order_ref, brick_ref, side_ref, other_ref):
@@ -286,7 +286,7 @@
         sums = [jnp.zeros((8, lanes), f32) for _ in range(3)]
         for pair in range(ext_y // 2):
             for at in range(0, 2 * ext_z, step):
-                gap_y = (first_y + 2 * pair + at // ext_z).astype(f32) + 0.5 - py
+                gap_y = (first_y + pair + at // ext_z * (ext_y // 2)).astype(f32) + 0.5 - py
                 gap_z = (iota((step, lanes), 0) + at % ext_z).astype(f32) + 0.5 - pz
                 base = gap_z * gap_z + wide(gap_y * gap_y + soften)
                 along = None
@@ -341,7 +341,8 @@
     mass = targets[3:4]
     row = iota((8, width), 0)
     moment = jnp.where(row < 3, targets * mass, jnp.where(row == 3, mass, 0.0))
-    left = stack4(moment)
+    pieces = split3(moment)
+    left = jnp.concatenate([v[0:4] for v in pieces] + [jnp.zeros((4, width), bf16)], 0)
     ask = one_hot(iota((24, 3 * lanes), 0) % 8 == iota((24, 3 * lanes), 1) // lanes).astype(bf16)
     spread = dot_of(stack3(targets), ask, 0, 0)
     tx, ty, tz = spread[:, 0:lanes], spread[:, lanes : 2 * lanes], spread[:, 2 * lanes :]
@@ -375,7 +376,9 @@
                 base_y[j] = base + gap_y * gap_y
             inv = lax.rsqrt(base_y[j] + square_x[pair])
             weights.append(inv * (inv * inv))
-        sums = fold3(weigh(left, jnp.concatenate(weights, 1)))
+        sums = weigh(left, jnp.concatenate(weights, 1))
+        sums = sums[0:8] + sums[8:16]
+        sums = sums + pltpu.roll(sums, 4, 0)
         for at, (j, pair) in enumerate(part):
             here = sums[:, at * lanes : (at + 1) * lanes]
             whole = here[3:4]

time: 29.8 us -> 29.8 us (level)
  waiting for transfers between devices: 2.33 us -> 2.63 us
  transfers between devices with their start and end apart: 6 -> 6, of which waited for: 2 -> 3; matrix products, arithmetic and copies ran while one was open for 0% -> 0% of each run, Pallas kernels for 24% -> 23%
where the time goes in v6:
time: 29.8 us; the launch traced here: 29.5 us
  starting transfers between devices  16.8 us (56%)
  Pallas kernels  9.36 us (31%)
  waiting for transfers between devices  2.63 us (9%)
  between operations  0.69 us (2%)
    all_to_all x2, starting transfers between devices, exchange(): lax.all_to_all(pieces, both, 0, 0, axis_index_groups=[order], tiled=True)  9.87 us
    pallas_call x9, Pallas kernels, call(): pl.pallas_call(kernel, out_shape=outs, scratch_shapes=list(scratch), cost...  9.36 us
    ppermute x2, starting transfers between devices, swap_pairs(): got_far = lax.ppermute(far, axis, between)  4.94 us
    all_to_all x2, waiting for transfers between devices, exchange(): lax.all_to_all(pieces, both, 0, 0, axis_index_groups=[order], tiled=True)  2.52 us
    ppermute x2, starting transfers between devices, swap_pairs(): got_near = lax.ppermute(near, axis, inside)  2.01 us
  transfers between devices with their start and end apart: 6, of which 3 were waited for; matrix products, arithmetic and copies ran while one was open for 0% of the time, Pallas kernels for 23%

profile of v6, /device:TPU:0, one launch (start us, length us, event | category | flops | bytes accessed | tf_op | source)
XLA Modules:
  0.0 29.5 jit_solution(15081342304033722966)
XLA Ops:
  0.6 1.8 %shard_map.103 = (f32[3,512]{1,0:T(4,128)S(1)}, f32[3,512]{1,0:T(4,128)S(1)}, f32[6,512]{1,0:T(8,128)S(1)}, f32[1,512]{1,0:T(1,128)}, s32[1,256]{1,0:T(1,128)S(1...) custom-call(f32[3,512]{1,0:T(4,128)} %refs_0_.1, ...), custom_call_target="tpu_custom_call" | custom-call | tf_op jit(solution)/shard_map/pallas_call | solution.py:77
  2.4 7.3 %all-to-all-start = ((f32[32,2,128]{2,1,0:T(2,128)}), f32[32,2,128]{2,1,0:T(2,128)S(1)}, u32[]{:S(2)}, u32[]{:S(2)}) async-start(f32[32,2,128]{2,1,0:T(2,128)} %get-tuple-element.41.order_ref), calls=%async_computation | async-start | bytes 65536 | tf_op jit(solution)/shard_map/all_to_all | solution.py:65
  9.7 0.1 shard_map.104
  9.8 1.8 %collective-permute-start.2 = (f32[4,4,4,128]{3,2,1,0:T(4,128)S(1)}, f32[4,4,4,128]{3,2,1,0:T(4,128)S(1)}, u32[]{:S(2)}, u32[]{:S(2)}) collective-permute-start(f32[4,4,4,128]{3,2,1,0:T(4,128)S(1)} %get-tuple-element.59), channel_id=1, source_target_pairs={{0,1},{1,0},{2,3},{3,2},{4,5},{5,4},{6,7},{7,6},{8,9},{9,8},{10,11... | collective-permute-start | bytes 98312 | tf_op jit(solution)/shard_map/ppermute | solution.py:518
  11.7 2.4 %collective-permute-start.3 = (f32[4,4,4,128]{3,2,1,0:T(4,128)S(1)}, f32[4,4,4,128]{3,2,1,0:T(4,128)S(1)}, u32[]{:S(2)}, u32[]{:S(2)}) collective-permute-start(f32[4,4,4,128]{3,2,1,0:T(4,128)S(1)} %get-tuple-element.60), channel_id=1, source_target_pairs={{0,3},{1,2},{2,1},{3,0},{4,7},{5,6},{6,5},{7,4},{8,11},{9,10},{10,... | collective-permute-start | bytes 98312 | tf_op jit(solution)/shard_map/ppermute | solution.py:517
  14.0 0.6 %shard_map.105 = (f32[1,256]{1,0:T(1,128)S(1)}, bf16[128,512]{1,0:T(8,128)(2,1)S(1)}, f32[1,512]{1,0:T(1,128)S(1)}, f32[512,768]{1,0:T(8,128)S(1)}, bf16[32,512]...) custom-call(s32[1,256]{1,0:T(1,128)S(1)} %get-tuple-element.42.active_ref, f32[8,512]{1,0:T(8,128)S(1)} %get-tuple-element.43.state_ref, ...), custom_call_target="tpu_custom_call" | custom-call | tf_op jit(solution)/shard_map/pallas_call | solution.py:77
  14.6 2.2 %all-to-all-done.got_ref = f32[32,2,128]{2,1,0:T(2,128)S(1)} async-done(((f32[32,2,128]{2,1,0:T(2,128)}), f32[32,2,128]{2,1,0:T(2,128)S(1)}, u32[]{:S(2)}, u32[]{:S(2)}) %all-to-all-start) | async-done | bytes 32800 | tf_op jit(solution)/shard_map/all_to_all | solution.py:65
  16.9 2.2 %shard_map.106 = (f32[32,2,128]{2,1,0:T(2,128)}, f32[8,256]{1,0:T(8,128)S(1)}) custom-call(f32[32,2,128]{2,1,0:T(2,128)S(1)} %all-to-all-done.got_ref, s32[1,256]{1,0:T(1,128)S(1)} %get-tuple-element.42.active_ref, f32[1,256]{1,0:T(1,128)S(1)} %get-tuple-element.48.place_ref, f32[512,768]{1,0:T(8,128)S(1)} %get-tuple-element.49.stars_ref, ...), custom_call_target="tpu_custom_call" | custom-call | tf_op jit(solution)/shard_map/pallas_call | solution.py:77
  19.0 2.6 %all-to-all-start.1 = ((f32[32,2,128]{2,1,0:T(2,128)}), f32[32,2,128]{2,1,0:T(2,128)S(1)}, u32[]{:S(2)}, u32[]{:S(2)}) async-start(f32[32,2,128]{2,1,0:T(2,128)} %get-tuple-element.52), calls=%async_computation.1 | async-start | bytes 65536 | tf_op jit(solution)/shard_map/all_to_all | solution.py:65
  21.6 0.0 collective-permute-done.2
  21.6 0.0 collective-permute-done.3
  21.6 6.8 %conditional.1 = ((f32[3,4,8,64]{3,2,1,0:T(8,128)}, f32[3,4,8,64]{3,2,1,0:T(8,128)})) conditional(s32[]{:T(128)} %convert_element_type.3, () %tuple.15, (f32[4,4,8,128]{3,2,1,0:T(8,128)S(1)}, f32[4,4,4,128]{3,2,1,0:T(4,128)S(1)}, f32[4,4,4,128]{3,2,1,0:T(4,128)S(1)}, f32[8,256]{1,0:T(8,128)S(1)}) %tuple.16), branch_computations={%region_0.0_spmd, %region_1.0_spmd} | conditional | bytes 720984 | solution.py:609
  21.7 0.2 collective-permute-start
  21.9 2.6 %collective-permute-start.1 = (f32[22,8,128]{2,1,0:T(8,128)S(1)}, f32[22,8,128]{2,1,0:T(8,128)S(1)}, u32[]{:S(2)}, u32[]{:S(2)}) collective-permute-start(f32[22,8,128]{2,1,0:T(8,128)S(1)} %get-tuple-element.14), channel_id=1, source_target_pairs={{0,28},{4,8},{8,4},{12,16},{16,12},{20,24},{24,20},{28,0},{1,29},{... | collective-permute-start | bytes 270344 | tf_op jit(solution)/shard_map/cond/branch_1_fun/ppermute | solution.py:517
  24.4 2.6 %branch_1_fun.4.kick_ref = f32[3,5,16,128]{3,2,1,0:T(8,128)S(1)} custom-call(f32[8,256]{1,0:T(8,128)S(1)} %get-tuple-element.11.order_ref.target_ref), custom_call_target="tpu_custom_call" | custom-call | tf_op jit(solution)/shard_map/cond/branch_1_fun/pallas_call | solution.py:77
  27.1 0.0 collective-permute-done.near_ref
  27.1 0.1 collective-permute-done.1.far_ref
  27.2 1.2 %branch_1_fun.5 = (f32[3,4,8,64]{3,2,1,0:T(8,128)}, f32[3,4,8,64]{3,2,1,0:T(8,128)}) custom-call(f32[4,4,16,128]{3,2,1,0:T(8,128)S(1)} %get-tuple-element.12.own_ref, f32[22,8,128]{2,1,0:T(8,128)S(1)} %collective-permute-done.near_ref, f32[22,8,128]{2,1,0:T(8,128)S(1)} %collective-permute-done.1.far_ref, f32[3,5,16,128]{3,2,1,0:T(8,128)S(1)} %branch_1_fun.4.kick_ref), custom_call_target="tpu_custom_call" | custom-call | tf_op jit(solution)/shard_map/cond/branch_1_fun/pallas_call | solution.py:77
  28.4 0.3 %all-to-all-done.1.back_ref = f32[32,2,128]{2,1,0:T(2,128)S(1)} async-done(((f32[32,2,128]{2,1,0:T(2,128)}), f32[32,2,128]{2,1,0:T(2,128)S(1)}, u32[]{:S(2)}, u32[]{:S(2)}) %all-to-all-start.1) | async-done | bytes 32800 | tf_op jit(solution)/shard_map/all_to_all | solution.py:65
  28.7 0.8 %shard_map.108 = f32[12,512]{1,0:T(8,128)} custom-call(f32[32,2,128]{2,1,0:T(2,128)S(1)} %all-to-all-done.1.back_ref, f32[3,512]{1,0:T(4,128)S(1)} %get-tuple-element.53.pos_ref, f32[3,512]{1,0:T(4,128)S(1)} %get-tuple-element.54.vel_ref, f32[6,512]{1,0:T(8,128)S(1)} %get-tuple-element.55.acc_ref, bf16[128,512]{1,0:T(8,128)(2,1)S(1)} %get-tuple-element.56.slot_ref, ...), custom_call_target="tpu_custom_call" | custom-call | tf_op jit(solution)/shard_map/pallas_call | solution.py:77
  (2 shorter events, 0.0 us)
Async XLA Ops:
  2.4 14.4 %all-to-all-start = ((f32[32,2,128]{2,1,0:T(2,128)}), f32[32,2,128]{2,1,0:T(2,128)S(1)}, u32[]{:S(2)}, u32[]{:S(2)}) async-start(f32[32,2,128]{2,1,0:T(2,128)} %get-tuple-element.41.order_ref), calls=%async_computation | async-start | bytes 65536 | tf_op jit(solution)/shard_map/all_to_all | solution.py:65
  9.8 11.8 %collective-permute-start.2 = (f32[4,4,4,128]{3,2,1,0:T(4,128)S(1)}, f32[4,4,4,128]{3,2,1,0:T(4,128)S(1)}, u32[]{:S(2)}, u32[]{:S(2)}) collective-permute-start(f32[4,4,4,128]{3,2,1,0:T(4,128)S(1)} %get-tuple-element.59), channel_id=1, source_target_pairs={{0,1},{1,0},{2,3},{3,2},{4,5},{5,4},{6,7},{7,6},{8,9},{9,8},{10,11... | collective-permute-start | bytes 98312 | tf_op jit(solution)/shard_map/ppermute | solution.py:518
  11.7 10.0 %collective-permute-start.3 = (f32[4,4,4,128]{3,2,1,0:T(4,128)S(1)}, f32[4,4,4,128]{3,2,1,0:T(4,128)S(1)}, u32[]{:S(2)}, u32[]{:S(2)}) collective-permute-start(f32[4,4,4,128]{3,2,1,0:T(4,128)S(1)} %get-tuple-element.60), channel_id=1, source_target_pairs={{0,3},{1,2},{2,1},{3,0},{4,7},{5,6},{6,5},{7,4},{8,11},{9,10},{10,... | collective-permute-start | bytes 98312 | tf_op jit(solution)/shard_map/ppermute | solution.py:517
  19.0 9.7 %all-to-all-start.1 = ((f32[32,2,128]{2,1,0:T(2,128)}), f32[32,2,128]{2,1,0:T(2,128)S(1)}, u32[]{:S(2)}, u32[]{:S(2)}) async-start(f32[32,2,128]{2,1,0:T(2,128)} %get-tuple-element.52), calls=%async_computation.1 | async-start | bytes 65536 | tf_op jit(solution)/shard_map/all_to_all | solution.py:65
  21.7 5.4 %collective-permute-start = (f32[22,8,128]{2,1,0:T(8,128)S(1)}, f32[22,8,128]{2,1,0:T(8,128)S(1)}, u32[]{:S(2)}, u32[]{:S(2)}) collective-permute-start(f32[22,8,128]{2,1,0:T(8,128)S(1)} %get-tuple-element.13), channel_id=1, source_target_pairs={{0,4},{4,0},{8,12},{12,8},{16,20},{20,16},{24,28},{28,24},{1,5},{5... | collective-permute-start | bytes 270344 | tf_op jit(solution)/shard_map/cond/branch_1_fun/ppermute | solution.py:518
  21.9 5.3 %collective-permute-start.1 = (f32[22,8,128]{2,1,0:T(8,128)S(1)}, f32[22,8,128]{2,1,0:T(8,128)S(1)}, u32[]{:S(2)}, u32[]{:S(2)}) collective-permute-start(f32[22,8,128]{2,1,0:T(8,128)S(1)} %get-tuple-element.14), channel_id=1, source_target_pairs={{0,28},{4,8},{8,4},{12,16},{16,12},{20,24},{24,20},{28,0},{1,29},{... | collective-permute-start | bytes 270344 | tf_op jit(solution)/shard_map/cond/branch_1_fun/ppermute | solution.py:517

commit v7 on v6

--- a/solution.py
+++ b/solution.py
@@ -108,17 +108,14 @@
     state = jnp.concatenate([pred_pos, mass_ref[...], pred_vel, jnp.zeros((1, total), f32)], 0)
     state_ref[...] = state
     local = active_ref[...] - my_rank() * total
-    first = jnp.sum(one_hot(local < 0)).astype(i32)
     hit = one_hot(iota((total, listed), 0) == local).astype(bf16)
     pieces = dot_of(stack3(state), hit)
     placed = pieces[0:8] + pieces[8:16] + pieces[16:24]
-    placed = pltpu.roll(placed, lax.rem(listed - first, listed), 1)[:, 0:lanes]
+    spread = sum(placed[:, k : k + lanes] for k in range(0, listed, lanes))
+    for shift in (2 * slots, slots):
+        spread = spread + pltpu.roll(spread, shift, 1)
     lane = iota((8, lanes), 1)
     row = iota((8, lanes), 0)
-    part = jnp.where(lane < slots, placed, 0.0)
-    spread = part
-    for k in range(1, 4):
-        spread = jnp.where(lane // slots == k, pltpu.roll(part, k * slots, 1), spread)
     spread = jnp.where(row % 4 == lane // slots, spread, 0.0)
     one = jnp.sum(spread[0:4], 0, keepdims=True)
     two = jnp.sum(spread[4:8], 0, keepdims=True)
@@ -183,22 +180,14 @@
     return tiles
 
 
-def index_kernel(active_ref, state_ref, density_ref, place_ref, slot_ref, listed_ref, stars_ref, star_left_ref, cells_ref):
+def index_kernel(active_ref, state_ref, density_ref, slot_ref, listed_ref, stars_ref, star_left_ref, cells_ref):
     listed = active_ref.shape[1]
     total = state_ref.shape[1]
-    devices = lax.axis_size("star") * lax.axis_size("gas")
     slots = lanes // 4
     active = active_ref[...]
-    starts = iota((devices, listed), 0) * total
-    before = one_hot(active < starts)
-    after = one_hot(active < starts + total)
-    owned = after - before
-    first = jnp.sum(before, 1, keepdims=True)
-    place = iota((1, listed), 1).astype(f32) - jnp.sum(owned * first, 0, keepdims=True)
-    place_ref[...] = place
     local = active - my_rank() * total
     mine = (local >= 0) & (local < total)
-    pick = one_hot((iota((lanes, listed), 0) % slots == place.astype(i32)) & mine).astype(bf16)
+    pick = one_hot((iota((lanes, listed), 0) % slots == iota((lanes, listed), 1) % slots) & mine).astype(bf16)
     hit = one_hot(iota((total, listed), 0) == local).astype(bf16)
     slot = dot_of(pick, hit, 1, 1)
     slot_ref[...] = slot.astype(bf16)
@@ -236,7 +225,7 @@
 
 
 def force_kernel(
-    ext, got_ref, active_ref, place_ref, stars_ref, star_left_ref, cells_ref, send_ref, target_ref, *, chunked
+    ext, got_ref, active_ref, stars_ref, star_left_ref, cells_ref, send_ref, target_ref, *, chunked
 ):
     ext_x, ext_y, ext_z = ext
     total = stars_ref.shape[0]
@@ -247,7 +236,7 @@
     active = active_ref[...]
     owned = one_hot((active >= starts) & (active < starts + total)).astype(bf16)
     owned3 = jnp.concatenate([owned, owned, owned], 0)
-    slot_hit = one_hot(iota((slots, width), 0) == place_ref[...].astype(i32))
+    slot_hit = one_hot(iota((slots, width), 0) == iota((slots, width), 1) % slots)
     spread = dot_of(stack3(jnp.concatenate([got_ref[:, 0, :], got_ref[:, 1, :]], 1)), owned3, 0, 0)
     targets = jnp.sum(spread.reshape(8, slots, width) * slot_hit[None], 1)
     target_ref[...] = targets
@@ -553,9 +542,9 @@
         field, flow, dense, send, after=1,
     )
     near, far = swap_pairs(near, far, "gas")
-    place, slot, is_listed, stars, star_left, cells = call(
+    slot, is_listed, stars, star_left, cells = call(
         index_kernel,
-        (shape(1, listed), shape(lanes, total, dtype=bf16), shape(1, total), shape(total, 6 * lanes),
+        (shape(lanes, total, dtype=bf16), shape(1, total), shape(total, 6 * lanes),
          shape(32, total, dtype=bf16), shape(2 * ext_z, ext_x * ext_y // 2 * lanes)),
         names, state, rows,
     )
@@ -573,9 +562,9 @@
     back, targets = call(
         functools.partial(force_kernel, ext, chunked=chunks > 1),
         (shape(devices, 2, lanes), shape(8, listed)),
-        got, names, place, stars, star_left, cells,
+        got, names, stars, star_left, cells,
         **in_parts(
-            [all_of(*got.shape), part_of(1), part_of(1)]
+            [all_of(*got.shape), part_of(1)]
             + [all_of(*x.shape) for x in (stars, star_left, cells)],
             (all_of(devices, 2, lanes), part_of(8)),
         ),

time: 29.8 us -> 29.8 us (level)
  no operation moved by 1% of the time
where the time goes in v7:
time: 29.8 us; the launch traced here: 29.5 us
  starting transfers between devices  16.8 us (56%)
  Pallas kernels  9.34 us (31%)
  waiting for transfers between devices  2.64 us (9%)
  between operations  0.69 us (2%)
    all_to_all x2, starting transfers between devices, exchange(): lax.all_to_all(pieces, both, 0, 0, axis_index_groups=[order], tiled=True)  9.87 us
    pallas_call x9, Pallas kernels, call(): pl.pallas_call(kernel, out_shape=outs, scratch_shapes=list(scratch), cost...  9.34 us
    ppermute x2, starting transfers between devices, swap_pairs(): got_far = lax.ppermute(far, axis, between)  4.94 us
    all_to_all x2, waiting for transfers between devices, exchange(): lax.all_to_all(pieces, both, 0, 0, axis_index_groups=[order], tiled=True)  2.53 us
    ppermute x2, starting transfers between devices, swap_pairs(): got_near = lax.ppermute(near, axis, inside)  2.01 us
  transfers between devices with their start and end apart: 6, of which 3 were waited for; matrix products, arithmetic and copies ran while one was open for 0% of the time, Pallas kernels for 23%

profile of v7, /device:TPU:0, one launch (start us, length us, event | category | flops | bytes accessed | tf_op | source)
XLA Modules:
  0.0 29.5 jit_solution(12842947693175703263)
XLA Ops:
  0.6 1.8 %shard_map.103 = (f32[3,512]{1,0:T(4,128)S(1)}, f32[3,512]{1,0:T(4,128)S(1)}, f32[6,512]{1,0:T(8,128)S(1)}, f32[1,512]{1,0:T(1,128)}, s32[1,256]{1,0:T(1,128)S(1...) custom-call(f32[3,512]{1,0:T(4,128)} %refs_0_.1, ...), custom_call_target="tpu_custom_call" | custom-call | tf_op jit(solution)/shard_map/pallas_call | solution.py:77
  2.4 7.3 %all-to-all-start = ((f32[32,2,128]{2,1,0:T(2,128)}), f32[32,2,128]{2,1,0:T(2,128)S(1)}, u32[]{:S(2)}, u32[]{:S(2)}) async-start(f32[32,2,128]{2,1,0:T(2,128)} %get-tuple-element.40.order_ref), calls=%async_computation | async-start | bytes 65536 | tf_op jit(solution)/shard_map/all_to_all | solution.py:65
  9.7 0.1 shard_map.104
  9.8 1.8 %collective-permute-start.2 = (f32[4,4,4,128]{3,2,1,0:T(4,128)S(1)}, f32[4,4,4,128]{3,2,1,0:T(4,128)S(1)}, u32[]{:S(2)}, u32[]{:S(2)}) collective-permute-start(f32[4,4,4,128]{3,2,1,0:T(4,128)S(1)} %get-tuple-element.57), channel_id=1, source_target_pairs={{0,1},{1,0},{2,3},{3,2},{4,5},{5,4},{6,7},{7,6},{8,9},{9,8},{10,11... | collective-permute-start | bytes 98312 | tf_op jit(solution)/shard_map/ppermute | solution.py:507
  11.7 2.4 %collective-permute-start.3 = (f32[4,4,4,128]{3,2,1,0:T(4,128)S(1)}, f32[4,4,4,128]{3,2,1,0:T(4,128)S(1)}, u32[]{:S(2)}, u32[]{:S(2)}) collective-permute-start(f32[4,4,4,128]{3,2,1,0:T(4,128)S(1)} %get-tuple-element.58), channel_id=1, source_target_pairs={{0,3},{1,2},{2,1},{3,0},{4,7},{5,6},{6,5},{7,4},{8,11},{9,10},{10,... | collective-permute-start | bytes 98312 | tf_op jit(solution)/shard_map/ppermute | solution.py:506
  14.0 0.6 %shard_map.105 = (bf16[128,512]{1,0:T(8,128)(2,1)S(1)}, f32[1,512]{1,0:T(1,128)S(1)}, f32[512,768]{1,0:T(8,128)S(1)}, bf16[32,512]{1,0:T(8,128)(2,1)S(1)}, f32[128,2048]{1,0:T(8,128)S(1)}) custom-call(s32[1,256]{1,0:T(1,128)S(1)} %get-tuple-element.41.active_ref, f32[8,512]{1,0:T(8,128)S(1)} %get-tuple-element.42.state_ref, ...), custom_call_target="tpu_custom_call" | custom-call | tf_op jit(solution)/shard_map/pallas_call | solution.py:77
  14.6 2.2 %all-to-all-done.got_ref = f32[32,2,128]{2,1,0:T(2,128)S(1)} async-done(((f32[32,2,128]{2,1,0:T(2,128)}), f32[32,2,128]{2,1,0:T(2,128)S(1)}, u32[]{:S(2)}, u32[]{:S(2)}) %all-to-all-start) | async-done | bytes 32800 | tf_op jit(solution)/shard_map/all_to_all | solution.py:65
  16.9 2.2 %shard_map.106 = (f32[32,2,128]{2,1,0:T(2,128)}, f32[8,256]{1,0:T(8,128)S(1)}) custom-call(f32[32,2,128]{2,1,0:T(2,128)S(1)} %all-to-all-done.got_ref, s32[1,256]{1,0:T(1,128)S(1)} %get-tuple-element.41.active_ref, f32[512,768]{1,0:T(8,128)S(1)} %get-tuple-element.47.stars_ref, bf16[32,512]{1,0:T(8,128)(2,1)S(1)} %get-tuple-element.48.star_left_ref, ...), custom_call_target="tpu_custom_call" | custom-call | tf_op jit(solution)/shard_map/pallas_call | solution.py:77
  19.0 2.6 %all-to-all-start.1 = ((f32[32,2,128]{2,1,0:T(2,128)}), f32[32,2,128]{2,1,0:T(2,128)S(1)}, u32[]{:S(2)}, u32[]{:S(2)}) async-start(f32[32,2,128]{2,1,0:T(2,128)} %get-tuple-element.50), calls=%async_computation.1 | async-start | bytes 65536 | tf_op jit(solution)/shard_map/all_to_all | solution.py:65
  21.6 0.0 collective-permute-done.2
  21.6 0.0 collective-permute-done.3
  21.6 6.8 %conditional.1 = ((f32[3,4,8,64]{3,2,1,0:T(8,128)}, f32[3,4,8,64]{3,2,1,0:T(8,128)})) conditional(s32[]{:T(128)} %convert_element_type.3, () %tuple.15, (f32[4,4,8,128]{3,2,1,0:T(8,128)S(1)}, f32[4,4,4,128]{3,2,1,0:T(4,128)S(1)}, f32[4,4,4,128]{3,2,1,0:T(4,128)S(1)}, f32[8,256]{1,0:T(8,128)S(1)}) %tuple.16), branch_computations={%region_0.0_spmd, %region_1.0_spmd} | conditional | bytes 720984 | solution.py:598
  21.7 0.2 collective-permute-start
  21.9 2.6 %collective-permute-start.1 = (f32[22,8,128]{2,1,0:T(8,128)S(1)}, f32[22,8,128]{2,1,0:T(8,128)S(1)}, u32[]{:S(2)}, u32[]{:S(2)}) collective-permute-start(f32[22,8,128]{2,1,0:T(8,128)S(1)} %get-tuple-element.14), channel_id=1, source_target_pairs={{0,28},{4,8},{8,4},{12,16},{16,12},{20,24},{24,20},{28,0},{1,29},{... | collective-permute-start | bytes 270344 | tf_op jit(solution)/shard_map/cond/branch_1_fun/ppermute | solution.py:506
  24.4 2.6 %branch_1_fun.4.kick_ref = f32[3,5,16,128]{3,2,1,0:T(8,128)S(1)} custom-call(f32[8,256]{1,0:T(8,128)S(1)} %get-tuple-element.11.order_ref.target_ref), custom_call_target="tpu_custom_call" | custom-call | tf_op jit(solution)/shard_map/cond/branch_1_fun/pallas_call | solution.py:77
  27.1 0.0 collective-permute-done.near_ref
  27.1 0.1 collective-permute-done.1.far_ref
  27.2 1.2 %branch_1_fun.5 = (f32[3,4,8,64]{3,2,1,0:T(8,128)}, f32[3,4,8,64]{3,2,1,0:T(8,128)}) custom-call(f32[4,4,16,128]{3,2,1,0:T(8,128)S(1)} %get-tuple-element.12.own_ref, f32[22,8,128]{2,1,0:T(8,128)S(1)} %collective-permute-done.near_ref, f32[22,8,128]{2,1,0:T(8,128)S(1)} %collective-permute-done.1.far_ref, f32[3,5,16,128]{3,2,1,0:T(8,128)S(1)} %branch_1_fun.4.kick_ref), custom_call_target="tpu_custom_call" | custom-call | tf_op jit(solution)/shard_map/cond/branch_1_fun/pallas_call | solution.py:77
  28.4 0.3 %all-to-all-done.1.back_ref = f32[32,2,128]{2,1,0:T(2,128)S(1)} async-done(((f32[32,2,128]{2,1,0:T(2,128)}), f32[32,2,128]{2,1,0:T(2,128)S(1)}, u32[]{:S(2)}, u32[]{:S(2)}) %all-to-all-start.1) | async-done | bytes 32800 | tf_op jit(solution)/shard_map/all_to_all | solution.py:65
  28.7 0.8 %shard_map.108 = f32[12,512]{1,0:T(8,128)} custom-call(f32[32,2,128]{2,1,0:T(2,128)S(1)} %all-to-all-done.1.back_ref, f32[3,512]{1,0:T(4,128)S(1)} %get-tuple-element.51.pos_ref, f32[3,512]{1,0:T(4,128)S(1)} %get-tuple-element.52.vel_ref, f32[6,512]{1,0:T(8,128)S(1)} %get-tuple-element.53.acc_ref, bf16[128,512]{1,0:T(8,128)(2,1)S(1)} %get-tuple-element.54.slot_ref, ...), custom_call_target="tpu_custom_call" | custom-call | tf_op jit(solution)/shard_map/pallas_call | solution.py:77
  (2 shorter events, 0.0 us)
Async XLA Ops:
  2.4 14.4 %all-to-all-start = ((f32[32,2,128]{2,1,0:T(2,128)}), f32[32,2,128]{2,1,0:T(2,128)S(1)}, u32[]{:S(2)}, u32[]{:S(2)}) async-start(f32[32,2,128]{2,1,0:T(2,128)} %get-tuple-element.40.order_ref), calls=%async_computation | async-start | bytes 65536 | tf_op jit(solution)/shard_map/all_to_all | solution.py:65
  9.8 11.8 %collective-permute-start.2 = (f32[4,4,4,128]{3,2,1,0:T(4,128)S(1)}, f32[4,4,4,128]{3,2,1,0:T(4,128)S(1)}, u32[]{:S(2)}, u32[]{:S(2)}) collective-permute-start(f32[4,4,4,128]{3,2,1,0:T(4,128)S(1)} %get-tuple-element.57), channel_id=1, source_target_pairs={{0,1},{1,0},{2,3},{3,2},{4,5},{5,4},{6,7},{7,6},{8,9},{9,8},{10,11... | collective-permute-start | bytes 98312 | tf_op jit(solution)/shard_map/ppermute | solution.py:507
  11.7 10.0 %collective-permute-start.3 = (f32[4,4,4,128]{3,2,1,0:T(4,128)S(1)}, f32[4,4,4,128]{3,2,1,0:T(4,128)S(1)}, u32[]{:S(2)}, u32[]{:S(2)}) collective-permute-start(f32[4,4,4,128]{3,2,1,0:T(4,128)S(1)} %get-tuple-element.58), channel_id=1, source_target_pairs={{0,3},{1,2},{2,1},{3,0},{4,7},{5,6},{6,5},{7,4},{8,11},{9,10},{10,... | collective-permute-start | bytes 98312 | tf_op jit(solution)/shard_map/ppermute | solution.py:506
  19.0 9.7 %all-to-all-start.1 = ((f32[32,2,128]{2,1,0:T(2,128)}), f32[32,2,128]{2,1,0:T(2,128)S(1)}, u32[]{:S(2)}, u32[]{:S(2)}) async-start(f32[32,2,128]{2,1,0:T(2,128)} %get-tuple-element.50), calls=%async_computation.1 | async-start | bytes 65536 | tf_op jit(solution)/shard_map/all_to_all | solution.py:65
  21.7 5.4 %collective-permute-start = (f32[22,8,128]{2,1,0:T(8,128)S(1)}, f32[22,8,128]{2,1,0:T(8,128)S(1)}, u32[]{:S(2)}, u32[]{:S(2)}) collective-permute-start(f32[22,8,128]{2,1,0:T(8,128)S(1)} %get-tuple-element.13), channel_id=1, source_target_pairs={{0,4},{4,0},{8,12},{12,8},{16,20},{20,16},{24,28},{28,24},{1,5},{5... | collective-permute-start | bytes 270344 | tf_op jit(solution)/shard_map/cond/branch_1_fun/ppermute | solution.py:507
  21.9 5.3 %collective-permute-start.1 = (f32[22,8,128]{2,1,0:T(8,128)S(1)}, f32[22,8,128]{2,1,0:T(8,128)S(1)}, u32[]{:S(2)}, u32[]{:S(2)}) collective-permute-start(f32[22,8,128]{2,1,0:T(8,128)S(1)} %get-tuple-element.14), channel_id=1, source_target_pairs={{0,28},{4,8},{8,4},{12,16},{16,12},{20,24},{24,20},{28,0},{1,29},{... | collective-permute-start | bytes 270344 | tf_op jit(solution)/shard_map/cond/branch_1_fun/ppermute | solution.py:506

commit v8 on v7

--- a/solution.py
+++ b/solution.py
@@ -234,11 +234,19 @@
     slots = lanes // 4
     starts = rank_at(iota((devices, width), 0)) * total
     active = active_ref[...]
-    owned = one_hot((active >= starts) & (active < starts + total)).astype(bf16)
-    owned3 = jnp.concatenate([owned, owned, owned], 0)
-    slot_hit = one_hot(iota((slots, width), 0) == iota((slots, width), 1) % slots)
-    spread = dot_of(stack3(jnp.concatenate([got_ref[:, 0, :], got_ref[:, 1, :]], 1)), owned3, 0, 0)
-    targets = jnp.sum(spread.reshape(8, slots, width) * slot_hit[None], 1)
+    owned = one_hot((active >= starts) & (active < starts + total))
+    group = iota((devices, lanes), 1) // slots
+    rows = []
+    for half in range(2):
+        raw = got_ref[:, half, :]
+        turned = [raw] + [pltpu.roll(raw, k * slots, 1) for k in range(1, 4)]
+        for comp in range(4 - half):
+            same = turned[(3 - comp) % 4]
+            for at in range(3):
+                same = jnp.where(group == at, turned[(at - comp) % 4], same)
+            picked = jnp.concatenate([same] * (width // lanes), 1) * owned
+            rows.append(jnp.sum(picked, 0, keepdims=True))
+    targets = jnp.concatenate(rows + [jnp.zeros((1, width), f32)], 0)
     target_ref[...] = targets
 
     first_x = lax.axis_index("star") * ext_x
@@ -294,13 +302,19 @@
     new_acc = gas_acc + (pulls[0:3] - targets[0:3] * pulls[3:4])
     new_jerk = pulls[4:7] - targets[4:7] * pulls[3:4]
     new_jerk = new_jerk - 3.0 * (bends[0:3] - targets[0:3] * bends[3:4])
-    none = jnp.zeros((1, width), f32)
-    partial = gravity * jnp.concatenate([new_acc, none, new_jerk, none], 0)
-    owned3 = jnp.concatenate([owned, owned, owned], 1)
-    for half in range(2):
-        spread = partial[4 * half : 4 * half + 4][:, None, :] * slot_hit[None]
-        spread = jnp.concatenate(split3(spread.reshape(4 * slots, width)), 1)
-        sent = dot_of(owned3, spread, 1, 1)
+    for half, terms in enumerate((new_acc, new_jerk)):
+        parts = []
+        for comp in range(3):
+            held = owned * (gravity * terms[comp : comp + 1])
+            parts.append(sum(held[:, k : k + lanes] for k in range(0, width, lanes)))
+        parts.append(jnp.zeros((devices, lanes), f32))
+        sent = None
+        for k in range(4):
+            mixed = parts[(3 + k) % 4]
+            for at in range(3):
+                mixed = jnp.where(group == at, parts[(at + k) % 4], mixed)
+            mixed = pltpu.roll(mixed, k * slots, 1) if k else mixed
+            sent = mixed if sent is None else sent + mixed
         if chunked:
             step_at = pl.program_id(0)
 

time: 29.8 us -> 29.5 us (0.990)
  transfers between devices with their start and end apart: 6 -> 6, of which waited for: 3 -> 3; matrix products, arithmetic and copies ran while one was open for 0% -> 0% of each run, Pallas kernels for 23% -> 22%
where the time goes in v8:
time: 29.5 us; the launch traced here: 29.3 us
  starting transfers between devices  16.8 us (57%)
  Pallas kernels  9.08 us (31%)
  waiting for transfers between devices  2.65 us (9%)
  between operations  0.69 us (2%)
    all_to_all x2, starting transfers between devices, exchange(): lax.all_to_all(pieces, both, 0, 0, axis_index_groups=[order], tiled=True)  9.87 us
    pallas_call x9, Pallas kernels, call(): pl.pallas_call(kernel, out_shape=outs, scratch_shapes=list(scratch), cost...  9.08 us
    ppermute x2, starting transfers between devices, swap_pairs(): got_far = lax.ppermute(far, axis, between)  4.94 us
    all_to_all x2, waiting for transfers between devices, exchange(): lax.all_to_all(pieces, both, 0, 0, axis_index_groups=[order], tiled=True)  2.53 us
    ppermute x2, starting transfers between devices, swap_pairs(): got_near = lax.ppermute(near, axis, inside)  2.01 us
  transfers between devices with their start and end apart: 6, of which 3 were waited for; matrix products, arithmetic and copies ran while one was open for 0% of the time, Pallas kernels for 22%

profile of v8, /device:TPU:0, one launch (start us, length us, event | category | flops | bytes accessed | tf_op | source)
XLA Modules:
  0.0 29.3 jit_solution(1451528552552620765)
XLA Ops:
  0.6 1.8 %shard_map.103 = (f32[3,512]{1,0:T(4,128)S(1)}, f32[3,512]{1,0:T(4,128)S(1)}, f32[6,512]{1,0:T(8,128)S(1)}, f32[1,512]{1,0:T(1,128)}, s32[1,256]{1,0:T(1,128)S(1...) custom-call(f32[3,512]{1,0:T(4,128)} %refs_0_.1, ...), custom_call_target="tpu_custom_call" | custom-call | tf_op jit(solution)/shard_map/pallas_call | solution.py:77
  2.4 7.3 %all-to-all-start = ((f32[32,2,128]{2,1,0:T(2,128)}), f32[32,2,128]{2,1,0:T(2,128)S(1)}, u32[]{:S(2)}, u32[]{:S(2)}) async-start(f32[32,2,128]{2,1,0:T(2,128)} %get-tuple-element.40.order_ref), calls=%async_computation | async-start | bytes 65536 | tf_op jit(solution)/shard_map/all_to_all | solution.py:65
  9.7 0.1 shard_map.104
  9.8 1.8 %collective-permute-start.2 = (f32[4,4,4,128]{3,2,1,0:T(4,128)S(1)}, f32[4,4,4,128]{3,2,1,0:T(4,128)S(1)}, u32[]{:S(2)}, u32[]{:S(2)}) collective-permute-start(f32[4,4,4,128]{3,2,1,0:T(4,128)S(1)} %get-tuple-element.57), channel_id=1, source_target_pairs={{0,1},{1,0},{2,3},{3,2},{4,5},{5,4},{6,7},{7,6},{8,9},{9,8},{10,11... | collective-permute-start | bytes 98312 | tf_op jit(solution)/shard_map/ppermute | solution.py:521
  11.7 2.4 %collective-permute-start.3 = (f32[4,4,4,128]{3,2,1,0:T(4,128)S(1)}, f32[4,4,4,128]{3,2,1,0:T(4,128)S(1)}, u32[]{:S(2)}, u32[]{:S(2)}) collective-permute-start(f32[4,4,4,128]{3,2,1,0:T(4,128)S(1)} %get-tuple-element.58), channel_id=1, source_target_pairs={{0,3},{1,2},{2,1},{3,0},{4,7},{5,6},{6,5},{7,4},{8,11},{9,10},{10,... | collective-permute-start | bytes 98312 | tf_op jit(solution)/shard_map/ppermute | solution.py:520
  14.0 0.6 %shard_map.105 = (bf16[128,512]{1,0:T(8,128)(2,1)S(1)}, f32[1,512]{1,0:T(1,128)S(1)}, f32[512,768]{1,0:T(8,128)S(1)}, bf16[32,512]{1,0:T(8,128)(2,1)S(1)}, f32[128,2048]{1,0:T(8,128)S(1)}) custom-call(s32[1,256]{1,0:T(1,128)S(1)} %get-tuple-element.41.active_ref, f32[8,512]{1,0:T(8,128)S(1)} %get-tuple-element.42.state_ref, ...), custom_call_target="tpu_custom_call" | custom-call | tf_op jit(solution)/shard_map/pallas_call | solution.py:77
  14.6 2.2 %all-to-all-done.got_ref = f32[32,2,128]{2,1,0:T(2,128)S(1)} async-done(((f32[32,2,128]{2,1,0:T(2,128)}), f32[32,2,128]{2,1,0:T(2,128)S(1)}, u32[]{:S(2)}, u32[]{:S(2)}) %all-to-all-start) | async-done | bytes 32800 | tf_op jit(solution)/shard_map/all_to_all | solution.py:65
  16.9 1.9 %shard_map.106 = (f32[32,2,128]{2,1,0:T(2,128)}, f32[8,256]{1,0:T(8,128)S(1)}) custom-call(f32[32,2,128]{2,1,0:T(2,128)S(1)} %all-to-all-done.got_ref, s32[1,256]{1,0:T(1,128)S(1)} %get-tuple-element.41.active_ref, f32[512,768]{1,0:T(8,128)S(1)} %get-tuple-element.47.stars_ref, bf16[32,512]{1,0:T(8,128)(2,1)S(1)} %get-tuple-element.48.star_left_ref, ...), custom_call_target="tpu_custom_call" | custom-call | tf_op jit(solution)/shard_map/pallas_call | solution.py:77
  18.8 2.6 %all-to-all-start.1 = ((f32[32,2,128]{2,1,0:T(2,128)}), f32[32,2,128]{2,1,0:T(2,128)S(1)}, u32[]{:S(2)}, u32[]{:S(2)}) async-start(f32[32,2,128]{2,1,0:T(2,128)} %get-tuple-element.50), calls=%async_computation.1 | async-start | bytes 65536 | tf_op jit(solution)/shard_map/all_to_all | solution.py:65
  21.4 0.0 collective-permute-done.2
  21.4 0.0 collective-permute-done.3
  21.4 6.8 %conditional.1 = ((f32[3,4,8,64]{3,2,1,0:T(8,128)}, f32[3,4,8,64]{3,2,1,0:T(8,128)})) conditional(s32[]{:T(128)} %convert_element_type.3, () %tuple.15, (f32[4,4,8,128]{3,2,1,0:T(8,128)S(1)}, f32[4,4,4,128]{3,2,1,0:T(4,128)S(1)}, f32[4,4,4,128]{3,2,1,0:T(4,128)S(1)}, f32[8,256]{1,0:T(8,128)S(1)}) %tuple.16), branch_computations={%region_0.0_spmd, %region_1.0_spmd} | conditional | bytes 720984 | solution.py:612
  21.4 0.2 collective-permute-start
  21.6 2.6 %collective-permute-start.1 = (f32[22,8,128]{2,1,0:T(8,128)S(1)}, f32[22,8,128]{2,1,0:T(8,128)S(1)}, u32[]{:S(2)}, u32[]{:S(2)}) collective-permute-start(f32[22,8,128]{2,1,0:T(8,128)S(1)} %get-tuple-element.14), channel_id=1, source_target_pairs={{0,28},{4,8},{8,4},{12,16},{16,12},{20,24},{24,20},{28,0},{1,29},{... | collective-permute-start | bytes 270344 | tf_op jit(solution)/shard_map/cond/branch_1_fun/ppermute | solution.py:520
  24.2 2.6 %branch_1_fun.4.kick_ref = f32[3,5,16,128]{3,2,1,0:T(8,128)S(1)} custom-call(f32[8,256]{1,0:T(8,128)S(1)} %get-tuple-element.11.order_ref.target_ref), custom_call_target="tpu_custom_call" | custom-call | tf_op jit(solution)/shard_map/cond/branch_1_fun/pallas_call | solution.py:77
  26.8 0.0 collective-permute-done.near_ref
  26.8 0.1 collective-permute-done.1.far_ref
  26.9 1.2 %branch_1_fun.5 = (f32[3,4,8,64]{3,2,1,0:T(8,128)}, f32[3,4,8,64]{3,2,1,0:T(8,128)}) custom-call(f32[4,4,16,128]{3,2,1,0:T(8,128)S(1)} %get-tuple-element.12.own_ref, f32[22,8,128]{2,1,0:T(8,128)S(1)} %collective-permute-done.near_ref, f32[22,8,128]{2,1,0:T(8,128)S(1)} %collective-permute-done.1.far_ref, f32[3,5,16,128]{3,2,1,0:T(8,128)S(1)} %branch_1_fun.4.kick_ref), custom_call_target="tpu_custom_call" | custom-call | tf_op jit(solution)/shard_map/cond/branch_1_fun/pallas_call | solution.py:77
  28.2 0.3 %all-to-all-done.1.back_ref = f32[32,2,128]{2,1,0:T(2,128)S(1)} async-done(((f32[32,2,128]{2,1,0:T(2,128)}), f32[32,2,128]{2,1,0:T(2,128)S(1)}, u32[]{:S(2)}, u32[]{:S(2)}) %all-to-all-start.1) | async-done | bytes 32800 | tf_op jit(solution)/shard_map/all_to_all | solution.py:65
  28.5 0.8 %shard_map.108 = f32[12,512]{1,0:T(8,128)} custom-call(f32[32,2,128]{2,1,0:T(2,128)S(1)} %all-to-all-done.1.back_ref, f32[3,512]{1,0:T(4,128)S(1)} %get-tuple-element.51.pos_ref, f32[3,512]{1,0:T(4,128)S(1)} %get-tuple-element.52.vel_ref, f32[6,512]{1,0:T(8,128)S(1)} %get-tuple-element.53.acc_ref, bf16[128,512]{1,0:T(8,128)(2,1)S(1)} %get-tuple-element.54.slot_ref, ...), custom_call_target="tpu_custom_call" | custom-call | tf_op jit(solution)/shard_map/pallas_call | solution.py:77
  (2 shorter events, 0.0 us)
Async XLA Ops:
  2.4 14.4 %all-to-all-start = ((f32[32,2,128]{2,1,0:T(2,128)}), f32[32,2,128]{2,1,0:T(2,128)S(1)}, u32[]{:S(2)}, u32[]{:S(2)}) async-start(f32[32,2,128]{2,1,0:T(2,128)} %get-tuple-element.40.order_ref), calls=%async_computation | async-start | bytes 65536 | tf_op jit(solution)/shard_map/all_to_all | solution.py:65
  9.8 11.5 %collective-permute-start.2 = (f32[4,4,4,128]{3,2,1,0:T(4,128)S(1)}, f32[4,4,4,128]{3,2,1,0:T(4,128)S(1)}, u32[]{:S(2)}, u32[]{:S(2)}) collective-permute-start(f32[4,4,4,128]{3,2,1,0:T(4,128)S(1)} %get-tuple-element.57), channel_id=1, source_target_pairs={{0,1},{1,0},{2,3},{3,2},{4,5},{5,4},{6,7},{7,6},{8,9},{9,8},{10,11... | collective-permute-start | bytes 98312 | tf_op jit(solution)/shard_map/ppermute | solution.py:521
  11.7 9.7 %collective-permute-start.3 = (f32[4,4,4,128]{3,2,1,0:T(4,128)S(1)}, f32[4,4,4,128]{3,2,1,0:T(4,128)S(1)}, u32[]{:S(2)}, u32[]{:S(2)}) collective-permute-start(f32[4,4,4,128]{3,2,1,0:T(4,128)S(1)} %get-tuple-element.58), channel_id=1, source_target_pairs={{0,3},{1,2},{2,1},{3,0},{4,7},{5,6},{6,5},{7,4},{8,11},{9,10},{10,... | collective-permute-start | bytes 98312 | tf_op jit(solution)/shard_map/ppermute | solution.py:520
  18.8 9.7 %all-to-all-start.1 = ((f32[32,2,128]{2,1,0:T(2,128)}), f32[32,2,128]{2,1,0:T(2,128)S(1)}, u32[]{:S(2)}, u32[]{:S(2)}) async-start(f32[32,2,128]{2,1,0:T(2,128)} %get-tuple-element.50), calls=%async_computation.1 | async-start | bytes 65536 | tf_op jit(solution)/shard_map/all_to_all | solution.py:65
  21.4 5.4 %collective-permute-start = (f32[22,8,128]{2,1,0:T(8,128)S(1)}, f32[22,8,128]{2,1,0:T(8,128)S(1)}, u32[]{:S(2)}, u32[]{:S(2)}) collective-permute-start(f32[22,8,128]{2,1,0:T(8,128)S(1)} %get-tuple-element.13), channel_id=1, source_target_pairs={{0,4},{4,0},{8,12},{12,8},{16,20},{20,16},{24,28},{28,24},{1,5},{5... | collective-permute-start | bytes 270344 | tf_op jit(solution)/shard_map/cond/branch_1_fun/ppermute | solution.py:521
  21.6 5.3 %collective-permute-start.1 = (f32[22,8,128]{2,1,0:T(8,128)S(1)}, f32[22,8,128]{2,1,0:T(8,128)S(1)}, u32[]{:S(2)}, u32[]{:S(2)}) collective-permute-start(f32[22,8,128]{2,1,0:T(8,128)S(1)} %get-tuple-element.14), channel_id=1, source_target_pairs={{0,28},{4,8},{8,4},{12,16},{16,12},{20,24},{24,20},{28,0},{1,29},{... | collective-permute-start | bytes 270344 | tf_op jit(solution)/shard_map/cond/branch_1_fun/ppermute | solution.py:520

commit v9 on v8

--- a/solution.py
+++ b/solution.py
@@ -108,12 +108,14 @@
     state = jnp.concatenate([pred_pos, mass_ref[...], pred_vel, jnp.zeros((1, total), f32)], 0)
     state_ref[...] = state
     local = active_ref[...] - my_rank() * total
-    hit = one_hot(iota((total, listed), 0) == local).astype(bf16)
+    local = jnp.where((local >= 0) & (local < total), local + 1, 0)
+    mine = sum(local[:, k : k + lanes] for k in range(0, listed, lanes))
+    mine = jnp.broadcast_to(mine, (8, lanes))
+    for shift in (2 * slots, slots):
+        mine = mine + pltpu.roll(mine, shift, 1)
+    hit = one_hot(iota((total, lanes), 0) + 1 == mine[0:1]).astype(bf16)
     pieces = dot_of(stack3(state), hit)
-    placed = pieces[0:8] + pieces[8:16] + pieces[16:24]
-    spread = sum(placed[:, k : k + lanes] for k in range(0, listed, lanes))
-    for shift in (2 * slots, slots):
-        spread = spread + pltpu.roll(spread, shift, 1)
+    spread = pieces[0:8] + pieces[8:16] + pieces[16:24]
     lane = iota((8, lanes), 1)
     row = iota((8, lanes), 0)
     spread = jnp.where(row % 4 == lane // slots, spread, 0.0)
@@ -190,7 +192,9 @@
     pick = one_hot((iota((lanes, listed), 0) % slots == iota((lanes, listed), 1) % slots) & mine).astype(bf16)
     hit = one_hot(iota((total, listed), 0) == local).astype(bf16)
     slot = dot_of(pick, hit, 1, 1)
-    slot_ref[...] = slot.astype(bf16)
+    at = jnp.sum(slot[0:slots] * iota((slots, total), 0).astype(f32), 0, keepdims=True)
+    part = iota((8, total), 0) % 3 * slots
+    slot_ref[...] = jnp.minimum(part, 2 * slots) + at.astype(i32)
     listed_ref[...] = jnp.sum(slot[0:slots], 0, keepdims=True)
     state = state_ref[...]
     ask = one_hot(iota((24, 6 * lanes), 0) % 8 == wide_row((24, 6 * lanes))).astype(bf16)
@@ -268,7 +272,7 @@
         pulls = pulls + weigh(left, weight)
         bends = bends + weigh(left, bend)
     gas_acc = []
-    step = 32
+    step = ext_z
     for lane in range(0, width, lanes):
         def row_of(k):
             return jnp.broadcast_to(targets[k : k + 1, lane : lane + lanes], (8, lanes))
@@ -489,14 +493,16 @@
 
 
 def update_kernel(back_ref, pos_ref, vel_ref, acc_ref, slot_ref, listed_ref, order_ref, out_ref):
-    slots = lanes // 4
     summed = jnp.sum(back_ref[...], 0)
-    row, lane = iota((8, lanes), 0), iota((8, lanes), 1)
-    terms = jnp.where(row < 3, summed[0:1], summed[1:2])
-    terms = jnp.where((row < 6) & (row % 3 == lane // slots), terms, 0.0)
+    terms = jnp.where(iota((8, lanes), 0) < 3, summed[0:1], summed[1:2])
     slot = slot_ref[...]
-    pieces = dot_of(stack3(terms), slot)
-    new = pieces[0:8] + pieces[8:16] + pieces[16:24]
+    new = jnp.concatenate(
+        [
+            jnp.take_along_axis(terms, slot[:, k : k + lanes], axis=1, mode="promise_in_bounds")
+            for k in range(0, slot.shape[1], lanes)
+        ],
+        1,
+    )
     new_acc, new_jerk = new[0:3], new[3:6]
     pos, vel = pos_ref[...], vel_ref[...]
     old_acc, old_jerk = acc_ref[0:3], acc_ref[3:6]
@@ -558,7 +564,7 @@
     near, far = swap_pairs(near, far, "gas")
     slot, is_listed, stars, star_left, cells = call(
         index_kernel,
-        (shape(lanes, total, dtype=bf16), shape(1, total), shape(total, 6 * lanes),
+        (shape(8, total, dtype=i32), shape(1, total), shape(total, 6 * lanes),
          shape(32, total, dtype=bf16), shape(2 * ext_z, ext_x * ext_y // 2 * lanes)),
         names, state, rows,
     )

time: 29.5 us -> 29.4 us (level)
  no operation moved by 1% of the time
where the time goes in v9:
time: 29.4 us; the launch traced here: 29.2 us
  starting transfers between devices  16.8 us (57%)
  Pallas kernels  8.98 us (31%)
  waiting for transfers between devices  2.64 us (9%)
  between operations  0.69 us (2%)
    all_to_all x2, starting transfers between devices, exchange(): lax.all_to_all(pieces, both, 0, 0, axis_index_groups=[order], tiled=True)  9.87 us
    pallas_call x9, Pallas kernels, call(): pl.pallas_call(kernel, out_shape=outs, scratch_shapes=list(scratch), cost...  8.98 us
    ppermute x2, starting transfers between devices, swap_pairs(): got_far = lax.ppermute(far, axis, between)  4.94 us
    all_to_all x2, waiting for transfers between devices, exchange(): lax.all_to_all(pieces, both, 0, 0, axis_index_groups=[order], tiled=True)  2.53 us
    ppermute x2, starting transfers between devices, swap_pairs(): got_near = lax.ppermute(near, axis, inside)  2.01 us
  transfers between devices with their start and end apart: 6, of which 3 were waited for; matrix products, arithmetic and copies ran while one was open for 0% of the time, Pallas kernels for 22%

profile of v9, /device:TPU:0, one launch (start us, length us, event | category | flops | bytes accessed | tf_op | source)
XLA Modules:
  0.0 29.2 jit_solution(1443330872799478727)
XLA Ops:
  0.6 1.8 %shard_map.103 = (f32[3,512]{1,0:T(4,128)S(1)}, f32[3,512]{1,0:T(4,128)S(1)}, f32[6,512]{1,0:T(8,128)S(1)}, f32[1,512]{1,0:T(1,128)}, s32[1,256]{1,0:T(1,128)S(1...) custom-call(f32[3,512]{1,0:T(4,128)} %refs_0_.1, ...), custom_call_target="tpu_custom_call" | custom-call | tf_op jit(solution)/shard_map/pallas_call | solution.py:77
  2.4 7.3 %all-to-all-start = ((f32[32,2,128]{2,1,0:T(2,128)}), f32[32,2,128]{2,1,0:T(2,128)S(1)}, u32[]{:S(2)}, u32[]{:S(2)}) async-start(f32[32,2,128]{2,1,0:T(2,128)} %get-tuple-element.40.order_ref), calls=%async_computation | async-start | bytes 65536 | tf_op jit(solution)/shard_map/all_to_all | solution.py:65
  9.7 0.1 shard_map.104
  9.8 1.8 %collective-permute-start.2 = (f32[4,4,4,128]{3,2,1,0:T(4,128)S(1)}, f32[4,4,4,128]{3,2,1,0:T(4,128)S(1)}, u32[]{:S(2)}, u32[]{:S(2)}) collective-permute-start(f32[4,4,4,128]{3,2,1,0:T(4,128)S(1)} %get-tuple-element.57), channel_id=1, source_target_pairs={{0,1},{1,0},{2,3},{3,2},{4,5},{5,4},{6,7},{7,6},{8,9},{9,8},{10,11... | collective-permute-start | bytes 98312 | tf_op jit(solution)/shard_map/ppermute | solution.py:527
  11.6 2.4 %collective-permute-start.3 = (f32[4,4,4,128]{3,2,1,0:T(4,128)S(1)}, f32[4,4,4,128]{3,2,1,0:T(4,128)S(1)}, u32[]{:S(2)}, u32[]{:S(2)}) collective-permute-start(f32[4,4,4,128]{3,2,1,0:T(4,128)S(1)} %get-tuple-element.58), channel_id=1, source_target_pairs={{0,3},{1,2},{2,1},{3,0},{4,7},{5,6},{6,5},{7,4},{8,11},{9,10},{10,... | collective-permute-start | bytes 98312 | tf_op jit(solution)/shard_map/ppermute | solution.py:526
  14.0 0.6 %shard_map.105 = (s32[8,512]{1,0:T(8,128)S(1)}, f32[1,512]{1,0:T(1,128)S(1)}, f32[512,768]{1,0:T(8,128)S(1)}, bf16[32,512]{1,0:T(8,128)(2,1)S(1)}, f32[128,2048]{1,0:T(8,128)S(1)}) custom-call(s32[1,256]{1,0:T(1,128)S(1)} %get-tuple-element.41.active_ref, f32[8,512]{1,0:T(8,128)S(1)} %get-tuple-element.42.state_ref, f32[16,128]{1,0:T(8,128)S(1)} %get-tuple-element.46.density_ref), custom_call_target="tpu_custom_call" | custom-call | tf_op jit(solution)/shard_map/pallas_call | solution.py:77
  14.6 2.2 %all-to-all-done.got_ref = f32[32,2,128]{2,1,0:T(2,128)S(1)} async-done(((f32[32,2,128]{2,1,0:T(2,128)}), f32[32,2,128]{2,1,0:T(2,128)S(1)}, u32[]{:S(2)}, u32[]{:S(2)}) %all-to-all-start) | async-done | bytes 32800 | tf_op jit(solution)/shard_map/all_to_all | solution.py:65
  16.8 1.9 %shard_map.106 = (f32[32,2,128]{2,1,0:T(2,128)}, f32[8,256]{1,0:T(8,128)S(1)}) custom-call(f32[32,2,128]{2,1,0:T(2,128)S(1)} %all-to-all-done.got_ref, s32[1,256]{1,0:T(1,128)S(1)} %get-tuple-element.41.active_ref, f32[512,768]{1,0:T(8,128)S(1)} %get-tuple-element.47.stars_ref, bf16[32,512]{1,0:T(8,128)(2,1)S(1)} %get-tuple-element.48.star_left_ref, ...), custom_call_target="tpu_custom_call" | custom-call | tf_op jit(solution)/shard_map/pallas_call | solution.py:77
  18.7 2.6 %all-to-all-start.1 = ((f32[32,2,128]{2,1,0:T(2,128)}), f32[32,2,128]{2,1,0:T(2,128)S(1)}, u32[]{:S(2)}, u32[]{:S(2)}) async-start(f32[32,2,128]{2,1,0:T(2,128)} %get-tuple-element.50), calls=%async_computation.1 | async-start | bytes 65536 | tf_op jit(solution)/shard_map/all_to_all | solution.py:65
  21.3 0.0 collective-permute-done.2
  21.3 0.0 collective-permute-done.3
  21.3 6.8 %conditional.1 = ((f32[3,4,8,64]{3,2,1,0:T(8,128)}, f32[3,4,8,64]{3,2,1,0:T(8,128)})) conditional(s32[]{:T(128)} %convert_element_type.3, () %tuple.15, (f32[4,4,8,128]{3,2,1,0:T(8,128)S(1)}, f32[4,4,4,128]{3,2,1,0:T(4,128)S(1)}, f32[4,4,4,128]{3,2,1,0:T(4,128)S(1)}, f32[8,256]{1,0:T(8,128)S(1)}) %tuple.16), branch_computations={%region_0.0_spmd, %region_1.0_spmd} | conditional | bytes 720984 | solution.py:618
  21.4 0.2 collective-permute-start
  21.6 2.6 %collective-permute-start.1 = (f32[22,8,128]{2,1,0:T(8,128)S(1)}, f32[22,8,128]{2,1,0:T(8,128)S(1)}, u32[]{:S(2)}, u32[]{:S(2)}) collective-permute-start(f32[22,8,128]{2,1,0:T(8,128)S(1)} %get-tuple-element.14), channel_id=1, source_target_pairs={{0,28},{4,8},{8,4},{12,16},{16,12},{20,24},{24,20},{28,0},{1,29},{... | collective-permute-start | bytes 270344 | tf_op jit(solution)/shard_map/cond/branch_1_fun/ppermute | solution.py:526
  24.1 2.6 %branch_1_fun.4.kick_ref = f32[3,5,16,128]{3,2,1,0:T(8,128)S(1)} custom-call(f32[8,256]{1,0:T(8,128)S(1)} %get-tuple-element.11.order_ref.target_ref), custom_call_target="tpu_custom_call" | custom-call | tf_op jit(solution)/shard_map/cond/branch_1_fun/pallas_call | solution.py:77
  26.8 0.0 collective-permute-done.near_ref
  26.8 0.1 collective-permute-done.1.far_ref
  26.9 1.2 %branch_1_fun.5 = (f32[3,4,8,64]{3,2,1,0:T(8,128)}, f32[3,4,8,64]{3,2,1,0:T(8,128)}) custom-call(f32[4,4,16,128]{3,2,1,0:T(8,128)S(1)} %get-tuple-element.12.own_ref, f32[22,8,128]{2,1,0:T(8,128)S(1)} %collective-permute-done.near_ref, f32[22,8,128]{2,1,0:T(8,128)S(1)} %collective-permute-done.1.far_ref, f32[3,5,16,128]{3,2,1,0:T(8,128)S(1)} %branch_1_fun.4.kick_ref), custom_call_target="tpu_custom_call" | custom-call | tf_op jit(solution)/shard_map/cond/branch_1_fun/pallas_call | solution.py:77
  28.1 0.3 %all-to-all-done.1.back_ref = f32[32,2,128]{2,1,0:T(2,128)S(1)} async-done(((f32[32,2,128]{2,1,0:T(2,128)}), f32[32,2,128]{2,1,0:T(2,128)S(1)}, u32[]{:S(2)}, u32[]{:S(2)}) %all-to-all-start.1) | async-done | bytes 32800 | tf_op jit(solution)/shard_map/all_to_all | solution.py:65
  28.4 0.7 %shard_map.108 = f32[12,512]{1,0:T(8,128)} custom-call(f32[32,2,128]{2,1,0:T(2,128)S(1)} %all-to-all-done.1.back_ref, f32[3,512]{1,0:T(4,128)S(1)} %get-tuple-element.51.pos_ref, f32[3,512]{1,0:T(4,128)S(1)} %get-tuple-element.52.vel_ref, f32[6,512]{1,0:T(8,128)S(1)} %get-tuple-element.53.acc_ref, s32[8,512]{1,0:T(8,128)S(1)} %get-tuple-element.54.slot_ref, ...), custom_call_target="tpu_custom_call" | custom-call | tf_op jit(solution)/shard_map/pallas_call | solution.py:77
  (2 shorter events, 0.0 us)
Async XLA Ops:
  2.4 14.4 %all-to-all-start = ((f32[32,2,128]{2,1,0:T(2,128)}), f32[32,2,128]{2,1,0:T(2,128)S(1)}, u32[]{:S(2)}, u32[]{:S(2)}) async-start(f32[32,2,128]{2,1,0:T(2,128)} %get-tuple-element.40.order_ref), calls=%async_computation | async-start | bytes 65536 | tf_op jit(solution)/shard_map/all_to_all | solution.py:65
  9.8 11.5 %collective-permute-start.2 = (f32[4,4,4,128]{3,2,1,0:T(4,128)S(1)}, f32[4,4,4,128]{3,2,1,0:T(4,128)S(1)}, u32[]{:S(2)}, u32[]{:S(2)}) collective-permute-start(f32[4,4,4,128]{3,2,1,0:T(4,128)S(1)} %get-tuple-element.57), channel_id=1, source_target_pairs={{0,1},{1,0},{2,3},{3,2},{4,5},{5,4},{6,7},{7,6},{8,9},{9,8},{10,11... | collective-permute-start | bytes 98312 | tf_op jit(solution)/shard_map/ppermute | solution.py:527
  11.6 9.7 %collective-permute-start.3 = (f32[4,4,4,128]{3,2,1,0:T(4,128)S(1)}, f32[4,4,4,128]{3,2,1,0:T(4,128)S(1)}, u32[]{:S(2)}, u32[]{:S(2)}) collective-permute-start(f32[4,4,4,128]{3,2,1,0:T(4,128)S(1)} %get-tuple-element.58), channel_id=1, source_target_pairs={{0,3},{1,2},{2,1},{3,0},{4,7},{5,6},{6,5},{7,4},{8,11},{9,10},{10,... | collective-permute-start | bytes 98312 | tf_op jit(solution)/shard_map/ppermute | solution.py:526
  18.7 9.7 %all-to-all-start.1 = ((f32[32,2,128]{2,1,0:T(2,128)}), f32[32,2,128]{2,1,0:T(2,128)S(1)}, u32[]{:S(2)}, u32[]{:S(2)}) async-start(f32[32,2,128]{2,1,0:T(2,128)} %get-tuple-element.50), calls=%async_computation.1 | async-start | bytes 65536 | tf_op jit(solution)/shard_map/all_to_all | solution.py:65
  21.4 5.4 %collective-permute-start = (f32[22,8,128]{2,1,0:T(8,128)S(1)}, f32[22,8,128]{2,1,0:T(8,128)S(1)}, u32[]{:S(2)}, u32[]{:S(2)}) collective-permute-start(f32[22,8,128]{2,1,0:T(8,128)S(1)} %get-tuple-element.13), channel_id=1, source_target_pairs={{0,4},{4,0},{8,12},{12,8},{16,20},{20,16},{24,28},{28,24},{1,5},{5... | collective-permute-start | bytes 270344 | tf_op jit(solution)/shard_map/cond/branch_1_fun/ppermute | solution.py:527
  21.6 5.3 %collective-permute-start.1 = (f32[22,8,128]{2,1,0:T(8,128)S(1)}, f32[22,8,128]{2,1,0:T(8,128)S(1)}, u32[]{:S(2)}, u32[]{:S(2)}) collective-permute-start(f32[22,8,128]{2,1,0:T(8,128)S(1)} %get-tuple-element.14), channel_id=1, source_target_pairs={{0,28},{4,8},{8,4},{12,16},{16,12},{20,24},{24,20},{28,0},{1,29},{... | collective-permute-start | bytes 270344 | tf_op jit(solution)/shard_map/cond/branch_1_fun/ppermute | solution.py:526

commit v10 on v9

--- a/solution.py
+++ b/solution.py
@@ -53,7 +53,7 @@
 
 def rank_at(place):
     star_count, gas_count = lax.axis_size("star"), lax.axis_size("gas")
-    pair, rest = place // (2 * star_count), place % (2 * star_count)
+    pair, rest = gas_count // 2 - 1 - place // (2 * star_count), place % (2 * star_count)
     side, along = rest % 2, rest // 2
     star = along + side * (star_count - 1 - 2 * along)
     gas = pair + side * (gas_count - 1 - 2 * pair)

time: 29.4 us -> 29.4 us (level)
  no operation moved by 1% of the time
where the time goes in v10:
time: 29.4 us; the launch traced here: 29.2 us
  starting transfers between devices  16.8 us (57%)
  Pallas kernels  8.98 us (31%)
  waiting for transfers between devices  2.64 us (9%)
  between operations  0.69 us (2%)
    all_to_all x2, starting transfers between devices, exchange(): lax.all_to_all(pieces, both, 0, 0, axis_index_groups=[order], tiled=True)  9.87 us
    pallas_call x9, Pallas kernels, call(): pl.pallas_call(kernel, out_shape=outs, scratch_shapes=list(scratch), cost...  8.98 us
    ppermute x2, starting transfers between devices, swap_pairs(): got_far = lax.ppermute(far, axis, between)  4.94 us
    all_to_all x2, waiting for transfers between devices, exchange(): lax.all_to_all(pieces, both, 0, 0, axis_index_groups=[order], tiled=True)  2.53 us
    ppermute x2, starting transfers between devices, swap_pairs(): got_near = lax.ppermute(near, axis, inside)  2.01 us
  transfers between devices with their start and end apart: 6, of which 3 were waited for; matrix products, arithmetic and copies ran while one was open for 0% of the time, Pallas kernels for 22%

profile of v10, /device:TPU:0, one launch (start us, length us, event | category | flops | bytes accessed | tf_op | source)
XLA Modules:
  0.0 29.2 jit_solution(10087994966712429554)
XLA Ops:
  0.6 1.8 %shard_map.103 = (f32[3,512]{1,0:T(4,128)S(1)}, f32[3,512]{1,0:T(4,128)S(1)}, f32[6,512]{1,0:T(8,128)S(1)}, f32[1,512]{1,0:T(1,128)}, s32[1,256]{1,0:T(1,128)S(1...) custom-call(f32[3,512]{1,0:T(4,128)} %refs_0_.1, ...), custom_call_target="tpu_custom_call" | custom-call | tf_op jit(solution)/shard_map/pallas_call | solution.py:77
  2.4 7.3 %all-to-all-start = ((f32[32,2,128]{2,1,0:T(2,128)}), f32[32,2,128]{2,1,0:T(2,128)S(1)}, u32[]{:S(2)}, u32[]{:S(2)}) async-start(f32[32,2,128]{2,1,0:T(2,128)} %get-tuple-element.40.order_ref), calls=%async_computation | async-start | bytes 65536 | tf_op jit(solution)/shard_map/all_to_all | solution.py:65
  9.7 0.1 shard_map.104
  9.8 1.8 %collective-permute-start.2 = (f32[4,4,4,128]{3,2,1,0:T(4,128)S(1)}, f32[4,4,4,128]{3,2,1,0:T(4,128)S(1)}, u32[]{:S(2)}, u32[]{:S(2)}) collective-permute-start(f32[4,4,4,128]{3,2,1,0:T(4,128)S(1)} %get-tuple-element.57), channel_id=1, source_target_pairs={{0,1},{1,0},{2,3},{3,2},{4,5},{5,4},{6,7},{7,6},{8,9},{9,8},{10,11... | collective-permute-start | bytes 98312 | tf_op jit(solution)/shard_map/ppermute | solution.py:527
  11.6 2.4 %collective-permute-start.3 = (f32[4,4,4,128]{3,2,1,0:T(4,128)S(1)}, f32[4,4,4,128]{3,2,1,0:T(4,128)S(1)}, u32[]{:S(2)}, u32[]{:S(2)}) collective-permute-start(f32[4,4,4,128]{3,2,1,0:T(4,128)S(1)} %get-tuple-element.58), channel_id=1, source_target_pairs={{0,3},{1,2},{2,1},{3,0},{4,7},{5,6},{6,5},{7,4},{8,11},{9,10},{10,... | collective-permute-start | bytes 98312 | tf_op jit(solution)/shard_map/ppermute | solution.py:526
  14.0 0.6 %shard_map.105 = (s32[8,512]{1,0:T(8,128)S(1)}, f32[1,512]{1,0:T(1,128)S(1)}, f32[512,768]{1,0:T(8,128)S(1)}, bf16[32,512]{1,0:T(8,128)(2,1)S(1)}, f32[128,2048]{1,0:T(8,128)S(1)}) custom-call(s32[1,256]{1,0:T(1,128)S(1)} %get-tuple-element.41.active_ref, f32[8,512]{1,0:T(8,128)S(1)} %get-tuple-element.42.state_ref, f32[16,128]{1,0:T(8,128)S(1)} %get-tuple-element.46.density_ref), custom_call_target="tpu_custom_call" | custom-call | tf_op jit(solution)/shard_map/pallas_call | solution.py:77
  14.6 2.2 %all-to-all-done.got_ref = f32[32,2,128]{2,1,0:T(2,128)S(1)} async-done(((f32[32,2,128]{2,1,0:T(2,128)}), f32[32,2,128]{2,1,0:T(2,128)S(1)}, u32[]{:S(2)}, u32[]{:S(2)}) %all-to-all-start) | async-done | bytes 32800 | tf_op jit(solution)/shard_map/all_to_all | solution.py:65
  16.8 1.9 %shard_map.106 = (f32[32,2,128]{2,1,0:T(2,128)}, f32[8,256]{1,0:T(8,128)S(1)}) custom-call(f32[32,2,128]{2,1,0:T(2,128)S(1)} %all-to-all-done.got_ref, s32[1,256]{1,0:T(1,128)S(1)} %get-tuple-element.41.active_ref, f32[512,768]{1,0:T(8,128)S(1)} %get-tuple-element.47.stars_ref, bf16[32,512]{1,0:T(8,128)(2,1)S(1)} %get-tuple-element.48.star_left_ref, ...), custom_call_target="tpu_custom_call" | custom-call | tf_op jit(solution)/shard_map/pallas_call | solution.py:77
  18.7 2.6 %all-to-all-start.1 = ((f32[32,2,128]{2,1,0:T(2,128)}), f32[32,2,128]{2,1,0:T(2,128)S(1)}, u32[]{:S(2)}, u32[]{:S(2)}) async-start(f32[32,2,128]{2,1,0:T(2,128)} %get-tuple-element.50), calls=%async_computation.1 | async-start | bytes 65536 | tf_op jit(solution)/shard_map/all_to_all | solution.py:65
  21.3 0.0 collective-permute-done.2
  21.3 0.0 collective-permute-done.3
  21.3 6.8 %conditional.1 = ((f32[3,4,8,64]{3,2,1,0:T(8,128)}, f32[3,4,8,64]{3,2,1,0:T(8,128)})) conditional(s32[]{:T(128)} %convert_element_type.3, () %tuple.15, (f32[4,4,8,128]{3,2,1,0:T(8,128)S(1)}, f32[4,4,4,128]{3,2,1,0:T(4,128)S(1)}, f32[4,4,4,128]{3,2,1,0:T(4,128)S(1)}, f32[8,256]{1,0:T(8,128)S(1)}) %tuple.16), branch_computations={%region_0.0_spmd, %region_1.0_spmd} | conditional | bytes 720984 | solution.py:618
  21.4 0.2 collective-permute-start
  21.6 2.6 %collective-permute-start.1 = (f32[22,8,128]{2,1,0:T(8,128)S(1)}, f32[22,8,128]{2,1,0:T(8,128)S(1)}, u32[]{:S(2)}, u32[]{:S(2)}) collective-permute-start(f32[22,8,128]{2,1,0:T(8,128)S(1)} %get-tuple-element.14), channel_id=1, source_target_pairs={{0,28},{4,8},{8,4},{12,16},{16,12},{20,24},{24,20},{28,0},{1,29},{... | collective-permute-start | bytes 270344 | tf_op jit(solution)/shard_map/cond/branch_1_fun/ppermute | solution.py:526
  24.1 2.6 %branch_1_fun.4.kick_ref = f32[3,5,16,128]{3,2,1,0:T(8,128)S(1)} custom-call(f32[8,256]{1,0:T(8,128)S(1)} %get-tuple-element.11.order_ref.target_ref), custom_call_target="tpu_custom_call" | custom-call | tf_op jit(solution)/shard_map/cond/branch_1_fun/pallas_call | solution.py:77
  26.8 0.0 collective-permute-done.near_ref
  26.8 0.1 collective-permute-done.1.far_ref
  26.9 1.2 %branch_1_fun.5 = (f32[3,4,8,64]{3,2,1,0:T(8,128)}, f32[3,4,8,64]{3,2,1,0:T(8,128)}) custom-call(f32[4,4,16,128]{3,2,1,0:T(8,128)S(1)} %get-tuple-element.12.own_ref, f32[22,8,128]{2,1,0:T(8,128)S(1)} %collective-permute-done.near_ref, f32[22,8,128]{2,1,0:T(8,128)S(1)} %collective-permute-done.1.far_ref, f32[3,5,16,128]{3,2,1,0:T(8,128)S(1)} %branch_1_fun.4.kick_ref), custom_call_target="tpu_custom_call" | custom-call | tf_op jit(solution)/shard_map/cond/branch_1_fun/pallas_call | solution.py:77
  28.1 0.3 %all-to-all-done.1.back_ref = f32[32,2,128]{2,1,0:T(2,128)S(1)} async-done(((f32[32,2,128]{2,1,0:T(2,128)}), f32[32,2,128]{2,1,0:T(2,128)S(1)}, u32[]{:S(2)}, u32[]{:S(2)}) %all-to-all-start.1) | async-done | bytes 32800 | tf_op jit(solution)/shard_map/all_to_all | solution.py:65
  28.4 0.7 %shard_map.108 = f32[12,512]{1,0:T(8,128)} custom-call(f32[32,2,128]{2,1,0:T(2,128)S(1)} %all-to-all-done.1.back_ref, f32[3,512]{1,0:T(4,128)S(1)} %get-tuple-element.51.pos_ref, f32[3,512]{1,0:T(4,128)S(1)} %get-tuple-element.52.vel_ref, f32[6,512]{1,0:T(8,128)S(1)} %get-tuple-element.53.acc_ref, s32[8,512]{1,0:T(8,128)S(1)} %get-tuple-element.54.slot_ref, ...), custom_call_target="tpu_custom_call" | custom-call | tf_op jit(solution)/shard_map/pallas_call | solution.py:77
  (2 shorter events, 0.0 us)
Async XLA Ops:
  2.4 14.4 %all-to-all-start = ((f32[32,2,128]{2,1,0:T(2,128)}), f32[32,2,128]{2,1,0:T(2,128)S(1)}, u32[]{:S(2)}, u32[]{:S(2)}) async-start(f32[32,2,128]{2,1,0:T(2,128)} %get-tuple-element.40.order_ref), calls=%async_computation | async-start | bytes 65536 | tf_op jit(solution)/shard_map/all_to_all | solution.py:65
  9.8 11.5 %collective-permute-start.2 = (f32[4,4,4,128]{3,2,1,0:T(4,128)S(1)}, f32[4,4,4,128]{3,2,1,0:T(4,128)S(1)}, u32[]{:S(2)}, u32[]{:S(2)}) collective-permute-start(f32[4,4,4,128]{3,2,1,0:T(4,128)S(1)} %get-tuple-element.57), channel_id=1, source_target_pairs={{0,1},{1,0},{2,3},{3,2},{4,5},{5,4},{6,7},{7,6},{8,9},{9,8},{10,11... | collective-permute-start | bytes 98312 | tf_op jit(solution)/shard_map/ppermute | solution.py:527
  11.6 9.7 %collective-permute-start.3 = (f32[4,4,4,128]{3,2,1,0:T(4,128)S(1)}, f32[4,4,4,128]{3,2,1,0:T(4,128)S(1)}, u32[]{:S(2)}, u32[]{:S(2)}) collective-permute-start(f32[4,4,4,128]{3,2,1,0:T(4,128)S(1)} %get-tuple-element.58), channel_id=1, source_target_pairs={{0,3},{1,2},{2,1},{3,0},{4,7},{5,6},{6,5},{7,4},{8,11},{9,10},{10,... | collective-permute-start | bytes 98312 | tf_op jit(solution)/shard_map/ppermute | solution.py:526
  18.7 9.7 %all-to-all-start.1 = ((f32[32,2,128]{2,1,0:T(2,128)}), f32[32,2,128]{2,1,0:T(2,128)S(1)}, u32[]{:S(2)}, u32[]{:S(2)}) async-start(f32[32,2,128]{2,1,0:T(2,128)} %get-tuple-element.50), calls=%async_computation.1 | async-start | bytes 65536 | tf_op jit(solution)/shard_map/all_to_all | solution.py:65
  21.4 5.4 %collective-permute-start = (f32[22,8,128]{2,1,0:T(8,128)S(1)}, f32[22,8,128]{2,1,0:T(8,128)S(1)}, u32[]{:S(2)}, u32[]{:S(2)}) collective-permute-start(f32[22,8,128]{2,1,0:T(8,128)S(1)} %get-tuple-element.13), channel_id=1, source_target_pairs={{0,4},{4,0},{8,12},{12,8},{16,20},{20,16},{24,28},{28,24},{1,5},{5... | collective-permute-start | bytes 270344 | tf_op jit(solution)/shard_map/cond/branch_1_fun/ppermute | solution.py:527
  21.6 5.3 %collective-permute-start.1 = (f32[22,8,128]{2,1,0:T(8,128)S(1)}, f32[22,8,128]{2,1,0:T(8,128)S(1)}, u32[]{:S(2)}, u32[]{:S(2)}) collective-permute-start(f32[22,8,128]{2,1,0:T(8,128)S(1)} %get-tuple-element.14), channel_id=1, source_target_pairs={{0,28},{4,8},{8,4},{12,16},{16,12},{20,24},{24,20},{28,0},{1,29},{... | collective-permute-start | bytes 270344 | tf_op jit(solution)/shard_map/cond/branch_1_fun/ppermute | solution.py:526
